TPU v7x, 32 devices: a whole 2x2x4 slice. The times are simulated.
32 devices in a mesh: grp: 2 (over x), row: 8 (over z, y), col: 2 (over core).
Axes of the slice: x: 2, y: 2, z: 4, core: 2. Of those that a mesh axis runs over, the one named last changes fastest.
Arguments:
- pair: bfloat16 [512, 256, 128], P(('grp', 'row'), 'col'), parts along dimension 0, may hold values from -6 to 6
- length: int32 [2], P('grp'), parts along dimension 0, may hold values from 128 to 256
- norm_in_gain: float32 [128], replicated, may hold values from 0.5 to 1.5
- norm_in_bias: float32 [128], replicated, may hold values from -3 to 3
- proj_in: bfloat16 [128, 256], replicated, may hold values from -0.5 to 0.5
- gate_in: bfloat16 [128, 256], replicated, may hold values from -0.5 to 0.5
- gate_out: bfloat16 [128, 128], replicated, may hold values from -0.5 to 0.5
- norm_out_gain: float32 [128], replicated, may hold values from 0.5 to 1.5
- norm_out_bias: float32 [128], replicated, may hold values from -3 to 3
- proj_out: bfloat16 [128, 128], replicated, may hold values from -0.5 to 0.5
Outputs:
- update: bfloat16 [512, 256, 128], P(('grp', 'row'), 'col'), parts along dimension 0
There are 2 independent parts, one for each index of `grp`. A program takes and returns all parts, laid end to end along the dimension named above; an argument that names none is the same for every part. Nothing has to cross between parts.
All inputs are finite; a program needn't handle non-finite values.
Results may differ from a plain program's by a relative error of at most 0.0059.
Values may be sent and summed in bfloat16 or wider, within the bound.
No kernel may reach another device: no remote copies, remote signals or barrier semaphores. Data moves between devices by JAX's collectives and lax.ppermute only.
A program may use at most 64 MiB of HBM per device.

v0:
```python
import jax
import jax.numpy as jnp
from jax import lax
from jax.sharding import PartitionSpec as P

epsilon = 1e-05


def from_partner(value, axis, apart):
    mask = 2**apart
    pairs = [(source, source ^ mask) for source in range(lax.axis_size(axis))]
    return lax.ppermute(value, axis, pairs)


def shards(
    pair,
    length,
    norm_in_gain,
    norm_in_bias,
    proj_in,
    gate_in,
    gate_out,
    norm_out_gain,
    norm_out_bias,
    proj_out,
):
    tile_rows = pair.shape[0]
    tile_cols = pair.shape[1]
    hidden = proj_out.shape[0]
    widened = pair.astype(jnp.float32)
    average = jnp.mean(widened, axis=-1, keepdims=True)
    centered = widened - average
    spread = jnp.mean(centered * centered, axis=-1, keepdims=True)
    normed = (centered * lax.rsqrt(spread + epsilon) * norm_in_gain + norm_in_bias).astype(
        jnp.bfloat16
    )
    row_start = lax.axis_index("row") * tile_rows
    col_start = lax.axis_index("col") * tile_cols
    valid_rows = (row_start + jnp.arange(tile_rows, dtype=jnp.int32) < length[0]).astype(
        jnp.float32
    )
    valid_cols = (col_start + jnp.arange(tile_cols, dtype=jnp.int32) < length[0]).astype(
        jnp.float32
    )
    pair_mask = valid_rows[:, None] * valid_cols[None, :]
    projected = jnp.einsum("ijc,ch->hij", normed, proj_in, preferred_element_type=jnp.float32)
    gating = jnp.einsum("ijc,ch->hij", normed, gate_in, preferred_element_type=jnp.float32)
    edges = (jax.nn.sigmoid(gating) * projected * pair_mask[None]).astype(jnp.bfloat16)
    left_half = edges[:hidden]
    right_half = edges[hidden:]
    left_rows, right_rows = (
        lax.all_to_all(left_half, "row", split_axis=0, concat_axis=1, tiled=True),
        lax.all_to_all(right_half, "row", split_axis=0, concat_axis=1, tiled=True),
    )
    other_half = from_partner(left_rows, "col", 0)
    first_col = lax.axis_index("col") == 0
    left_full = jnp.where(
        first_col,
        jnp.concatenate([left_rows, other_half], axis=2),
        jnp.concatenate([other_half, left_rows], axis=2),
    )
    contracted = jnp.einsum(
        "hki,hkj->hij", left_full, right_rows, preferred_element_type=jnp.float32
    ).astype(jnp.bfloat16)
    returned = lax.all_to_all(contracted, "row", split_axis=1, concat_axis=0, tiled=True)
    widened_out = returned.astype(jnp.float32)
    out_average = jnp.mean(widened_out, axis=0, keepdims=True)
    out_centered = widened_out - out_average
    out_spread = jnp.mean(out_centered * out_centered, axis=0, keepdims=True)
    contracted_norm = (
        out_centered * lax.rsqrt(out_spread + epsilon) * norm_out_gain[:, None, None]
        + norm_out_bias[:, None, None]
    ).astype(jnp.bfloat16)
    out_gate = jax.nn.sigmoid(
        jnp.einsum("ijc,cd->ijd", normed, gate_out, preferred_element_type=jnp.float32)
    )
    projected_out = jnp.einsum(
        "hij,hc->ijc", contracted_norm, proj_out, preferred_element_type=jnp.float32
    )
    return (out_gate * projected_out).astype(jnp.bfloat16)


def solution(mesh):
    placed = (P(("grp", "row"), "col", None), P("grp"), P(), P(), P(), P(), P(), P(), P(), P())
    return jax.shard_map(
        shards,
        mesh=mesh,
        in_specs=placed,
        out_specs=P(("grp", "row"), "col", None),
        check_vma=False,
    )
```

profile of v0, /device:TPU:0, one launch (start us, length us, event | category | flops | bytes accessed | tf_op | source)
XLA Modules:
  0.0 112.1 jit_solution(6083945797700703547)
XLA Ops:
  0.0 1.7 %convert_reduce_fusion = f32[32,128]{1,0:T(8,128)S(1)} fusion(bf16[32,128,128]{2,1,0:T(8,128)(2,1)} %param.10), kind=kLoop, calls=%fused_computation.2 | loop fusion | flops 1044480 | bytes 1064960 | tf_op jit(solution)/shard_map/reduce_sum | solution.py:31
  1.7 2.3 %fusion.2 = f32[32,128]{1,0:T(8,128)S(1)} fusion(bf16[32,128,128]{2,1,0:T(8,128)(2,1)} %param.10, f32[32,128]{1,0:T(8,128)S(1)} %broadcast_multiply_fusion.2), kind=kLoop, calls=%fused_computation.5 | loop fusion | flops 2093056 | bytes 1081344 | tf_op jit(solution)/shard_map/reduce_sum | solution.py:33
  4.7 0.1 add_rsqrt_fusion.1
  4.8 0.0 copy-start.8
  4.8 1.3 %fusion.21 = f32[32,128,256]{2,1,0:T(8,128)S(1)} fusion(bf16[128,256]{1,0:T(8,128)(2,1)S(1)} %copy-done, bf16[32,128,128]{2,1,0:T(8,128)(2,1)S(1)} %copy-done.1, f32[128]{0:T(128)S(1)} %copy-done.4, f32[128]{0:T(128)S(1)} %copy-done.5, f32[32,128]{1,0:T(8,128)S(1)} %get-tuple-element.9, f32[32,128]{1,0:T(8,128)S(1)} %broadcast_multiply_fusion.2), kind=kOutput, calls=%fused_computation.29 | convolution fusion | flops 271581184 | bytes 5342208 | tf_op jit(solution)/shard_map/ijc,ch->hij/dot_general | solution.py:46
  6.1 2.2 %fusion.17 = bf16[256,32,128]{0,2,1:T(8,128)(2,1)S(1)} fusion(f32[32,128]{1,0:T(8,128)S(1)} %get-tuple-element.10, f32[32,128,256]{2,1,0:T(8,128)S(1)} %fusion.21, bf16[128,256]{1,0:T(8,128)(2,1)S(1)} %copy-done.8, bf16[32,128,128]{2,1,0:T(8,128)(2,1)S(1)} %copy-done.1, f32[128]{0:T(128)S(1)} %copy-done.4, f32[128]{0:T(128)S(1)} %copy-done.5, ...), kind=kOutput, calls=%fused_computation.25 | convolution fusion | flops 277872640 | bytes 7455744 | tf_op jit(solution)/shard_map/ijc,ch->hij/dot_general | solution.py:47
  8.3 0.6 fusion.31
  8.9 1.7 %copy.28 = bf16[128,32,128]{2,1,0:T(8,128)(2,1)} copy(bf16[128,32,128]{0,2,1:T(8,128)(2,1)S(1)} %get-tuple-element.5) | data formatting | bytes 2097152 | tf_op jit(solution)/shard_map/slice | solution.py:49
  10.6 7.3 %all-to-all-start = ((bf16[128,32,128]{2,1,0:T(8,128)(2,1)}), bf16[128,32,128]{2,1,0:T(8,128)(2,1)S(1)}, u32[]{:S(2)}, u32[]{:S(2)}) async-start(bf16[128,32,128]{2,1,0:T(8,128)(2,1)} %copy.28), calls=%async_computation | async-start | bytes 2097152 | tf_op jit(solution)/shard_map/all_to_all | solution.py:52
  17.9 1.7 %copy.30 = bf16[128,32,128]{2,1,0:T(8,128)(2,1)} copy(bf16[128,32,128]{0,2,1:T(8,128)(2,1)S(1)} %get-tuple-element.6) | data formatting | bytes 2097152 | tf_op jit(solution)/shard_map/slice | solution.py:50
  19.6 24.1 %all-to-all-done = bf16[128,32,128]{2,1,0:T(8,128)(2,1)S(1)} async-done(((bf16[128,32,128]{2,1,0:T(8,128)(2,1)}), bf16[128,32,128]{2,1,0:T(8,128)(2,1)S(1)}, u32[]{:S(2)}, u32[]{:S(2)}) %all-to-all-start) | async-done | bytes 1048608 | tf_op jit(solution)/shard_map/all_to_all | solution.py:52
  43.7 3.6 %all-to-all-start.1 = ((bf16[128,32,128]{2,1,0:T(8,128)(2,1)}), bf16[128,32,128]{2,1,0:T(8,128)(2,1)S(1)}, u32[]{:S(2)}, u32[]{:S(2)}) async-start(bf16[128,32,128]{2,1,0:T(8,128)(2,1)} %copy.30), calls=%async_computation.1 | async-start | bytes 2097152 | tf_op jit(solution)/shard_map/all_to_all | solution.py:53
  47.3 1.1 copy.29
  48.3 24.9 %all-to-all-done.1 = bf16[128,32,128]{2,1,0:T(8,128)(2,1)S(1)} async-done(((bf16[128,32,128]{2,1,0:T(8,128)(2,1)}), bf16[128,32,128]{2,1,0:T(8,128)(2,1)S(1)}, u32[]{:S(2)}, u32[]{:S(2)}) %all-to-all-start.1) | async-done | bytes 1048608 | tf_op jit(solution)/shard_map/all_to_all | solution.py:53
  73.2 0.1 copy.31
  73.3 2.5 %fusion.18 = bf16[16,256,128]{2,1,0:T(8,128)(2,1)S(1)} fusion(bf16[16,256,128]{2,1,0:T(8,128)(2,1)S(1)} %bitcast.49, bf16[16,256,128]{2,1,0:T(8,128)(2,1)S(1)} %collective-permute-done, bf16[16,256,128]{2,1,0:T(8,128)(2,1)} %bitcast.7, pred[]{:T(512)S(6)} %eq.3), kind=kOutput, calls=%fused_computation.26 | convolution fusion | flops 278396928 | bytes 4194305 | tf_op jit(solution)/shard_map/hki,hkj->hij/dot_general | solution.py:62
  75.8 0.0 copy-start.3
  75.8 1.6 %copy.33 = bf16[16,256,128]{2,0,1:T(8,128)(2,1)} copy(bf16[16,256,128]{2,1,0:T(8,128)(2,1)S(1)} %fusion.18) | data formatting | bytes 2097152 | tf_op jit(solution)/shard_map/convert_element_type | solution.py:64
  77.4 3.6 %all-to-all-start.2 = ((bf16[16,256,128]{2,0,1:T(8,128)(2,1)}), bf16[16,256,128]{2,0,1:T(8,128)(2,1)S(1)}, u32[]{:S(2)}, u32[]{:S(2)}) async-start(bf16[16,256,128]{2,0,1:T(8,128)(2,1)} %copy.33), calls=%async_computation.2 | async-start | bytes 2097152 | tf_op jit(solution)/shard_map/all_to_all | solution.py:65
  81.1 2.5 %fusion.25 = f32[32,128,128]{2,1,0:T(8,128)} fusion(bf16[128,128]{1,0:T(8,128)(2,1)S(1)} %copy-done.3, bf16[32,128,128]{2,1,0:T(8,128)(2,1)S(1)} %copy-done.1, f32[128]{0:T(128)S(1)} %copy-done.4, f32[128]{0:T(128)S(1)} %copy-done.5, f32[32,128]{1,0:T(8,128)S(1)} %get-tuple-element.9, f32[32,128]{1,0:T(8,128)S(1)} %broadcast_multiply_fusion.2), kind=kOutput, calls=%fused_computation.33 | convolution fusion | flops 137363456 | bytes 3212288 | tf_op jit(solution)/shard_map/ijc,cd->ijd/dot_general | solution.py:75
  83.6 23.4 %all-to-all-done.2 = bf16[16,256,128]{2,0,1:T(8,128)(2,1)S(1)} async-done(((bf16[16,256,128]{2,0,1:T(8,128)(2,1)}), bf16[16,256,128]{2,0,1:T(8,128)(2,1)S(1)}, u32[]{:S(2)}, u32[]{:S(2)}) %all-to-all-start.2) | async-done | bytes 1048608 | tf_op jit(solution)/shard_map/all_to_all | solution.py:65
  107.0 0.3 fusion.32
  107.4 0.2 fusion.19
  107.6 0.3 multiply_reduce_fusion
  107.9 0.0 copy-start.6
  107.9 0.0 copy-start.7
  107.9 0.2 copy.35
  108.2 0.4 copy-done.6
  108.6 0.0 copy-done.7
  108.6 0.4 fusion.15
  109.0 1.2 %copy-done.2 = f32[32,128,128]{2,1,0:T(8,128)S(1)} copy-done((f32[32,128,128]{2,1,0:T(8,128)S(1)}, f32[32,128,128]{2,1,0:T(8,128)}, u32[]{:S(2)}) %copy-start.2) | copy-done | bytes 2097176
  110.2 2.0 %multiply_convert_fusion.1 = bf16[32,128,128]{2,1,0:T(8,128)(2,1)} fusion(f32[32,128,128]{2,1,0:T(8,128)S(1)} %copy-done.2, bf16[128,32,128]{2,1,0:T(8,128)(2,1)S(1)} %fusion.15, bf16[128,128]{1,0:T(8,128)(2,1)S(1)} %copy-done.9), kind=kOutput, calls=%fused_computation.22 | convolution fusion | flops 136839168 | bytes 4227072 | tf_op jit(solution)/shard_map/hij,hc->ijc/dot_general | solution.py:77
  (20 shorter events, 0.1 us)
Async XLA Ops:
  0.0 4.8 %copy-start = (bf16[128,256]{1,0:T(8,128)(2,1)S(1)}, bf16[128,256]{1,0:T(8,128)(2,1)}, u32[]{:S(2)}) copy-start(bf16[128,256]{1,0:T(8,128)(2,1)} %param.14) | copy-start | bytes 196612
  0.0 4.8 %copy-start.1 = (bf16[32,128,128]{2,1,0:T(8,128)(2,1)S(1)}, bf16[32,128,128]{2,1,0:T(8,128)(2,1)}, u32[]{:S(2)}) copy-start(bf16[32,128,128]{2,1,0:T(8,128)(2,1)} %param.10) | copy-start | bytes 3145732
  0.0 4.8 %copy-start.5 = (f32[128]{0:T(128)S(1)}, f32[128]{0:T(128)}, u32[]{:S(2)}) copy-start(f32[128]{0:T(128)} %param.12) | copy-start | bytes 1540
  0.0 4.8 %copy-start.4 = (f32[128]{0:T(128)S(1)}, f32[128]{0:T(128)}, u32[]{:S(2)}) copy-start(f32[128]{0:T(128)} %param.13) | copy-start | bytes 1540
  4.8 1.3 %copy-start.8 = (bf16[128,256]{1,0:T(8,128)(2,1)S(1)}, bf16[128,256]{1,0:T(8,128)(2,1)}, u32[]{:S(2)}) copy-start(bf16[128,256]{1,0:T(8,128)(2,1)} %param.15) | copy-start | bytes 196612
  10.6 33.1 %all-to-all-start = ((bf16[128,32,128]{2,1,0:T(8,128)(2,1)}), bf16[128,32,128]{2,1,0:T(8,128)(2,1)S(1)}, u32[]{:S(2)}, u32[]{:S(2)}) async-start(bf16[128,32,128]{2,1,0:T(8,128)(2,1)} %copy.28), calls=%async_computation | async-start | bytes 2097152 | tf_op jit(solution)/shard_map/all_to_all | solution.py:52
  43.7 29.5 %all-to-all-start.1 = ((bf16[128,32,128]{2,1,0:T(8,128)(2,1)}), bf16[128,32,128]{2,1,0:T(8,128)(2,1)S(1)}, u32[]{:S(2)}, u32[]{:S(2)}) async-start(bf16[128,32,128]{2,1,0:T(8,128)(2,1)} %copy.30), calls=%async_computation.1 | async-start | bytes 2097152 | tf_op jit(solution)/shard_map/all_to_all | solution.py:53
  48.3 25.0 %collective-permute-start = (bf16[16,256,128]{2,1,0:T(8,128)(2,1)}, bf16[16,256,128]{2,1,0:T(8,128)(2,1)S(1)}, u32[]{:S(2)}, u32[]{:S(2)}) collective-permute-start(bf16[16,256,128]{2,1,0:T(8,128)(2,1)} %bitcast.7), channel_id=1, source_target_pairs={{0,1},{1,0},{2,3},{3,2},{4,5},{5,4},{6,7},{7,6},{8,9},{9,8},{10,11... | collective-permute-start | bytes 3145736 | tf_op jit(solution)/shard_map/ppermute | solution.py:12
  75.8 5.3 %copy-start.3 = (bf16[128,128]{1,0:T(8,128)(2,1)S(1)}, bf16[128,128]{1,0:T(8,128)(2,1)}, u32[]{:S(2)}) copy-start(bf16[128,128]{1,0:T(8,128)(2,1)} %param.16) | copy-start | bytes 98308
  77.4 29.6 %all-to-all-start.2 = ((bf16[16,256,128]{2,0,1:T(8,128)(2,1)}), bf16[16,256,128]{2,0,1:T(8,128)(2,1)S(1)}, u32[]{:S(2)}, u32[]{:S(2)}) async-start(bf16[16,256,128]{2,0,1:T(8,128)(2,1)} %copy.33), calls=%async_computation.2 | async-start | bytes 2097152 | tf_op jit(solution)/shard_map/all_to_all | solution.py:65
  107.9 0.7 copy-start.6
  107.9 0.7 copy-start.7
  108.6 1.6 %copy-start.2 = (f32[32,128,128]{2,1,0:T(8,128)S(1)}, f32[32,128,128]{2,1,0:T(8,128)}, u32[]{:S(2)}) copy-start(f32[32,128,128]{2,1,0:T(8,128)} %fusion.25) | copy-start | bytes 6291460
  108.6 1.6 %copy-start.9 = (bf16[128,128]{1,0:T(8,128)(2,1)S(1)}, bf16[128,128]{1,0:T(8,128)(2,1)}, u32[]{:S(2)}) copy-start(bf16[128,128]{1,0:T(8,128)(2,1)} %param.19) | copy-start | bytes 98308
where the time goes:
time: 113 us; the launch traced here: 112 us
  waiting for transfers between devices  72.4 us (64%)
  starting transfers between devices  14.5 us (13%)
  matrix products  10.4 us (9%)
  local copies, waits for them, and re-layouts  8.66 us (8%)
  other arithmetic  5.37 us (5%)
    all_to_all x1, waiting for transfers between devices, shards(): lax.all_to_all(right_half, 'row', split_axis=0, concat_axis=1, tiled=True)  24.9 us
    all_to_all x1, waiting for transfers between devices, shards(): lax.all_to_all(left_half, 'row', split_axis=0, concat_axis=1, tiled=True)  24.1 us
    all_to_all x1, waiting for transfers between devices, shards(): lax.all_to_all(contracted, 'row', split_axis=1, concat_axis=0, tiled=True)  23.4 us
    all_to_all x1, starting transfers between devices, shards(): lax.all_to_all(left_half, 'row', split_axis=0, concat_axis=1, tiled=True)  7.29 us
    all_to_all x1, starting transfers between devices, shards(): lax.all_to_all(contracted, 'row', split_axis=1, concat_axis=0, tiled=True)  3.64 us
    all_to_all x1, starting transfers between devices, shards(): lax.all_to_all(right_half, 'row', split_axis=0, concat_axis=1, tiled=True)  3.59 us
    dot_general x1, matrix products, shards(): jnp.einsum('ijc,cd->ijd', normed, gate_out, preferred_element_type=jnp.fl...  2.52 us
    dot_general x1, matrix products, shards(): jnp.einsum('hki,hkj->hij', left_full, right_rows, preferred_element_type=...  2.45 us
  transfers between devices with their start and end apart: 4, of which 3 were waited for; matrix products, arithmetic and copies ran while one was open for 5% of the time, Pallas kernels for 0%

commit v1 on v0

v1 whole, which is shorter than its diff:
```python
import functools

import jax
import jax.numpy as jnp
from jax import lax
from jax.experimental import pallas as pl
from jax.experimental.pallas import tpu as pltpu
from jax.sharding import PartitionSpec as P

epsilon = 1e-05
chunk_sizes = (12, 20)
swap_pieces = (1, 2)
vmem_all = 60 * 1024 * 1024
vmem_part = 28 * 1024 * 1024


def from_partner(value, axis, apart):
    mask = 2**apart
    pairs = [(source, source ^ mask) for source in range(lax.axis_size(axis))]
    return lax.ppermute(value, axis, pairs)


def normalize_in(pair, gain, bias):
    widened = pair.astype(jnp.float32)
    average = jnp.mean(widened, axis=-1, keepdims=True)
    centered = widened - average
    spread = jnp.mean(centered * centered, axis=-1, keepdims=True)
    return (centered * lax.rsqrt(spread + epsilon) * gain + bias).astype(jnp.bfloat16)


def token_mask(tile_rows, tile_cols, length):
    row_start = lax.axis_index("row") * tile_rows
    col_start = lax.axis_index("col") * tile_cols
    valid_rows = row_start + jnp.arange(tile_rows, dtype=jnp.int32) < length[0]
    valid_cols = col_start + jnp.arange(tile_cols, dtype=jnp.int32) < length[0]
    return (valid_rows[:, None] & valid_cols[None, :]).astype(jnp.float32)


def make_edges(normed, proj, gate, mask):
    projected = jnp.einsum("ijc,ch->hij", normed, proj, preferred_element_type=jnp.float32)
    gating = jnp.einsum("ijc,ch->hij", normed, gate, preferred_element_type=jnp.float32)
    return (jax.nn.sigmoid(gating) * projected * mask[None]).astype(jnp.bfloat16)


def finish(contracted, normed, gate_out, gain, bias, proj_out):
    widened = contracted.astype(jnp.float32)
    average = jnp.mean(widened, axis=0, keepdims=True)
    centered = widened - average
    spread = jnp.mean(centered * centered, axis=0, keepdims=True)
    scaled = centered * lax.rsqrt(spread + epsilon) * gain[:, None, None]
    contracted_norm = (scaled + bias[:, None, None]).astype(jnp.bfloat16)
    out_gate = jax.nn.sigmoid(
        jnp.einsum("ijc,cd->ijd", normed, gate_out, preferred_element_type=jnp.float32)
    )
    projected_out = jnp.einsum(
        "hij,hc->ijc", contracted_norm, proj_out, preferred_element_type=jnp.float32
    )
    return (out_gate * projected_out).astype(jnp.bfloat16)


def contract(left, right):
    return jnp.einsum("hki,hkj->hij", left, right, preferred_element_type=jnp.float32)


def shards_by_exchange(
    pair,
    length,
    norm_in_gain,
    norm_in_bias,
    proj_in,
    gate_in,
    gate_out,
    norm_out_gain,
    norm_out_bias,
    proj_out,
):
    hidden = proj_out.shape[0]
    normed = normalize_in(pair, norm_in_gain, norm_in_bias)
    mask = token_mask(pair.shape[0], pair.shape[1], length)
    edges = make_edges(normed, proj_in, gate_in, mask)
    left_rows = lax.all_to_all(edges[:hidden], "row", split_axis=0, concat_axis=1, tiled=True)
    right_rows = lax.all_to_all(edges[hidden:], "row", split_axis=0, concat_axis=1, tiled=True)
    other_half = from_partner(left_rows, "col", 0)
    first_col = lax.axis_index("col") == 0
    left_full = jnp.where(
        first_col,
        jnp.concatenate([left_rows, other_half], axis=2),
        jnp.concatenate([other_half, left_rows], axis=2),
    )
    contracted = contract(left_full, right_rows).astype(jnp.bfloat16)
    returned = lax.all_to_all(contracted, "row", split_axis=1, concat_axis=0, tiled=True)
    return finish(returned, normed, gate_out, norm_out_gain, norm_out_bias, proj_out)


in_smem = pl.BlockSpec(memory_space=pltpu.SMEM)
in_any = pl.BlockSpec(memory_space=pl.ANY)
matmul_tn = (((0,), (0,)), ((), ()))
matmul_nt = (((1,), (1,)), ((), ()))


def call(kernel, outputs, scratch, specs, name, limit=vmem_part):
    return pl.pallas_call(
        kernel,
        out_shape=outputs,
        in_specs=specs,
        out_specs=[in_any] * len(outputs),
        scratch_shapes=scratch,
        compiler_params=pltpu.CompilerParams(vmem_limit_bytes=limit),
        cost_estimate=pl.CostEstimate(flops=0, bytes_accessed=1024, transcendentals=0),
        name=name,
    )


def array(shape, dtype=jnp.bfloat16):
    return jax.ShapeDtypeStruct(shape, dtype)


def load(source, target, sem):
    copy = pltpu.make_async_copy(source, target, sem)
    copy.start()
    return copy


def transposed_weights(proj, gate, held):
    width = proj.shape[1]
    held[pl.ds(0, width), :] = proj[...].astype(jnp.float32).T.astype(jnp.bfloat16)
    held[pl.ds(width, width), :] = gate[...].astype(jnp.float32).T.astype(jnp.bfloat16)


def chunk_weights(held, start, stop):
    width = held.shape[0] // 2
    hidden = width // 2
    offsets = (0, hidden, width, width + hidden)
    return jnp.concatenate([held[offset + start : offset + stop, :] for offset in offsets], axis=0)


def block_edges(length, normed, weights, at, row_start, col_start, out):
    rows, tile_cols, channels = normed.shape
    slots, both, _, _ = out.shape
    size = both // 2
    pairs = lax.dot_general(
        weights,
        normed.reshape(rows * tile_cols, channels),
        matmul_nt,
        preferred_element_type=jnp.float32,
    )
    count = pairs.shape[0] // 2
    values = jax.nn.sigmoid(pairs[count:]) * pairs[:count]
    cols = col_start + lax.broadcasted_iota(jnp.int32, (count, tile_cols), 1)
    masked = []
    for row in range(rows):
        limit = jnp.where(row_start + at + row < length, length, 0)
        piece = values[:, row * tile_cols : (row + 1) * tile_cols]
        masked.append(jnp.where(cols < limit, piece, 0.0))
    swapped = jnp.swapaxes(jnp.stack(masked, axis=0), 0, 1).astype(jnp.bfloat16)
    for slot in range(slots):
        for side in range(2):
            first = (side * slots + slot) * size
            out[slot, side * size : (side + 1) * size, at : at + rows, :] = swapped[
                first : first + size
            ]


def first_kernel(bounds, length, pair, gain, bias, proj, gate, normed, *rest):
    start, stop, rows = bounds
    outs = rest[:4]
    pair_held, gain_held, bias_held, proj_held, gate_held, weights_held = rest[4:10]
    normed_held, out_held, sems = rest[10:]
    tile_rows, tile_cols, channels = pair.shape
    blocks = tile_rows // rows
    small = [
        load(source, target, sems.at[at])
        for at, (source, target) in enumerate(
            ((proj, proj_held), (gate, gate_held), (gain, gain_held), (bias, bias_held))
        )
    ]
    pieces = [
        load(pair.at[pl.ds(b * rows, rows)], pair_held.at[pl.ds(b * rows, rows)], sems.at[4 + b])
        for b in range(blocks)
    ]
    row = lax.axis_index("row")
    row_start = row * tile_rows
    col_start = lax.axis_index("col") * tile_cols
    for copy in small:
        copy.wait()
    transposed_weights(proj_held, gate_held, weights_held)
    weights = chunk_weights(weights_held, start, stop)
    for b in range(blocks):
        at = b * rows
        pieces[b].wait()
        widened = pair_held[at : at + rows].astype(jnp.float32).reshape(rows * tile_cols, channels)
        average = jnp.mean(widened, axis=-1, keepdims=True)
        centered = widened - average
        spread = jnp.mean(centered * centered, axis=-1, keepdims=True)
        scaled = centered * lax.rsqrt(spread + epsilon) * gain_held[...] + bias_held[...]
        rounded = scaled.astype(jnp.bfloat16).reshape(rows, tile_cols, channels)
        normed_held[at : at + rows] = rounded
        block_edges(length[0], rounded, weights, at, row_start, col_start, out_held)
    base = 4 + blocks
    stores = [load(normed_held, normed, sems.at[base])]
    for slot, out in enumerate(outs):
        stores.append(load(out_held.at[(row % 4) ^ slot], out, sems.at[base + 1 + slot]))
    for copy in stores:
        copy.wait()


def later_kernel(bounds, length, normed, proj, gate, *rest):
    start, stop, rows = bounds
    outs = rest[:4]
    normed_held, proj_held, gate_held, weights_held, out_held, sems = rest[4:]
    tile_rows = normed.shape[0]
    blocks = tile_rows // rows
    loads = [
        load(source, target, sems.at[at])
        for at, (source, target) in enumerate(
            ((proj, proj_held), (gate, gate_held), (normed, normed_held))
        )
    ]
    row = lax.axis_index("row")
    row_start = row * tile_rows
    col_start = lax.axis_index("col") * normed.shape[1]
    loads[0].wait()
    loads[1].wait()
    transposed_weights(proj_held, gate_held, weights_held)
    weights = chunk_weights(weights_held, start, stop)
    loads[2].wait()
    for b in range(blocks):
        at = b * rows
        tokens = normed_held[at : at + rows]
        block_edges(length[0], tokens, weights, at, row_start, col_start, out_held)
    stores = [
        load(out_held.at[(row % 4) ^ slot], out, sems.at[3 + slot]) for slot, out in enumerate(outs)
    ]
    for copy in stores:
        copy.wait()


def gate_kernel(rows, after, normed, weights, out, normed_held, weights_held, out_held, sems):
    tile_rows, tile_cols, channels = normed.shape
    load(weights, weights_held, sems.at[0]).wait()
    load(normed, normed_held, sems.at[1]).wait()
    stores = []
    for b in range(tile_rows // rows):
        at = b * rows
        gating = jnp.dot(
            normed_held[at : at + rows].reshape(rows * tile_cols, channels),
            weights_held[...],
            preferred_element_type=jnp.float32,
        )
        out_held[at : at + rows] = jax.nn.sigmoid(gating).reshape(rows, tile_cols, channels)
        part = pl.ds(at, rows)
        stores.append(load(out_held.at[part], out.at[part], sems.at[2 + b]))
    for copy in stores:
        copy.wait()


def pack_kernel(after, a, b, c, d, *rest):
    outs, sems = rest[:-1], rest[-1]
    size, count, _ = outs[0].shape
    part = count // 4
    copies = []
    for piece, out in enumerate(outs):
        for at, ref in enumerate((a, b, c, d)):
            rows = out.at[:, pl.ds(at * part, part), :]
            copies.append(load(ref.at[pl.ds(piece * size, size)], rows, sems.at[piece, at]))
    for copy in copies:
        copy.wait()


def products(lefts, parts, left_held, right_held, sems, outs):
    _, size, depth, _ = left_held.shape
    part = depth // 4
    row, col = lax.axis_index("row"), lax.axis_index("col")
    loads, start = [], 0
    for at in range(len(lefts) // 2):
        count = lefts[2 * at].shape[0]
        which = pl.ds(start, count)
        loads.append(load(lefts[2 * at], left_held.at[col, which], sems.at[len(loads)]))
        loads.append(load(lefts[2 * at + 1], left_held.at[1 - col, which], sems.at[len(loads)]))
        start += count
    for at, ref in enumerate(parts):
        loads.append(
            load(
                ref.at[pl.ds(size, size)],
                right_held.at[:, pl.ds(at * part, part), :],
                sems.at[len(loads)],
            )
        )
    low = (row < 4).astype(jnp.int32)
    for copy in loads:
        copy.wait()
    for side, held in ((low, outs[0]), (1 - low, outs[1])):
        for u in range(size):
            product = lax.dot_general(
                left_held[side, u], right_held[u], matmul_tn, preferred_element_type=jnp.float32
            )
            held[u] = product.astype(held.dtype)
        yield held


def contract_kernel(count, *refs):
    lefts, parts = refs[:count], refs[count : count + 4]
    away, keep, left_held, right_held, away_held, keep_held, sems = refs[count + 4 :]
    stores = []
    helds = (away_held, keep_held)
    for at, held in enumerate(products(lefts, parts, left_held, right_held, sems, helds)):
        stores.append(load(held, (away, keep)[at], sems.at[count + 4 + at]))
    for copy in stores:
        copy.wait()


def last_contract_kernel(count, *refs):
    lefts, parts = refs[:count], refs[count : count + 4]
    outs = refs[count + 4 : count + 8], refs[count + 8 : count + 12]
    left_held, right_held, away_held, keep_held, sems = refs[count + 12 :]
    part = left_held.shape[2] // 4
    row = lax.axis_index("row")
    stores = []
    helds = (away_held, keep_held)
    for half, held in enumerate(products(lefts, parts, left_held, right_held, sems, helds)):
        for slot, out in enumerate(outs[half]):
            rows = pl.ds(pl.multiple_of(((row % 4) ^ slot) * part, part), part)
            place = count + 4 + 4 * half + slot
            stores.append(load(held.at[:, rows, :], out, sems.at[place]))
    for copy in stores:
        copy.wait()


def add_kernel(keep, arrived, *refs):
    lasts, outs = refs[:4], refs[4:8]
    keep_held, arrived_held, sems = refs[8:]
    size, part = keep.shape[0], outs[0].shape[1]
    row = lax.axis_index("row")
    loads = [load(keep, keep_held, sems.at[0]), load(arrived, arrived_held, sems.at[1])]
    stores = [
        load(last, out.at[pl.ds(size, last.shape[0])], sems.at[2 + at])
        for at, (last, out) in enumerate(zip(lasts, outs, strict=True))
    ]
    for copy in loads:
        copy.wait()
    for u in range(size):
        total = keep_held[u] + arrived_held[u].astype(jnp.float32)
        arrived_held[u] = total.astype(jnp.bfloat16)
    for slot, out in enumerate(outs):
        rows = pl.ds(pl.multiple_of(((row % 4) ^ slot) * part, part), part)
        stores.append(
            load(arrived_held.at[:, rows, :], out.at[pl.ds(0, size)], sems.at[6 + slot])
        )
    for copy in stores:
        copy.wait()


def finish_kernel(rows, ranges, *refs):
    aways, totals = refs[:4], refs[4:8]
    opened, gain, bias, proj, out = refs[8:13]
    parts_held, last_held, opened_held, gain_held, bias_held, proj_held, out_held, sems = refs[13:]
    hidden, tile_rows, tile_cols = parts_held.shape
    last_start = ranges[-1][0]
    row = lax.axis_index("row")
    moves = [(gain, gain_held), (bias, bias_held), (proj, proj_held)]
    for slot in range(4):
        from_slot = (row % 4) ^ slot
        offset = 0
        for start, stop in ranges:
            size = (stop - start) // 4
            target = parts_held.at[pl.ds(start + from_slot * size, size)]
            moves.append((totals[slot].at[pl.ds(offset, size)], target))
            offset += size
        moves.append((aways[slot], last_held.at[pl.ds(from_slot * size, size)]))
    moves.append((opened, opened_held))
    loads = [load(source, target, sems.at[at]) for at, (source, target) in enumerate(moves)]
    for copy in loads[:-1]:
        copy.wait()
    gain_rows = jnp.broadcast_to(gain_held[...], (hidden, hidden)).T
    bias_rows = jnp.broadcast_to(bias_held[...], (hidden, hidden)).T
    zero = jnp.zeros((tile_rows, tile_cols), jnp.float32)

    def early(h):
        return parts_held[h].astype(jnp.float32)

    def late(h):
        return early(h) + last_held[h - last_start].astype(jnp.float32)

    def over_channels(step):
        done = lax.fori_loop(0, last_start, lambda h, s: s + step(early(h)), zero, unroll=8)
        done = lax.fori_loop(last_start, hidden, lambda h, s: s + step(late(h)), done, unroll=8)
        return done * (1.0 / hidden)

    average = over_channels(lambda value: value)
    spread = over_channels(lambda value: (value - average) * (value - average))
    scale = lax.rsqrt(spread + epsilon)
    stores = []
    loads[-1].wait()
    for b in range(tile_rows // rows):
        at = b * rows
        own = slice(at, at + rows)
        first = parts_held[:last_start, own, :].astype(jnp.float32)
        second = parts_held[last_start:, own, :].astype(jnp.float32)
        second = second + last_held[:, own, :].astype(jnp.float32)
        centered = jnp.concatenate([first, second], axis=0) - average[None, own]
        swapped = jnp.swapaxes(centered * scale[None, own], 0, 1)
        scaled = (swapped * gain_rows[None] + bias_rows[None]).astype(jnp.bfloat16)
        for step in range(rows):
            projected = lax.dot_general(
                scaled[step], proj_held[...], matmul_tn, preferred_element_type=jnp.float32
            )
            out_held[at + step] = (opened_held[at + step] * projected).astype(jnp.bfloat16)
        part = pl.ds(at, rows)
        stores.append(load(out_held.at[part], out.at[part], sems.at[len(moves) + b]))
    for copy in stores:
        copy.wait()


def shards_by_halves(
    pair,
    length,
    norm_in_gain,
    norm_in_bias,
    proj_in,
    gate_in,
    gate_out,
    norm_out_gain,
    norm_out_bias,
    proj_out,
):
    tile_rows, tile_cols, channels = pair.shape
    hidden = proj_out.shape[0]
    rows = lax.axis_size("row")
    block = min(16, tile_rows)
    blocks = tile_rows // block
    stops = [4 * sum(chunk_sizes[: at + 1]) for at in range(len(chunk_sizes))]
    ranges = list(zip([0, *stops[:-1]], stops, strict=True))
    wide = proj_in.shape[1]
    vmem, semaphores = pltpu.VMEM, pltpu.SemaphoreType.DMA
    small = jnp.bfloat16
    weights_scratch = [vmem(proj_in.shape, small), vmem(gate_in.shape, small)]
    turned = vmem((2 * wide, channels), small)
    depth = 4 * tile_rows

    def exchanged(value, mask):
        return lax.ppermute(value, "row", [(source, source ^ mask) for source in range(rows)])

    def edge_arrays(size):
        return [array((2 * size, tile_rows, tile_cols))] * 4

    def edge_scratch(size):
        return vmem((4, 2 * size, tile_rows, tile_cols), small)

    def edges_of(at, normed):
        return call(
            functools.partial(later_kernel, (*ranges[at], block)),
            edge_arrays(chunk_sizes[at]),
            [
                vmem(pair.shape, small),
                *weights_scratch,
                turned,
                edge_scratch(chunk_sizes[at]),
                semaphores((7,)),
            ],
            [in_smem] + [in_any] * 3,
            "later_edges",
        )(length, normed, proj_in, gate_in)

    def received(pieces):
        return [pieces[0], *[exchanged(pieces[mask], mask) for mask in (3, 2, 1)][::-1]]

    def swapped_left(at, after, pieces):
        size = chunk_sizes[at] // swap_pieces[at]
        lefts = call(
            pack_kernel,
            [array((size, depth, tile_cols))] * swap_pieces[at],
            [semaphores((swap_pieces[at], 4))],
            [in_any] * 5,
            "pack_left",
        )(after, *pieces)
        return [side for left in lefts for side in (left, from_partner(left, "col", 0))]

    def product_scratch(size, kept, count):
        shape = (size, depth, tile_cols)
        return [
            vmem((2, *shape), small),
            vmem(shape, small),
            vmem(shape, small),
            vmem(shape, kept),
            semaphores((count,)),
        ]

    def contracted(at, after, pieces):
        size = chunk_sizes[at]
        shape = (size, depth, tile_cols)
        lefts = swapped_left(at, after, pieces)
        return call(
            functools.partial(contract_kernel, len(lefts)),
            [array(shape), array(shape, jnp.float32)],
            product_scratch(size, jnp.float32, len(lefts) + 6),
            [in_any] * (len(lefts) + 4),
            "contract",
        )(*lefts, *pieces)

    def last_contracted(at, after, pieces):
        size = chunk_sizes[at]
        lefts = swapped_left(at, after, pieces)
        return call(
            functools.partial(last_contract_kernel, len(lefts)),
            [array((size, tile_rows, tile_cols))] * 8,
            product_scratch(size, small, len(lefts) + 12),
            [in_any] * (len(lefts) + 4),
            "contract",
        )(*lefts, *pieces)

    normed, *first = call(
        functools.partial(first_kernel, (*ranges[0], block)),
        [array(pair.shape), *edge_arrays(chunk_sizes[0])],
        [
            vmem(pair.shape, small),
            vmem((1, channels), jnp.float32),
            vmem((1, channels), jnp.float32),
            *weights_scratch,
            turned,
            vmem(pair.shape, small),
            edge_scratch(chunk_sizes[0]),
            semaphores((9 + blocks,)),
        ],
        [in_smem] + [in_any] * 5,
        "norm_and_first_edges",
        vmem_all,
    )(length, pair, norm_in_gain[None], norm_in_bias[None], proj_in, gate_in)
    first = received(first)
    second = edges_of(1, normed)
    away, keep = contracted(0, second[0], first)
    second = received(second)
    arrived = exchanged(away, 4)
    (opened,) = call(
        functools.partial(gate_kernel, block),
        [array(pair.shape, jnp.float32)],
        [
            vmem(pair.shape, small),
            vmem(gate_out.shape, small),
            vmem(pair.shape, jnp.float32),
            semaphores((2 + blocks,)),
        ],
        [in_any] * 3,
        "output_gate",
    )(away, normed, gate_out)
    last = last_contracted(1, opened, second)
    aways = [exchanged(last[mask], 4 ^ mask) for mask in range(4)]
    size = chunk_sizes[0]
    totals = call(
        add_kernel,
        [array((sum(chunk_sizes), tile_rows, tile_cols))] * 4,
        [
            vmem((size, depth, tile_cols), jnp.float32),
            vmem((size, depth, tile_cols), small),
            semaphores((10,)),
        ],
        [in_any] * 6,
        "add_halves",
    )(keep, arrived, *last[4:])
    totals = [totals[0], *[exchanged(totals[mask], mask) for mask in (1, 2, 3)]]
    (update,) = call(
        functools.partial(finish_kernel, 8, ranges),
        [array(pair.shape)],
        [
            vmem((hidden, tile_rows, tile_cols), small),
            vmem((4 * chunk_sizes[-1], tile_rows, tile_cols), small),
            vmem(pair.shape, jnp.float32),
            vmem((1, hidden), jnp.float32),
            vmem((1, hidden), jnp.float32),
            vmem(proj_out.shape, small),
            vmem(pair.shape, small),
            semaphores((4 + 4 * (len(ranges) + 1) + tile_rows // 8,)),
        ],
        [in_any] * 12,
        "norm_and_project_out",
    )(*aways, *totals, opened, norm_out_gain[None], norm_out_bias[None], proj_out)
    return update


def solution(mesh):
    placed = (P(("grp", "row"), "col", None), P("grp"), P(), P(), P(), P(), P(), P(), P(), P())
    return jax.shard_map(
        shards_by_halves if mesh.shape["row"] == 8 else shards_by_exchange,
        mesh=mesh,
        in_specs=placed,
        out_specs=P(("grp", "row"), "col", None),
        check_vma=False,
    )
```

time: 113 us -> 89.3 us (0.79)
  waiting for transfers between devices: 72.4 us -> 43.6 us
  Pallas kernels: 0 us -> 17.6 us
  matrix products: 10.4 us -> 0 us
  starting transfers between devices: 14.5 us -> 23.1 us
  other arithmetic: 5.37 us -> 0 us
  local copies, waits for them, and re-layouts: 8.66 us -> 3.86 us
    all_to_all x3 -> x0, waiting for transfers between devices: 72.4 us -> none  [the longest x1 24.9 us: shards(): lax.all_to_all(right_half, 'row', split_axis=0, concat_axis=1, tiled=True)]
    ppermute x0 -> x14, waiting for transfers between devices: none -> 42 us  [exchanged(): lax.ppermute(value, 'row', [(source, source ^ mask) for source in range(r...]
    ppermute x0 -> x14, starting transfers between devices: none -> 22.5 us  [exchanged(): lax.ppermute(value, 'row', [(source, source ^ mask) for source in range(r...]
    pallas_call x0 -> x9, Pallas kernels: none -> 17.6 us  [the longest x1 5.4 us: shards_by_halves(): call(functools.partial(finish_kernel, 8, ranges), [array(pair.shape)], [v...]
    all_to_all x3 -> x0, starting transfers between devices: 14.5 us -> none  [the longest x1 7.29 us: shards(): lax.all_to_all(left_half, 'row', split_axis=0, concat_axis=1, tiled=True)]
    dot_general x5 -> x0, matrix products: 10.4 us -> none  [the longest x1 2.52 us: shards(): jnp.einsum('ijc,cd->ijd', normed, gate_out, preferred_element_type=jnp.fl...]
    reduce_sum x4 -> x0, other arithmetic: 4.53 us -> none  [the longest x1 2.33 us: shards(): spread = jnp.mean(centered * centered, axis=-1, keepdims=True)]
    slice x3 -> x0, local copies, waits for them, and re-layouts: 3.98 us -> none  [the longest x2 2.31 us: shards(): left_half = edges[:hidden]]
  transfers between devices with their start and end apart: 4 -> 17, of which waited for: 3 -> 12; matrix products, arithmetic and copies ran while one was open for 5% -> 0% of each run, Pallas kernels for 0% -> 9%
where the time goes in v1:
time: 89.3 us; the launch traced here: 89 us
  waiting for transfers between devices  43.6 us (49%)
  starting transfers between devices  23.1 us (26%)
  Pallas kernels  17.6 us (20%)
  local copies, waits for them, and re-layouts  3.86 us (4%)
    ppermute x14, waiting for transfers between devices, exchanged(): lax.ppermute(value, 'row', [(source, source ^ mask) for source in range(r...  42 us
    ppermute x14, starting transfers between devices, exchanged(): lax.ppermute(value, 'row', [(source, source ^ mask) for source in range(r...  22.5 us
    pallas_call x1, Pallas kernels, shards_by_halves(): call(functools.partial(finish_kernel, 8, ranges), [array(pair.shape)], [v...  5.4 us
    pallas_call x1, Pallas kernels, shards_by_halves(): call(functools.partial(first_kernel, (*ranges[0], block)), [array(pair.sh...  4.48 us
    unnamed x18, local copies, waits for them, and re-layouts  3.86 us
    pallas_call x1, Pallas kernels, edges_of(): call(functools.partial(later_kernel, (*ranges[at], block)), edge_arrays(c...  2.11 us
  transfers between devices with their start and end apart: 17, of which 12 were waited for; matrix products, arithmetic and copies ran while one was open for 0% of the time, Pallas kernels for 9%

profile of v1, /device:TPU:0, one launch (start us, length us, event | category | flops | bytes accessed | tf_op | source)
XLA Modules:
  0.0 89.0 jit_solution(17775630662894602642)
XLA Ops:
  0.7 4.5 %norm_and_first_edges.1 = (bf16[32,128,128]{2,1,0:T(8,128)(2,1)}, bf16[24,32,128]{2,1,0:T(8,128)(2,1)}, bf16[24,32,128]{2,1,0:T(8,128)(2,1)}, bf16[24,32,128]{2,1,0:T(8,128)(2,1)}, bf16[24,32,128]{2,1,0:T(8,128)(2,1)}) custom-call(s32[1]{0:T(128)S(6)} %copy.11.length, bf16[32,128,128]{2,1,0:T(8,128)(2,1)} %pair.1, f32[1,128]{1,0:T(1,128)} %bitcast.6, ...), custom_call_target="tpu_custom_call" | custom-call | bytes 1024 | tf_op jit(solution)/shard_map/norm_and_first_edges/pallas_call | solution.py:511
  5.1 3.0 %collective-permute-start = (bf16[24,32,128]{2,1,0:T(8,128)(2,1)}, bf16[24,32,128]{2,1,0:T(8,128)(2,1)S(1)}, u32[]{:S(2)}, u32[]{:S(2)}) collective-permute-start(bf16[24,32,128]{2,1,0:T(8,128)(2,1)} %get-tuple-element.33), channel_id=1, source_target_pairs={{0,2},{2,0},{4,6},{6,4},{8,10},{10,8},{12,14},{14,12},{1,3},{3,1},... | collective-permute-start | bytes 589832 | tf_op jit(solution)/shard_map/ppermute | solution.py:441
  8.2 1.6 %collective-permute-start.1 = (bf16[24,32,128]{2,1,0:T(8,128)(2,1)}, bf16[24,32,128]{2,1,0:T(8,128)(2,1)S(1)}, u32[]{:S(2)}, u32[]{:S(2)}) collective-permute-start(bf16[24,32,128]{2,1,0:T(8,128)(2,1)} %get-tuple-element.34), channel_id=1, source_target_pairs={{0,4},{2,6},{4,0},{6,2},{8,12},{10,14},{12,8},{14,10},{1,5},{3,7},... | collective-permute-start | bytes 589832 | tf_op jit(solution)/shard_map/ppermute | solution.py:441
  9.8 1.2 %copy-done = bf16[32,128,128]{2,1,0:T(8,128)(2,1)S(1)} copy-done((bf16[32,128,128]{2,1,0:T(8,128)(2,1)S(1)}, bf16[32,128,128]{2,1,0:T(8,128)(2,1)}, u32[]{:S(2)}) %copy-start) | copy-done | bytes 1048600
  11.0 0.8 copy-done.3
  12.7 2.1 %later_edges.1 = (bf16[40,32,128]{2,1,0:T(8,128)(2,1)S(1)}, bf16[40,32,128]{2,1,0:T(8,128)(2,1)S(1)}, bf16[40,32,128]{2,1,0:T(8,128)(2,1)S(1)}, bf16[40,32,128]{2,1,0:T(8,128)(2,1)S(1)}) custom-call(s32[1]{0:T(128)S(6)} %copy.11.length, bf16[32,128,128]{2,1,0:T(8,128)(2,1)S(1)} %copy-done, bf16[128,256]{1,0:T(8,128)(2,1)S(1)} %copy-done.3, ...), custom_call_target="tpu_custom_call" | custom-call | bytes 1024 | tf_op jit(solution)/shard_map/later_edges/pallas_call | solution.py:450
  14.8 1.4 %collective-permute-done.1.c.refs_4_ = bf16[24,32,128]{2,1,0:T(8,128)(2,1)S(1)} collective-permute-done((bf16[24,32,128]{2,1,0:T(8,128)(2,1)}, bf16[24,32,128]{2,1,0:T(8,128)(2,1)S(1)}, u32[]{:S(2)}, u32[]{:S(2)}) %collective-permute-start.1) | collective-permute-done | bytes 196640 | tf_op jit(solution)/shard_map/ppermute | solution.py:441
  16.2 2.5 %collective-permute-done.2.d.refs_5_ = bf16[24,32,128]{2,1,0:T(8,128)(2,1)S(1)} collective-permute-done((bf16[24,32,128]{2,1,0:T(8,128)(2,1)}, bf16[24,32,128]{2,1,0:T(8,128)(2,1)S(1)}, u32[]{:S(2)}, u32[]{:S(2)}) %collective-permute-start.2) | collective-permute-done | bytes 196640 | tf_op jit(solution)/shard_map/ppermute | solution.py:441
  18.8 0.9 %copy-done.2 = bf16[24,32,128]{2,1,0:T(8,128)(2,1)S(1)} copy-done((bf16[24,32,128]{2,1,0:T(8,128)(2,1)S(1)}, bf16[24,32,128]{2,1,0:T(8,128)(2,1)}, u32[]{:S(2)}) %copy-start.2) | copy-done | bytes 196632
  19.9 1.7 %collective-permute-start.4 = (bf16[40,32,128]{2,1,0:T(8,128)(2,1)S(1)}, bf16[40,32,128]{2,1,0:T(8,128)(2,1)S(1)}, u32[]{:S(2)}, u32[]{:S(2)}) collective-permute-start(bf16[40,32,128]{2,1,0:T(8,128)(2,1)S(1)} %get-tuple-element.37), channel_id=1, source_target_pairs={{0,2},{2,0},{4,6},{6,4},{8,10},{10,8},{12,14},{14,12},{1,3},{3,1},... | collective-permute-start | bytes 983048 | tf_op jit(solution)/shard_map/ppermute | solution.py:441
  21.6 1.6 %collective-permute-start.5 = (bf16[40,32,128]{2,1,0:T(8,128)(2,1)S(1)}, bf16[40,32,128]{2,1,0:T(8,128)(2,1)S(1)}, u32[]{:S(2)}, u32[]{:S(2)}) collective-permute-start(bf16[40,32,128]{2,1,0:T(8,128)(2,1)S(1)} %get-tuple-element.38), channel_id=1, source_target_pairs={{0,4},{2,6},{4,0},{6,2},{8,12},{10,14},{12,8},{14,10},{1,5},{3,7},... | collective-permute-start | bytes 983048 | tf_op jit(solution)/shard_map/ppermute | solution.py:441
  23.4 1.4 %contract.2 = (bf16[12,128,128]{2,1,0:T(8,128)(2,1)S(1)}, f32[12,128,128]{2,1,0:T(8,128)S(1)}) custom-call(bf16[12,128,128]{2,1,0:T(8,128)(2,1)S(1)} %pack_left.2.refs_0_, bf16[12,128,128]{2,1,0:T(8,128)(2,1)S(1)} %collective-permute-done.3.refs_1_, bf16[24,32,128]{2,1,0:T(8,128)(2,1)S(1)} %copy-done.2, ...), custom_call_target="tpu_custom_call" | custom-call | bytes 1024 | tf_op jit(solution)/shard_map/contract/pallas_call | solution.py:492
  24.8 2.8 %collective-permute-start.13 = (bf16[12,128,128]{2,1,0:T(8,128)(2,1)S(1)}, bf16[12,128,128]{2,1,0:T(8,128)(2,1)S(1)}, u32[]{:S(2)}, u32[]{:S(2)}) collective-permute-start(bf16[12,128,128]{2,1,0:T(8,128)(2,1)S(1)} %get-tuple-element.36.after), channel_id=1, source_target_pairs={{0,8},{2,10},{4,12},{6,14},{8,0},{10,2},{12,4},{14,6},{1,9},{3,11}... | collective-permute-start | bytes 1179656 | tf_op jit(solution)/shard_map/ppermute | solution.py:441
  27.6 1.1 %output_gate.1.after.refs_8_ = f32[32,128,128]{2,1,0:T(8,128)S(1)} custom-call(bf16[12,128,128]{2,1,0:T(8,128)(2,1)S(1)} %get-tuple-element.36.after, bf16[32,128,128]{2,1,0:T(8,128)(2,1)S(1)} %copy-done.1, bf16[128,128]{1,0:T(8,128)(2,1)S(1)} %copy-done.5), custom_call_target="tpu_custom_call" | custom-call | bytes 1024 | tf_op jit(solution)/shard_map/output_gate/pallas_call | solution.py:533
  28.7 1.3 %collective-permute-done.4.b.refs_5_ = bf16[40,32,128]{2,1,0:T(8,128)(2,1)S(1)} collective-permute-done((bf16[40,32,128]{2,1,0:T(8,128)(2,1)S(1)}, bf16[40,32,128]{2,1,0:T(8,128)(2,1)S(1)}, u32[]{:S(2)}, u32[]{:S(2)}) %collective-permute-start.4) | collective-permute-done | bytes 327712 | tf_op jit(solution)/shard_map/ppermute | solution.py:441
  30.0 10.6 %collective-permute-done.5.c.refs_6_ = bf16[40,32,128]{2,1,0:T(8,128)(2,1)S(1)} collective-permute-done((bf16[40,32,128]{2,1,0:T(8,128)(2,1)S(1)}, bf16[40,32,128]{2,1,0:T(8,128)(2,1)S(1)}, u32[]{:S(2)}, u32[]{:S(2)}) %collective-permute-start.5) | collective-permute-done | bytes 327712 | tf_op jit(solution)/shard_map/ppermute | solution.py:441
  40.6 6.0 %collective-permute-done.6.d.refs_7_ = bf16[40,32,128]{2,1,0:T(8,128)(2,1)S(1)} collective-permute-done((bf16[40,32,128]{2,1,0:T(8,128)(2,1)S(1)}, bf16[40,32,128]{2,1,0:T(8,128)(2,1)S(1)}, u32[]{:S(2)}, u32[]{:S(2)}) %collective-permute-start.6) | collective-permute-done | bytes 327712 | tf_op jit(solution)/shard_map/ppermute | solution.py:441
  47.4 1.1 %collective-permute-done.7.refs_1_ = bf16[10,128,128]{2,1,0:T(8,128)(2,1)S(1)} collective-permute-done((bf16[10,128,128]{2,1,0:T(8,128)(2,1)S(1)}, bf16[10,128,128]{2,1,0:T(8,128)(2,1)S(1)}, u32[]{:S(2)}, u32[]{:S(2)}) %collective-permute-start.7) | collective-permute-done | bytes 327712 | tf_op jit(solution)/shard_map/ppermute | solution.py:20
  48.9 1.6 %contract.3 = (bf16[20,32,128]{2,1,0:T(8,128)(2,1)S(1)}, bf16[20,32,128]{2,1,0:T(8,128)(2,1)S(1)}, bf16[20,32,128]{2,1,0:T(8,128)(2,1)S(1)}, bf16[20,32,128]{2,1...) custom-call(bf16[10,128,128]{2,1,0:T(8,128)(2,1)S(1)} %get-tuple-ele, ...), custom_call_target="tpu_custom_call" | custom-call | bytes 1024 | tf_op jit(solution)/shard_map/contract/pallas_call | solution.py:503
  50.5 2.0 %collective-permute-start.9 = (bf16[20,32,128]{2,1,0:T(8,128)(2,1)S(1)}, bf16[20,32,128]{2,1,0:T(8,128)(2,1)S(1)}, u32[]{:S(2)}, u32[]{:S(2)}) collective-permute-start(bf16[20,32,128]{2,1,0:T(8,128)(2,1)S(1)} %get-tuple-element.42), channel_id=1, source_target_pairs={{0,8},{2,10},{4,12},{6,14},{8,0},{10,2},{12,4},{14,6},{1,9},{3,11}... | collective-permute-start | bytes 491528 | tf_op jit(solution)/shard_map/ppermute | solution.py:441
  52.5 2.1 %collective-permute-start.10 = (bf16[20,32,128]{2,1,0:T(8,128)(2,1)S(1)}, bf16[20,32,128]{2,1,0:T(8,128)(2,1)S(1)}, u32[]{:S(2)}, u32[]{:S(2)}) collective-permute-start(bf16[20,32,128]{2,1,0:T(8,128)(2,1)S(1)} %get-tuple-element.43), channel_id=1, source_target_pairs={{0,10},{2,8},{4,14},{6,12},{8,2},{10,0},{12,6},{14,4},{1,11},{3,9}... | collective-permute-start | bytes 491528 | tf_op jit(solution)/shard_map/ppermute | solution.py:441
  54.6 1.3 %add_halves.1 = (bf16[32,32,128]{2,1,0:T(8,128)(2,1)S(1)}, bf16[32,32,128]{2,1,0:T(8,128)(2,1)S(1)}, bf16[32,32,128]{2,1,0:T(8,128)(2,1)S(1)}, bf16[32,32,128]{2,1,0:T(8,128)(2,1)S(1)}) custom-call(f32[12,128,128]{2,1,0:T(8,128)S(1)} %get-tuple-element.46.keep, bf16[12,128,128]{2,1,0:T(8,128)(2,1)S(1)} %collective-permute-done.13.arrived, ...), custom_call_target="tpu_custom_call" | custom-call | bytes 1024 | tf_op jit(solution)/shard_map/add_halves/pallas_call | solution.py:548
  56.4 1.5 %collective-permute-start.15 = (bf16[32,32,128]{2,1,0:T(8,128)(2,1)S(1)}, bf16[32,32,128]{2,1,0:T(8,128)(2,1)S(1)}, u32[]{:S(2)}, u32[]{:S(2)}) collective-permute-start(bf16[32,32,128]{2,1,0:T(8,128)(2,1)S(1)} %get-tuple-element.53), channel_id=1, source_target_pairs={{0,4},{2,6},{4,0},{6,2},{8,12},{10,14},{12,8},{14,10},{1,5},{3,7},... | collective-permute-start | bytes 786440 | tf_op jit(solution)/shard_map/ppermute | solution.py:441
  57.9 1.7 %collective-permute-start.16 = (bf16[32,32,128]{2,1,0:T(8,128)(2,1)S(1)}, bf16[32,32,128]{2,1,0:T(8,128)(2,1)S(1)}, u32[]{:S(2)}, u32[]{:S(2)}) collective-permute-start(bf16[32,32,128]{2,1,0:T(8,128)(2,1)S(1)} %get-tuple-element.54), channel_id=1, source_target_pairs={{0,6},{2,4},{4,2},{6,0},{8,14},{10,12},{12,10},{14,8},{1,7},{3,5},... | collective-permute-start | bytes 786440 | tf_op jit(solution)/shard_map/ppermute | solution.py:441
  59.5 6.1 %collective-permute-done.9.refs_0_ = bf16[20,32,128]{2,1,0:T(8,128)(2,1)S(1)} collective-permute-done((bf16[20,32,128]{2,1,0:T(8,128)(2,1)S(1)}, bf16[20,32,128]{2,1,0:T(8,128)(2,1)S(1)}, u32[]{:S(2)}, u32[]{:S(2)}) %collective-permute-start.9) | collective-permute-done | bytes 163872 | tf_op jit(solution)/shard_map/ppermute | solution.py:441
  65.7 2.1 %collective-permute-start.11 = (bf16[20,32,128]{2,1,0:T(8,128)(2,1)S(1)}, bf16[20,32,128]{2,1,0:T(8,128)(2,1)S(1)}, u32[]{:S(2)}, u32[]{:S(2)}) collective-permute-start(bf16[20,32,128]{2,1,0:T(8,128)(2,1)S(1)} %get-tuple-element.44), channel_id=1, source_target_pairs={{0,12},{2,14},{4,8},{6,10},{8,4},{10,6},{12,0},{14,2},{1,13},{3,15... | collective-permute-start | bytes 491528 | tf_op jit(solution)/shard_map/ppermute | solution.py:441
  67.7 2.5 %collective-permute-done.10.refs_1_ = bf16[20,32,128]{2,1,0:T(8,128)(2,1)S(1)} collective-permute-done((bf16[20,32,128]{2,1,0:T(8,128)(2,1)S(1)}, bf16[20,32,128]{2,1,0:T(8,128)(2,1)S(1)}, u32[]{:S(2)}, u32[]{:S(2)}) %collective-permute-start.10) | collective-permute-done | bytes 163872 | tf_op jit(solution)/shard_map/ppermute | solution.py:441
  70.2 1.9 %collective-permute-start.12 = (bf16[20,32,128]{2,1,0:T(8,128)(2,1)S(1)}, bf16[20,32,128]{2,1,0:T(8,128)(2,1)S(1)}, u32[]{:S(2)}, u32[]{:S(2)}) collective-permute-start(bf16[20,32,128]{2,1,0:T(8,128)(2,1)S(1)} %get-tuple-element.45), channel_id=1, source_target_pairs={{0,14},{2,12},{4,10},{6,8},{8,6},{10,4},{12,2},{14,0},{1,15},{3,13... | collective-permute-start | bytes 491528 | tf_op jit(solution)/shard_map/ppermute | solution.py:441
  72.1 6.1 %collective-permute-done.11.refs_2_ = bf16[20,32,128]{2,1,0:T(8,128)(2,1)S(1)} collective-permute-done((bf16[20,32,128]{2,1,0:T(8,128)(2,1)S(1)}, bf16[20,32,128]{2,1,0:T(8,128)(2,1)S(1)}, u32[]{:S(2)}, u32[]{:S(2)}) %collective-permute-start.11) | collective-permute-done | bytes 163872 | tf_op jit(solution)/shard_map/ppermute | solution.py:441
  78.2 3.6 %collective-permute-done.12.refs_3_ = bf16[20,32,128]{2,1,0:T(8,128)(2,1)S(1)} collective-permute-done((bf16[20,32,128]{2,1,0:T(8,128)(2,1)S(1)}, bf16[20,32,128]{2,1,0:T(8,128)(2,1)S(1)}, u32[]{:S(2)}, u32[]{:S(2)}) %collective-permute-start.12) | collective-permute-done | bytes 163872 | tf_op jit(solution)/shard_map/ppermute | solution.py:441
  81.8 1.8 %collective-permute-done.16.refs_7_ = bf16[32,32,128]{2,1,0:T(8,128)(2,1)S(1)} collective-permute-done((bf16[32,32,128]{2,1,0:T(8,128)(2,1)S(1)}, bf16[32,32,128]{2,1,0:T(8,128)(2,1)S(1)}, u32[]{:S(2)}, u32[]{:S(2)}) %collective-permute-start.16) | collective-permute-done | bytes 262176 | tf_op jit(solution)/shard_map/ppermute | solution.py:441
  83.6 5.4 %norm_and_project_out.1 = bf16[32,128,128]{2,1,0:T(8,128)(2,1)} custom-call(bf16[20,32,128]{2,1,0:T(8,128)(2,1)S(1)} %collective-permute-done.9.refs_0_, bf16[20,32,128]{2,1,0:T(8,128)(2,1)S(1)} %collective-permute-done.10.refs_1_, bf16[20,32,128]{2,1,0:T(8,128)(2,1)S(1)} %collective-permute-done.11.refs_2_, ...), custom_call_target="tpu_custom_call" | custom-call | bytes 1024 | tf_op jit(solution)/shard_map/norm_and_project_out/pallas_call | solution.py:560
  (29 shorter events, 2.9 us)
Async XLA Ops:
  5.1 9.6 %collective-permute-start = (bf16[24,32,128]{2,1,0:T(8,128)(2,1)}, bf16[24,32,128]{2,1,0:T(8,128)(2,1)S(1)}, u32[]{:S(2)}, u32[]{:S(2)}) collective-permute-start(bf16[24,32,128]{2,1,0:T(8,128)(2,1)} %get-tuple-element.33), channel_id=1, source_target_pairs={{0,2},{2,0},{4,6},{6,4},{8,10},{10,8},{12,14},{14,12},{1,3},{3,1},... | collective-permute-start | bytes 589832 | tf_op jit(solution)/shard_map/ppermute | solution.py:441
  8.2 8.0 %collective-permute-start.1 = (bf16[24,32,128]{2,1,0:T(8,128)(2,1)}, bf16[24,32,128]{2,1,0:T(8,128)(2,1)S(1)}, u32[]{:S(2)}, u32[]{:S(2)}) collective-permute-start(bf16[24,32,128]{2,1,0:T(8,128)(2,1)} %get-tuple-element.34), channel_id=1, source_target_pairs={{0,4},{2,6},{4,0},{6,2},{8,12},{10,14},{12,8},{14,10},{1,5},{3,7},... | collective-permute-start | bytes 589832 | tf_op jit(solution)/shard_map/ppermute | solution.py:441
  9.8 9.0 %collective-permute-start.2 = (bf16[24,32,128]{2,1,0:T(8,128)(2,1)}, bf16[24,32,128]{2,1,0:T(8,128)(2,1)S(1)}, u32[]{:S(2)}, u32[]{:S(2)}) collective-permute-start(bf16[24,32,128]{2,1,0:T(8,128)(2,1)} %get-tuple-element.35), channel_id=1, source_target_pairs={{0,6},{2,4},{4,2},{6,0},{8,14},{10,12},{12,10},{14,8},{1,7},{3,5},... | collective-permute-start | bytes 589832 | tf_op jit(solution)/shard_map/ppermute | solution.py:441
  9.8 1.2 %copy-start = (bf16[32,128,128]{2,1,0:T(8,128)(2,1)S(1)}, bf16[32,128,128]{2,1,0:T(8,128)(2,1)}, u32[]{:S(2)}) copy-start(bf16[32,128,128]{2,1,0:T(8,128)(2,1)} %get-tuple-element.30.normed) | copy-start | bytes 3145732
  11.0 0.8 copy-start.3
  11.8 0.8 copy-start.4
  12.7 14.9 %copy-start.1 = (bf16[32,128,128]{2,1,0:T(8,128)(2,1)S(1)}, bf16[32,128,128]{2,1,0:T(8,128)(2,1)}, u32[]{:S(2)}) copy-start(bf16[32,128,128]{2,1,0:T(8,128)(2,1)} %get-tuple-element.30.normed) | copy-start | bytes 3145732
  12.7 14.9 %copy-start.5 = (bf16[128,128]{1,0:T(8,128)(2,1)S(1)}, bf16[128,128]{1,0:T(8,128)(2,1)}, u32[]{:S(2)}) copy-start(bf16[128,128]{1,0:T(8,128)(2,1)} %weights.1) | copy-start | bytes 98308
  18.8 0.9 %copy-start.2 = (bf16[24,32,128]{2,1,0:T(8,128)(2,1)S(1)}, bf16[24,32,128]{2,1,0:T(8,128)(2,1)}, u32[]{:S(2)}) copy-start(bf16[24,32,128]{2,1,0:T(8,128)(2,1)} %get-tuple-element.32.a.refs_2_) | copy-start | bytes 589828
  19.8 3.6 %collective-permute-start.3 = (bf16[12,128,128]{2,1,0:T(8,128)(2,1)S(1)}, bf16[12,128,128]{2,1,0:T(8,128)(2,1)S(1)}, u32[]{:S(2)}, u32[]{:S(2)}) collective-permute-start(bf16[12,128,128]{2,1,0:T(8,128)(2,1)S(1)} %pack_left.2.refs_0_), channel_id=1, source_target_pairs={{0,1},{1,0},{2,3},{3,2},{4,5},{5,4},{6,7},{7,6},{8,9},{9,8},{10,11... | collective-permute-start | bytes 1179656 | tf_op jit(solution)/shard_map/ppermute | solution.py:20
  19.9 10.1 %collective-permute-start.4 = (bf16[40,32,128]{2,1,0:T(8,128)(2,1)S(1)}, bf16[40,32,128]{2,1,0:T(8,128)(2,1)S(1)}, u32[]{:S(2)}, u32[]{:S(2)}) collective-permute-start(bf16[40,32,128]{2,1,0:T(8,128)(2,1)S(1)} %get-tuple-element.37), channel_id=1, source_target_pairs={{0,2},{2,0},{4,6},{6,4},{8,10},{10,8},{12,14},{14,12},{1,3},{3,1},... | collective-permute-start | bytes 983048 | tf_op jit(solution)/shard_map/ppermute | solution.py:441
  21.6 19.0 %collective-permute-start.5 = (bf16[40,32,128]{2,1,0:T(8,128)(2,1)S(1)}, bf16[40,32,128]{2,1,0:T(8,128)(2,1)S(1)}, u32[]{:S(2)}, u32[]{:S(2)}) collective-permute-start(bf16[40,32,128]{2,1,0:T(8,128)(2,1)S(1)} %get-tuple-element.38), channel_id=1, source_target_pairs={{0,4},{2,6},{4,0},{6,2},{8,12},{10,14},{12,8},{14,10},{1,5},{3,7},... | collective-permute-start | bytes 983048 | tf_op jit(solution)/shard_map/ppermute | solution.py:441
  23.2 23.4 %collective-permute-start.6 = (bf16[40,32,128]{2,1,0:T(8,128)(2,1)S(1)}, bf16[40,32,128]{2,1,0:T(8,128)(2,1)S(1)}, u32[]{:S(2)}, u32[]{:S(2)}) collective-permute-start(bf16[40,32,128]{2,1,0:T(8,128)(2,1)S(1)} %get-tuple-element.39), channel_id=1, source_target_pairs={{0,6},{2,4},{4,2},{6,0},{8,14},{10,12},{12,10},{14,8},{1,7},{3,5},... | collective-permute-start | bytes 983048 | tf_op jit(solution)/shard_map/ppermute | solution.py:441
  24.8 29.9 %collective-permute-start.13 = (bf16[12,128,128]{2,1,0:T(8,128)(2,1)S(1)}, bf16[12,128,128]{2,1,0:T(8,128)(2,1)S(1)}, u32[]{:S(2)}, u32[]{:S(2)}) collective-permute-start(bf16[12,128,128]{2,1,0:T(8,128)(2,1)S(1)} %get-tuple-element.36.after), channel_id=1, source_target_pairs={{0,8},{2,10},{4,12},{6,14},{8,0},{10,2},{12,4},{14,6},{1,9},{3,11}... | collective-permute-start | bytes 1179656 | tf_op jit(solution)/shard_map/ppermute | solution.py:441
  46.8 1.7 %collective-permute-start.7 = (bf16[10,128,128]{2,1,0:T(8,128)(2,1)S(1)}, bf16[10,128,128]{2,1,0:T(8,128)(2,1)S(1)}, u32[]{:S(2)}, u32[]{:S(2)}) collective-permute-start(bf16[10,128,128]{2,1,0:T(8,128)(2,1)S(1)} %get-tuple-element.40.refs_0_), channel_id=1, source_target_pairs={{0,1},{1,0},{2,3},{3,2},{4,5},{5,4},{6,7},{7,6},{8,9},{9,8},{10,11... | collective-permute-start | bytes 983048 | tf_op jit(solution)/shard_map/ppermute | solution.py:20
  46.9 36.7 %copy-start.6 = (bf16[128,128]{1,0:T(8,128)(2,1)S(1)}, bf16[128,128]{1,0:T(8,128)(2,1)}, u32[]{:S(2)}) copy-start(bf16[128,128]{1,0:T(8,128)(2,1)} %refs_11_.1) | copy-start | bytes 98308
  46.9 36.7 %copy-start.7 = (f32[128]{0:T(128)S(1)}, f32[128]{0:T(128)}, u32[]{:S(2)}) copy-start(f32[128]{0:T(128)} %param.17) | copy-start | bytes 1540
  46.9 36.7 %copy-start.8 = (f32[128]{0:T(128)S(1)}, f32[128]{0:T(128)}, u32[]{:S(2)}) copy-start(f32[128]{0:T(128)} %param.18) | copy-start | bytes 1540
  46.9 2.0 %collective-permute-start.8 = (bf16[10,128,128]{2,1,0:T(8,128)(2,1)S(1)}, bf16[10,128,128]{2,1,0:T(8,128)(2,1)S(1)}, u32[]{:S(2)}, u32[]{:S(2)}) collective-permute-start(bf16[10,128,128]{2,1,0:T(8,128)(2,1)S(1)} %get-tuple-element.41.refs_2_), channel_id=1, source_target_pairs={{0,1},{1,0},{2,3},{3,2},{4,5},{5,4},{6,7},{7,6},{8,9},{9,8},{10,11... | collective-permute-start | bytes 983048 | tf_op jit(solution)/shard_map/ppermute | solution.py:20
  50.5 15.1 %collective-permute-start.9 = (bf16[20,32,128]{2,1,0:T(8,128)(2,1)S(1)}, bf16[20,32,128]{2,1,0:T(8,128)(2,1)S(1)}, u32[]{:S(2)}, u32[]{:S(2)}) collective-permute-start(bf16[20,32,128]{2,1,0:T(8,128)(2,1)S(1)} %get-tuple-element.42), channel_id=1, source_target_pairs={{0,8},{2,10},{4,12},{6,14},{8,0},{10,2},{12,4},{14,6},{1,9},{3,11}... | collective-permute-start | bytes 491528 | tf_op jit(solution)/shard_map/ppermute | solution.py:441
  52.5 17.7 %collective-permute-start.10 = (bf16[20,32,128]{2,1,0:T(8,128)(2,1)S(1)}, bf16[20,32,128]{2,1,0:T(8,128)(2,1)S(1)}, u32[]{:S(2)}, u32[]{:S(2)}) collective-permute-start(bf16[20,32,128]{2,1,0:T(8,128)(2,1)S(1)} %get-tuple-element.43), channel_id=1, source_target_pairs={{0,10},{2,8},{4,14},{6,12},{8,2},{10,0},{12,6},{14,4},{1,11},{3,9}... | collective-permute-start | bytes 491528 | tf_op jit(solution)/shard_map/ppermute | solution.py:441
  56.0 25.8 %collective-permute-start.14 = (bf16[32,32,128]{2,1,0:T(8,128)(2,1)S(1)}, bf16[32,32,128]{2,1,0:T(8,128)(2,1)S(1)}, u32[]{:S(2)}, u32[]{:S(2)}) collective-permute-start(bf16[32,32,128]{2,1,0:T(8,128)(2,1)S(1)} %get-tuple-element.52), channel_id=1, source_target_pairs={{0,2},{2,0},{4,6},{6,4},{8,10},{10,8},{12,14},{14,12},{1,3},{3,1},... | collective-permute-start | bytes 786440 | tf_op jit(solution)/shard_map/ppermute | solution.py:441
  56.4 25.4 %collective-permute-start.15 = (bf16[32,32,128]{2,1,0:T(8,128)(2,1)S(1)}, bf16[32,32,128]{2,1,0:T(8,128)(2,1)S(1)}, u32[]{:S(2)}, u32[]{:S(2)}) collective-permute-start(bf16[32,32,128]{2,1,0:T(8,128)(2,1)S(1)} %get-tuple-element.53), channel_id=1, source_target_pairs={{0,4},{2,6},{4,0},{6,2},{8,12},{10,14},{12,8},{14,10},{1,5},{3,7},... | collective-permute-start | bytes 786440 | tf_op jit(solution)/shard_map/ppermute | solution.py:441
  57.9 25.7 %collective-permute-start.16 = (bf16[32,32,128]{2,1,0:T(8,128)(2,1)S(1)}, bf16[32,32,128]{2,1,0:T(8,128)(2,1)S(1)}, u32[]{:S(2)}, u32[]{:S(2)}) collective-permute-start(bf16[32,32,128]{2,1,0:T(8,128)(2,1)S(1)} %get-tuple-element.54), channel_id=1, source_target_pairs={{0,6},{2,4},{4,2},{6,0},{8,14},{10,12},{12,10},{14,8},{1,7},{3,5},... | collective-permute-start | bytes 786440 | tf_op jit(solution)/shard_map/ppermute | solution.py:441
  65.7 12.5 %collective-permute-start.11 = (bf16[20,32,128]{2,1,0:T(8,128)(2,1)S(1)}, bf16[20,32,128]{2,1,0:T(8,128)(2,1)S(1)}, u32[]{:S(2)}, u32[]{:S(2)}) collective-permute-start(bf16[20,32,128]{2,1,0:T(8,128)(2,1)S(1)} %get-tuple-element.44), channel_id=1, source_target_pairs={{0,12},{2,14},{4,8},{6,10},{8,4},{10,6},{12,0},{14,2},{1,13},{3,15... | collective-permute-start | bytes 491528 | tf_op jit(solution)/shard_map/ppermute | solution.py:441
  70.2 11.6 %collective-permute-start.12 = (bf16[20,32,128]{2,1,0:T(8,128)(2,1)S(1)}, bf16[20,32,128]{2,1,0:T(8,128)(2,1)S(1)}, u32[]{:S(2)}, u32[]{:S(2)}) collective-permute-start(bf16[20,32,128]{2,1,0:T(8,128)(2,1)S(1)} %get-tuple-element.45), channel_id=1, source_target_pairs={{0,14},{2,12},{4,10},{6,8},{8,6},{10,4},{12,2},{14,0},{1,15},{3,13... | collective-permute-start | bytes 491528 | tf_op jit(solution)/shard_map/ppermute | solution.py:441

commit v2 on v1

--- a/solution.py
+++ b/solution.py
@@ -9,7 +9,7 @@
 
 epsilon = 1e-05
 chunk_sizes = (12, 20)
-swap_pieces = (1, 2)
+swap_pieces = (2, 2)
 vmem_all = 60 * 1024 * 1024
 vmem_part = 28 * 1024 * 1024
 

time: 89.3 us -> 83.2 us (0.932)
  waiting for transfers between devices: 43.6 us -> 27.2 us
  starting transfers between devices: 23.1 us -> 32.8 us
    ppermute x14, waiting for transfers between devices: 42 us -> 24.4 us  [exchanged(): lax.ppermute(value, 'row', [(source, source ^ mask) for source in range(r...]
    ppermute x14, starting transfers between devices: 22.5 us -> 31.7 us  [exchanged(): lax.ppermute(value, 'row', [(source, source ^ mask) for source in range(r...]
    ppermute x3 -> x4, waiting for transfers between devices: 1.58 us -> 2.79 us  [from_partner(): return lax.ppermute(value, axis, pairs)]
  transfers between devices with their start and end apart: 17 -> 18, of which waited for: 12 -> 10; matrix products, arithmetic and copies ran while one was open for 0% -> 0% of each run, Pallas kernels for 9% -> 10%
where the time goes in v2:
time: 83.2 us; the launch traced here: 82.9 us
  starting transfers between devices  32.8 us (39%)
  waiting for transfers between devices  27.2 us (33%)
  Pallas kernels  18.3 us (22%)
  local copies, waits for them, and re-layouts  3.86 us (5%)
    ppermute x14, starting transfers between devices, exchanged(): lax.ppermute(value, 'row', [(source, source ^ mask) for source in range(r...  31.7 us
    ppermute x14, waiting for transfers between devices, exchanged(): lax.ppermute(value, 'row', [(source, source ^ mask) for source in range(r...  24.4 us
    pallas_call x1, Pallas kernels, shards_by_halves(): call(functools.partial(finish_kernel, 8, ranges), [array(pair.shape)], [v...  5.4 us
    pallas_call x1, Pallas kernels, shards_by_halves(): call(functools.partial(first_kernel, (*ranges[0], block)), [array(pair.sh...  4.49 us
    unnamed x18, local copies, waits for them, and re-layouts  3.86 us
    ppermute x4, waiting for transfers between devices, from_partner(): return lax.ppermute(value, axis, pairs)  2.79 us
    pallas_call x1, Pallas kernels, edges_of(): call(functools.partial(later_kernel, (*ranges[at], block)), edge_arrays(c...  2.11 us
    pallas_call x1, Pallas kernels, contracted(): call(functools.partial(contract_kernel, len(lefts)), [array(shape), array...  1.99 us
  transfers between devices with their start and end apart: 18, of which 10 were waited for; matrix products, arithmetic and copies ran while one was open for 0% of the time, Pallas kernels for 10%

profile of v2, /device:TPU:0, one launch (start us, length us, event | category | flops | bytes accessed | tf_op | source)
XLA Modules:
  0.0 82.9 jit_solution(17246600481527062822)
XLA Ops:
  0.7 4.5 %norm_and_first_edges.1 = (bf16[32,128,128]{2,1,0:T(8,128)(2,1)}, bf16[24,32,128]{2,1,0:T(8,128)(2,1)}, bf16[24,32,128]{2,1,0:T(8,128)(2,1)}, bf16[24,32,128]{2,1,0:T(8,128)(2,1)}, bf16[24,32,128]{2,1,0:T(8,128)(2,1)}) custom-call(s32[1]{0:T(128)S(6)} %copy.11.length, bf16[32,128,128]{2,1,0:T(8,128)(2,1)} %pair.1, f32[1,128]{1,0:T(1,128)} %bitcast.6, ...), custom_call_target="tpu_custom_call" | custom-call | bytes 1024 | tf_op jit(solution)/shard_map/norm_and_first_edges/pallas_call | solution.py:511
  5.2 3.0 %collective-permute-start = (bf16[24,32,128]{2,1,0:T(8,128)(2,1)}, bf16[24,32,128]{2,1,0:T(8,128)(2,1)S(1)}, u32[]{:S(2)}, u32[]{:S(2)}) collective-permute-start(bf16[24,32,128]{2,1,0:T(8,128)(2,1)} %get-tuple-element.35), channel_id=1, source_target_pairs={{0,2},{2,0},{4,6},{6,4},{8,10},{10,8},{12,14},{14,12},{1,3},{3,1},... | collective-permute-start | bytes 589832 | tf_op jit(solution)/shard_map/ppermute | solution.py:441
  8.2 1.6 %collective-permute-start.1 = (bf16[24,32,128]{2,1,0:T(8,128)(2,1)}, bf16[24,32,128]{2,1,0:T(8,128)(2,1)S(1)}, u32[]{:S(2)}, u32[]{:S(2)}) collective-permute-start(bf16[24,32,128]{2,1,0:T(8,128)(2,1)} %get-tuple-element.36), channel_id=1, source_target_pairs={{0,4},{2,6},{4,0},{6,2},{8,12},{10,14},{12,8},{14,10},{1,5},{3,7},... | collective-permute-start | bytes 589832 | tf_op jit(solution)/shard_map/ppermute | solution.py:441
  9.8 1.2 %copy-done = bf16[32,128,128]{2,1,0:T(8,128)(2,1)S(1)} copy-done((bf16[32,128,128]{2,1,0:T(8,128)(2,1)S(1)}, bf16[32,128,128]{2,1,0:T(8,128)(2,1)}, u32[]{:S(2)}) %copy-start) | copy-done | bytes 1048600
  11.0 0.8 %copy-done.3 = bf16[128,256]{1,0:T(8,128)(2,1)S(1)} copy-done((bf16[128,256]{1,0:T(8,128)(2,1)S(1)}, bf16[128,256]{1,0:T(8,128)(2,1)}, u32[]{:S(2)}) %copy-start.3) | copy-done | bytes 65560
  11.8 0.8 %copy-done.4 = bf16[128,256]{1,0:T(8,128)(2,1)S(1)} copy-done((bf16[128,256]{1,0:T(8,128)(2,1)S(1)}, bf16[128,256]{1,0:T(8,128)(2,1)}, u32[]{:S(2)}) %copy-start.4) | copy-done | bytes 65560
  12.7 2.1 %later_edges.1 = (bf16[40,32,128]{2,1,0:T(8,128)(2,1)S(1)}, bf16[40,32,128]{2,1,0:T(8,128)(2,1)S(1)}, bf16[40,32,128]{2,1,0:T(8,128)(2,1)S(1)}, bf16[40,32,128]{2,1,0:T(8,128)(2,1)S(1)}) custom-call(s32[1]{0:T(128)S(6)} %copy.11.length, bf16[32,128,128]{2,1,0:T(8,128)(2,1)S(1)} %copy-done, bf16[128,256]{1,0:T(8,128)(2,1)S(1)} %copy-done.3, ...), custom_call_target="tpu_custom_call" | custom-call | bytes 1024 | tf_op jit(solution)/shard_map/later_edges/pallas_call | solution.py:450
  14.8 2.0 %collective-permute-start.5 = (bf16[40,32,128]{2,1,0:T(8,128)(2,1)S(1)}, bf16[40,32,128]{2,1,0:T(8,128)(2,1)S(1)}, u32[]{:S(2)}, u32[]{:S(2)}) collective-permute-start(bf16[40,32,128]{2,1,0:T(8,128)(2,1)S(1)} %get-tuple-element.41), channel_id=1, source_target_pairs={{0,2},{2,0},{4,6},{6,4},{8,10},{10,8},{12,14},{14,12},{1,3},{3,1},... | collective-permute-start | bytes 983048 | tf_op jit(solution)/shard_map/ppermute | solution.py:441
  16.8 1.6 %collective-permute-start.6 = (bf16[40,32,128]{2,1,0:T(8,128)(2,1)S(1)}, bf16[40,32,128]{2,1,0:T(8,128)(2,1)S(1)}, u32[]{:S(2)}, u32[]{:S(2)}) collective-permute-start(bf16[40,32,128]{2,1,0:T(8,128)(2,1)S(1)} %get-tuple-element.42), channel_id=1, source_target_pairs={{0,4},{2,6},{4,0},{6,2},{8,12},{10,14},{12,8},{14,10},{1,5},{3,7},... | collective-permute-start | bytes 983048 | tf_op jit(solution)/shard_map/ppermute | solution.py:441
  18.4 1.2 %collective-permute-done.2.d.refs_7_ = bf16[24,32,128]{2,1,0:T(8,128)(2,1)S(1)} collective-permute-done((bf16[24,32,128]{2,1,0:T(8,128)(2,1)}, bf16[24,32,128]{2,1,0:T(8,128)(2,1)S(1)}, u32[]{:S(2)}, u32[]{:S(2)}) %collective-permute-start.2) | collective-permute-done | bytes 196640 | tf_op jit(solution)/shard_map/ppermute | solution.py:441
  19.6 0.9 %copy-done.2 = bf16[24,32,128]{2,1,0:T(8,128)(2,1)S(1)} copy-done((bf16[24,32,128]{2,1,0:T(8,128)(2,1)S(1)}, bf16[24,32,128]{2,1,0:T(8,128)(2,1)}, u32[]{:S(2)}) %copy-start.2) | copy-done | bytes 196632
  20.7 0.5 collective-permute-start.4
  21.2 0.9 %collective-permute-done.3.refs_1_ = bf16[6,128,128]{2,1,0:T(8,128)(2,1)S(1)} collective-permute-done((bf16[6,128,128]{2,1,0:T(8,128)(2,1)S(1)}, bf16[6,128,128]{2,1,0:T(8,128)(2,1)S(1)}, u32[]{:S(2)}, u32[]{:S(2)}) %collective-permute-start.3) | collective-permute-done | bytes 196640 | tf_op jit(solution)/shard_map/ppermute | solution.py:20
  22.4 2.0 %contract.2 = (bf16[12,128,128]{2,1,0:T(8,128)(2,1)S(1)}, f32[12,128,128]{2,1,0:T(8,128)S(1)}) custom-call(bf16[6,128,128]{2,1,0:T(8,128)(2,1)S(1)} %get-tuple-element.38.refs_0_, bf16[6,128,128]{2,1,0:T(8,128)(2,1)S(1)} %collective-permute-done.3.refs_1_, bf16[6,128,128]{2,1,0:T(8,128)(2,1)S(1)} %get-tuple-element.39.refs_2_, ...), custom_call_target="tpu_custom_call" | custom-call | bytes 1024 | tf_op jit(solution)/shard_map/contract/pallas_call | solution.py:492
  24.4 2.9 %collective-permute-start.14 = (bf16[12,128,128]{2,1,0:T(8,128)(2,1)S(1)}, bf16[12,128,128]{2,1,0:T(8,128)(2,1)S(1)}, u32[]{:S(2)}, u32[]{:S(2)}) collective-permute-start(bf16[12,128,128]{2,1,0:T(8,128)(2,1)S(1)} %get-tuple-element.40.after), channel_id=1, source_target_pairs={{0,8},{2,10},{4,12},{6,14},{8,0},{10,2},{12,4},{14,6},{1,9},{3,11}... | collective-permute-start | bytes 1179656 | tf_op jit(solution)/shard_map/ppermute | solution.py:441
  27.3 1.1 %output_gate.1.after.refs_8_ = f32[32,128,128]{2,1,0:T(8,128)S(1)} custom-call(bf16[12,128,128]{2,1,0:T(8,128)(2,1)S(1)} %get-tuple-element.40.after, bf16[32,128,128]{2,1,0:T(8,128)(2,1)S(1)} %copy-done.1, bf16[128,128]{1,0:T(8,128)(2,1)S(1)} %copy-done.5), custom_call_target="tpu_custom_call" | custom-call | bytes 1024 | tf_op jit(solution)/shard_map/output_gate/pallas_call | solution.py:533
  28.4 10.0 %collective-permute-done.7.d.refs_7_ = bf16[40,32,128]{2,1,0:T(8,128)(2,1)S(1)} collective-permute-done((bf16[40,32,128]{2,1,0:T(8,128)(2,1)S(1)}, bf16[40,32,128]{2,1,0:T(8,128)(2,1)S(1)}, u32[]{:S(2)}, u32[]{:S(2)}) %collective-permute-start.7) | collective-permute-done | bytes 327712 | tf_op jit(solution)/shard_map/ppermute | solution.py:441
  39.2 1.1 %collective-permute-done.8.refs_1_ = bf16[10,128,128]{2,1,0:T(8,128)(2,1)S(1)} collective-permute-done((bf16[10,128,128]{2,1,0:T(8,128)(2,1)S(1)}, bf16[10,128,128]{2,1,0:T(8,128)(2,1)S(1)}, u32[]{:S(2)}, u32[]{:S(2)}) %collective-permute-start.8) | collective-permute-done | bytes 327712 | tf_op jit(solution)/shard_map/ppermute | solution.py:20
  40.3 0.5 collective-permute-done.9.refs_3_
  40.8 1.6 %contract.3 = (bf16[20,32,128]{2,1,0:T(8,128)(2,1)S(1)}, bf16[20,32,128]{2,1,0:T(8,128)(2,1)S(1)}, bf16[20,32,128]{2,1,0:T(8,128)(2,1)S(1)}, bf16[20,32,128]{2,1...) custom-call(bf16[10,128,128]{2,1,0:T(8,128)(2,1)S(1)} %get-tuple-ele, ...), custom_call_target="tpu_custom_call" | custom-call | bytes 1024 | tf_op jit(solution)/shard_map/contract/pallas_call | solution.py:503
  42.4 0.7 collective-permute-start.10
  43.1 4.4 %collective-permute-start.11 = (bf16[20,32,128]{2,1,0:T(8,128)(2,1)S(1)}, bf16[20,32,128]{2,1,0:T(8,128)(2,1)S(1)}, u32[]{:S(2)}, u32[]{:S(2)}) collective-permute-start(bf16[20,32,128]{2,1,0:T(8,128)(2,1)S(1)} %get-tuple-element.47), channel_id=1, source_target_pairs={{0,10},{2,8},{4,14},{6,12},{8,2},{10,0},{12,6},{14,4},{1,11},{3,9}... | collective-permute-start | bytes 491528 | tf_op jit(solution)/shard_map/ppermute | solution.py:441
  47.6 1.3 %add_halves.1 = (bf16[32,32,128]{2,1,0:T(8,128)(2,1)S(1)}, bf16[32,32,128]{2,1,0:T(8,128)(2,1)S(1)}, bf16[32,32,128]{2,1,0:T(8,128)(2,1)S(1)}, bf16[32,32,128]{2,1,0:T(8,128)(2,1)S(1)}) custom-call(f32[12,128,128]{2,1,0:T(8,128)S(1)} %get-tuple-element.50.keep, bf16[12,128,128]{2,1,0:T(8,128)(2,1)S(1)} %collective-permute-done.14.arrived, ...), custom_call_target="tpu_custom_call" | custom-call | bytes 1024 | tf_op jit(solution)/shard_map/add_halves/pallas_call | solution.py:548
  49.0 6.8 %collective-permute-start.16 = (bf16[32,32,128]{2,1,0:T(8,128)(2,1)S(1)}, bf16[32,32,128]{2,1,0:T(8,128)(2,1)S(1)}, u32[]{:S(2)}, u32[]{:S(2)}) collective-permute-start(bf16[32,32,128]{2,1,0:T(8,128)(2,1)S(1)} %get-tuple-element.57), channel_id=1, source_target_pairs={{0,4},{2,6},{4,0},{6,2},{8,12},{10,14},{12,8},{14,10},{1,5},{3,7},... | collective-permute-start | bytes 786440 | tf_op jit(solution)/shard_map/ppermute | solution.py:441
  55.8 0.7 collective-permute-start.17
  56.5 0.5 collective-permute-done.10.refs_0_
  57.1 4.5 %collective-permute-start.12 = (bf16[20,32,128]{2,1,0:T(8,128)(2,1)S(1)}, bf16[20,32,128]{2,1,0:T(8,128)(2,1)S(1)}, u32[]{:S(2)}, u32[]{:S(2)}) collective-permute-start(bf16[20,32,128]{2,1,0:T(8,128)(2,1)S(1)} %get-tuple-element.48), channel_id=1, source_target_pairs={{0,12},{2,14},{4,8},{6,10},{8,4},{10,6},{12,0},{14,2},{1,13},{3,15... | collective-permute-start | bytes 491528 | tf_op jit(solution)/shard_map/ppermute | solution.py:441
  61.6 3.3 %collective-permute-start.13 = (bf16[20,32,128]{2,1,0:T(8,128)(2,1)S(1)}, bf16[20,32,128]{2,1,0:T(8,128)(2,1)S(1)}, u32[]{:S(2)}, u32[]{:S(2)}) collective-permute-start(bf16[20,32,128]{2,1,0:T(8,128)(2,1)S(1)} %get-tuple-element.49), channel_id=1, source_target_pairs={{0,14},{2,12},{4,10},{6,8},{8,6},{10,4},{12,2},{14,0},{1,15},{3,13... | collective-permute-start | bytes 491528 | tf_op jit(solution)/shard_map/ppermute | solution.py:441
  64.9 6.8 %collective-permute-done.12.refs_2_ = bf16[20,32,128]{2,1,0:T(8,128)(2,1)S(1)} collective-permute-done((bf16[20,32,128]{2,1,0:T(8,128)(2,1)S(1)}, bf16[20,32,128]{2,1,0:T(8,128)(2,1)S(1)}, u32[]{:S(2)}, u32[]{:S(2)}) %collective-permute-start.12) | collective-permute-done | bytes 163872 | tf_op jit(solution)/shard_map/ppermute | solution.py:441
  71.7 2.2 %collective-permute-done.13.refs_3_ = bf16[20,32,128]{2,1,0:T(8,128)(2,1)S(1)} collective-permute-done((bf16[20,32,128]{2,1,0:T(8,128)(2,1)S(1)}, bf16[20,32,128]{2,1,0:T(8,128)(2,1)S(1)}, u32[]{:S(2)}, u32[]{:S(2)}) %collective-permute-start.13) | collective-permute-done | bytes 163872 | tf_op jit(solution)/shard_map/ppermute | solution.py:441
  73.9 3.6 %collective-permute-done.17.refs_7_ = bf16[32,32,128]{2,1,0:T(8,128)(2,1)S(1)} collective-permute-done((bf16[32,32,128]{2,1,0:T(8,128)(2,1)S(1)}, bf16[32,32,128]{2,1,0:T(8,128)(2,1)S(1)}, u32[]{:S(2)}, u32[]{:S(2)}) %collective-permute-start.17) | collective-permute-done | bytes 262176 | tf_op jit(solution)/shard_map/ppermute | solution.py:441
  77.5 5.4 %norm_and_project_out.1 = bf16[32,128,128]{2,1,0:T(8,128)(2,1)} custom-call(bf16[20,32,128]{2,1,0:T(8,128)(2,1)S(1)} %collective-permute-done.10.refs_0_, bf16[20,32,128]{2,1,0:T(8,128)(2,1)S(1)} %collective-permute-done.11.refs_1_, bf16[20,32,128]{2,1,0:T(8,128)(2,1)S(1)} %collective-permute-done.12.refs_2_, ...), custom_call_target="tpu_custom_call" | custom-call | bytes 1024 | tf_op jit(solution)/shard_map/norm_and_project_out/pallas_call | solution.py:560
  (31 shorter events, 1.3 us)
Async XLA Ops:
  0.7 26.6 %copy-start.5 = (bf16[128,128]{1,0:T(8,128)(2,1)S(1)}, bf16[128,128]{1,0:T(8,128)(2,1)}, u32[]{:S(2)}) copy-start(bf16[128,128]{1,0:T(8,128)(2,1)} %weights.1) | copy-start | bytes 98308
  5.2 13.2 %collective-permute-start = (bf16[24,32,128]{2,1,0:T(8,128)(2,1)}, bf16[24,32,128]{2,1,0:T(8,128)(2,1)S(1)}, u32[]{:S(2)}, u32[]{:S(2)}) collective-permute-start(bf16[24,32,128]{2,1,0:T(8,128)(2,1)} %get-tuple-element.35), channel_id=1, source_target_pairs={{0,2},{2,0},{4,6},{6,4},{8,10},{10,8},{12,14},{14,12},{1,3},{3,1},... | collective-permute-start | bytes 589832 | tf_op jit(solution)/shard_map/ppermute | solution.py:441
  8.2 10.2 %collective-permute-start.1 = (bf16[24,32,128]{2,1,0:T(8,128)(2,1)}, bf16[24,32,128]{2,1,0:T(8,128)(2,1)S(1)}, u32[]{:S(2)}, u32[]{:S(2)}) collective-permute-start(bf16[24,32,128]{2,1,0:T(8,128)(2,1)} %get-tuple-element.36), channel_id=1, source_target_pairs={{0,4},{2,6},{4,0},{6,2},{8,12},{10,14},{12,8},{14,10},{1,5},{3,7},... | collective-permute-start | bytes 589832 | tf_op jit(solution)/shard_map/ppermute | solution.py:441
  9.8 9.8 %collective-permute-start.2 = (bf16[24,32,128]{2,1,0:T(8,128)(2,1)}, bf16[24,32,128]{2,1,0:T(8,128)(2,1)S(1)}, u32[]{:S(2)}, u32[]{:S(2)}) collective-permute-start(bf16[24,32,128]{2,1,0:T(8,128)(2,1)} %get-tuple-element.37), channel_id=1, source_target_pairs={{0,6},{2,4},{4,2},{6,0},{8,14},{10,12},{12,10},{14,8},{1,7},{3,5},... | collective-permute-start | bytes 589832 | tf_op jit(solution)/shard_map/ppermute | solution.py:441
  9.8 1.2 %copy-start = (bf16[32,128,128]{2,1,0:T(8,128)(2,1)S(1)}, bf16[32,128,128]{2,1,0:T(8,128)(2,1)}, u32[]{:S(2)}) copy-start(bf16[32,128,128]{2,1,0:T(8,128)(2,1)} %get-tuple-element.32.normed) | copy-start | bytes 3145732
  11.0 0.8 %copy-start.3 = (bf16[128,256]{1,0:T(8,128)(2,1)S(1)}, bf16[128,256]{1,0:T(8,128)(2,1)}, u32[]{:S(2)}) copy-start(bf16[128,256]{1,0:T(8,128)(2,1)} %proj.3) | copy-start | bytes 196612
  11.8 0.8 %copy-start.4 = (bf16[128,256]{1,0:T(8,128)(2,1)S(1)}, bf16[128,256]{1,0:T(8,128)(2,1)}, u32[]{:S(2)}) copy-start(bf16[128,256]{1,0:T(8,128)(2,1)} %gate.3) | copy-start | bytes 196612
  12.7 14.6 %copy-start.1 = (bf16[32,128,128]{2,1,0:T(8,128)(2,1)S(1)}, bf16[32,128,128]{2,1,0:T(8,128)(2,1)}, u32[]{:S(2)}) copy-start(bf16[32,128,128]{2,1,0:T(8,128)(2,1)} %get-tuple-element.32.normed) | copy-start | bytes 3145732
  14.8 13.6 %collective-permute-start.5 = (bf16[40,32,128]{2,1,0:T(8,128)(2,1)S(1)}, bf16[40,32,128]{2,1,0:T(8,128)(2,1)S(1)}, u32[]{:S(2)}, u32[]{:S(2)}) collective-permute-start(bf16[40,32,128]{2,1,0:T(8,128)(2,1)S(1)} %get-tuple-element.41), channel_id=1, source_target_pairs={{0,2},{2,0},{4,6},{6,4},{8,10},{10,8},{12,14},{14,12},{1,3},{3,1},... | collective-permute-start | bytes 983048 | tf_op jit(solution)/shard_map/ppermute | solution.py:441
  16.8 11.7 %collective-permute-start.6 = (bf16[40,32,128]{2,1,0:T(8,128)(2,1)S(1)}, bf16[40,32,128]{2,1,0:T(8,128)(2,1)S(1)}, u32[]{:S(2)}, u32[]{:S(2)}) collective-permute-start(bf16[40,32,128]{2,1,0:T(8,128)(2,1)S(1)} %get-tuple-element.42), channel_id=1, source_target_pairs={{0,4},{2,6},{4,0},{6,2},{8,12},{10,14},{12,8},{14,10},{1,5},{3,7},... | collective-permute-start | bytes 983048 | tf_op jit(solution)/shard_map/ppermute | solution.py:441
  18.3 20.1 %collective-permute-start.7 = (bf16[40,32,128]{2,1,0:T(8,128)(2,1)S(1)}, bf16[40,32,128]{2,1,0:T(8,128)(2,1)S(1)}, u32[]{:S(2)}, u32[]{:S(2)}) collective-permute-start(bf16[40,32,128]{2,1,0:T(8,128)(2,1)S(1)} %get-tuple-element.43), channel_id=1, source_target_pairs={{0,6},{2,4},{4,2},{6,0},{8,14},{10,12},{12,10},{14,8},{1,7},{3,5},... | collective-permute-start | bytes 983048 | tf_op jit(solution)/shard_map/ppermute | solution.py:441
  19.6 0.9 %copy-start.2 = (bf16[24,32,128]{2,1,0:T(8,128)(2,1)S(1)}, bf16[24,32,128]{2,1,0:T(8,128)(2,1)}, u32[]{:S(2)}) copy-start(bf16[24,32,128]{2,1,0:T(8,128)(2,1)} %get-tuple-element.34.a.refs_4_) | copy-start | bytes 589828
  20.6 1.5 %collective-permute-start.3 = (bf16[6,128,128]{2,1,0:T(8,128)(2,1)S(1)}, bf16[6,128,128]{2,1,0:T(8,128)(2,1)S(1)}, u32[]{:S(2)}, u32[]{:S(2)}) collective-permute-start(bf16[6,128,128]{2,1,0:T(8,128)(2,1)S(1)} %get-tuple-element.38.refs_0_), channel_id=1, source_target_pairs={{0,1},{1,0},{2,3},{3,2},{4,5},{5,4},{6,7},{7,6},{8,9},{9,8},{10,11... | collective-permute-start | bytes 589832 | tf_op jit(solution)/shard_map/ppermute | solution.py:20
  20.7 1.7 %collective-permute-start.4 = (bf16[6,128,128]{2,1,0:T(8,128)(2,1)S(1)}, bf16[6,128,128]{2,1,0:T(8,128)(2,1)S(1)}, u32[]{:S(2)}, u32[]{:S(2)}) collective-permute-start(bf16[6,128,128]{2,1,0:T(8,128)(2,1)S(1)} %get-tuple-element.39.refs_2_), channel_id=1, source_target_pairs={{0,1},{1,0},{2,3},{3,2},{4,5},{5,4},{6,7},{7,6},{8,9},{9,8},{10,11... | collective-permute-start | bytes 589832 | tf_op jit(solution)/shard_map/ppermute | solution.py:20
  24.4 23.1 %collective-permute-start.14 = (bf16[12,128,128]{2,1,0:T(8,128)(2,1)S(1)}, bf16[12,128,128]{2,1,0:T(8,128)(2,1)S(1)}, u32[]{:S(2)}, u32[]{:S(2)}) collective-permute-start(bf16[12,128,128]{2,1,0:T(8,128)(2,1)S(1)} %get-tuple-element.40.after), channel_id=1, source_target_pairs={{0,8},{2,10},{4,12},{6,14},{8,0},{10,2},{12,4},{14,6},{1,9},{3,11}... | collective-permute-start | bytes 1179656 | tf_op jit(solution)/shard_map/ppermute | solution.py:441
  38.6 1.7 %collective-permute-start.8 = (bf16[10,128,128]{2,1,0:T(8,128)(2,1)S(1)}, bf16[10,128,128]{2,1,0:T(8,128)(2,1)S(1)}, u32[]{:S(2)}, u32[]{:S(2)}) collective-permute-start(bf16[10,128,128]{2,1,0:T(8,128)(2,1)S(1)} %get-tuple-element.44.refs_0_), channel_id=1, source_target_pairs={{0,1},{1,0},{2,3},{3,2},{4,5},{5,4},{6,7},{7,6},{8,9},{9,8},{10,11... | collective-permute-start | bytes 983048 | tf_op jit(solution)/shard_map/ppermute | solution.py:20
  38.7 38.8 %copy-start.6 = (bf16[128,128]{1,0:T(8,128)(2,1)S(1)}, bf16[128,128]{1,0:T(8,128)(2,1)}, u32[]{:S(2)}) copy-start(bf16[128,128]{1,0:T(8,128)(2,1)} %refs_11_.1) | copy-start | bytes 98308
  38.7 38.8 %copy-start.7 = (f32[128]{0:T(128)S(1)}, f32[128]{0:T(128)}, u32[]{:S(2)}) copy-start(f32[128]{0:T(128)} %param.17) | copy-start | bytes 1540
  38.8 38.8 %copy-start.8 = (f32[128]{0:T(128)S(1)}, f32[128]{0:T(128)}, u32[]{:S(2)}) copy-start(f32[128]{0:T(128)} %param.18) | copy-start | bytes 1540
  38.8 2.0 %collective-permute-start.9 = (bf16[10,128,128]{2,1,0:T(8,128)(2,1)S(1)}, bf16[10,128,128]{2,1,0:T(8,128)(2,1)S(1)}, u32[]{:S(2)}, u32[]{:S(2)}) collective-permute-start(bf16[10,128,128]{2,1,0:T(8,128)(2,1)S(1)} %get-tuple-element.45.refs_2_), channel_id=1, source_target_pairs={{0,1},{1,0},{2,3},{3,2},{4,5},{5,4},{6,7},{7,6},{8,9},{9,8},{10,11... | collective-permute-start | bytes 983048 | tf_op jit(solution)/shard_map/ppermute | solution.py:20
  42.4 14.6 %collective-permute-start.10 = (bf16[20,32,128]{2,1,0:T(8,128)(2,1)S(1)}, bf16[20,32,128]{2,1,0:T(8,128)(2,1)S(1)}, u32[]{:S(2)}, u32[]{:S(2)}) collective-permute-start(bf16[20,32,128]{2,1,0:T(8,128)(2,1)S(1)} %get-tuple-element.46), channel_id=1, source_target_pairs={{0,8},{2,10},{4,12},{6,14},{8,0},{10,2},{12,4},{14,6},{1,9},{3,11}... | collective-permute-start | bytes 491528 | tf_op jit(solution)/shard_map/ppermute | solution.py:441
  43.1 18.5 %collective-permute-start.11 = (bf16[20,32,128]{2,1,0:T(8,128)(2,1)S(1)}, bf16[20,32,128]{2,1,0:T(8,128)(2,1)S(1)}, u32[]{:S(2)}, u32[]{:S(2)}) collective-permute-start(bf16[20,32,128]{2,1,0:T(8,128)(2,1)S(1)} %get-tuple-element.47), channel_id=1, source_target_pairs={{0,10},{2,8},{4,14},{6,12},{8,2},{10,0},{12,6},{14,4},{1,11},{3,9}... | collective-permute-start | bytes 491528 | tf_op jit(solution)/shard_map/ppermute | solution.py:441
  48.9 25.0 %collective-permute-start.15 = (bf16[32,32,128]{2,1,0:T(8,128)(2,1)S(1)}, bf16[32,32,128]{2,1,0:T(8,128)(2,1)S(1)}, u32[]{:S(2)}, u32[]{:S(2)}) collective-permute-start(bf16[32,32,128]{2,1,0:T(8,128)(2,1)S(1)} %get-tuple-element.56), channel_id=1, source_target_pairs={{0,2},{2,0},{4,6},{6,4},{8,10},{10,8},{12,14},{14,12},{1,3},{3,1},... | collective-permute-start | bytes 786440 | tf_op jit(solution)/shard_map/ppermute | solution.py:441
  49.0 24.9 %collective-permute-start.16 = (bf16[32,32,128]{2,1,0:T(8,128)(2,1)S(1)}, bf16[32,32,128]{2,1,0:T(8,128)(2,1)S(1)}, u32[]{:S(2)}, u32[]{:S(2)}) collective-permute-start(bf16[32,32,128]{2,1,0:T(8,128)(2,1)S(1)} %get-tuple-element.57), channel_id=1, source_target_pairs={{0,4},{2,6},{4,0},{6,2},{8,12},{10,14},{12,8},{14,10},{1,5},{3,7},... | collective-permute-start | bytes 786440 | tf_op jit(solution)/shard_map/ppermute | solution.py:441
  55.8 21.7 %collective-permute-start.17 = (bf16[32,32,128]{2,1,0:T(8,128)(2,1)S(1)}, bf16[32,32,128]{2,1,0:T(8,128)(2,1)S(1)}, u32[]{:S(2)}, u32[]{:S(2)}) collective-permute-start(bf16[32,32,128]{2,1,0:T(8,128)(2,1)S(1)} %get-tuple-element.58), channel_id=1, source_target_pairs={{0,6},{2,4},{4,2},{6,0},{8,14},{10,12},{12,10},{14,8},{1,7},{3,5},... | collective-permute-start | bytes 786440 | tf_op jit(solution)/shard_map/ppermute | solution.py:441
  57.1 14.6 %collective-permute-start.12 = (bf16[20,32,128]{2,1,0:T(8,128)(2,1)S(1)}, bf16[20,32,128]{2,1,0:T(8,128)(2,1)S(1)}, u32[]{:S(2)}, u32[]{:S(2)}) collective-permute-start(bf16[20,32,128]{2,1,0:T(8,128)(2,1)S(1)} %get-tuple-element.48), channel_id=1, source_target_pairs={{0,12},{2,14},{4,8},{6,10},{8,4},{10,6},{12,0},{14,2},{1,13},{3,15... | collective-permute-start | bytes 491528 | tf_op jit(solution)/shard_map/ppermute | solution.py:441
  61.6 12.2 %collective-permute-start.13 = (bf16[20,32,128]{2,1,0:T(8,128)(2,1)S(1)}, bf16[20,32,128]{2,1,0:T(8,128)(2,1)S(1)}, u32[]{:S(2)}, u32[]{:S(2)}) collective-permute-start(bf16[20,32,128]{2,1,0:T(8,128)(2,1)S(1)} %get-tuple-element.49), channel_id=1, source_target_pairs={{0,14},{2,12},{4,10},{6,8},{8,6},{10,4},{12,2},{14,0},{1,15},{3,13... | collective-permute-start | bytes 491528 | tf_op jit(solution)/shard_map/ppermute | solution.py:441

commit v3 on v0

v3 whole, which is shorter than its diff:
```python
import functools

import jax
import jax.numpy as jnp
from jax import lax
from jax.experimental import pallas as pl
from jax.experimental.pallas import tpu as pltpu
from jax.sharding import PartitionSpec as P

epsilon = 1e-05
chunk_sizes = (12, 20)
swap_pieces = ((6, 6), (10, 10))
vmem_all = 60 * 1024 * 1024
vmem_part = 28 * 1024 * 1024


def from_partner(value, axis, apart):
    mask = 2**apart
    pairs = [(source, source ^ mask) for source in range(lax.axis_size(axis))]
    return lax.ppermute(value, axis, pairs)


def normalize_in(pair, gain, bias):
    widened = pair.astype(jnp.float32)
    average = jnp.mean(widened, axis=-1, keepdims=True)
    centered = widened - average
    spread = jnp.mean(centered * centered, axis=-1, keepdims=True)
    return (centered * lax.rsqrt(spread + epsilon) * gain + bias).astype(jnp.bfloat16)


def token_mask(tile_rows, tile_cols, length):
    row_start = lax.axis_index("row") * tile_rows
    col_start = lax.axis_index("col") * tile_cols
    valid_rows = row_start + jnp.arange(tile_rows, dtype=jnp.int32) < length[0]
    valid_cols = col_start + jnp.arange(tile_cols, dtype=jnp.int32) < length[0]
    return (valid_rows[:, None] & valid_cols[None, :]).astype(jnp.float32)


def make_edges(normed, proj, gate, mask):
    projected = jnp.einsum("ijc,ch->hij", normed, proj, preferred_element_type=jnp.float32)
    gating = jnp.einsum("ijc,ch->hij", normed, gate, preferred_element_type=jnp.float32)
    return (jax.nn.sigmoid(gating) * projected * mask[None]).astype(jnp.bfloat16)


def finish(contracted, normed, gate_out, gain, bias, proj_out):
    widened = contracted.astype(jnp.float32)
    average = jnp.mean(widened, axis=0, keepdims=True)
    centered = widened - average
    spread = jnp.mean(centered * centered, axis=0, keepdims=True)
    scaled = centered * lax.rsqrt(spread + epsilon) * gain[:, None, None]
    contracted_norm = (scaled + bias[:, None, None]).astype(jnp.bfloat16)
    out_gate = jax.nn.sigmoid(
        jnp.einsum("ijc,cd->ijd", normed, gate_out, preferred_element_type=jnp.float32)
    )
    projected_out = jnp.einsum(
        "hij,hc->ijc", contracted_norm, proj_out, preferred_element_type=jnp.float32
    )
    return (out_gate * projected_out).astype(jnp.bfloat16)


def contract(left, right):
    return jnp.einsum("hki,hkj->hij", left, right, preferred_element_type=jnp.float32)


def shards_by_exchange(
    pair,
    length,
    norm_in_gain,
    norm_in_bias,
    proj_in,
    gate_in,
    gate_out,
    norm_out_gain,
    norm_out_bias,
    proj_out,
):
    hidden = proj_out.shape[0]
    normed = normalize_in(pair, norm_in_gain, norm_in_bias)
    mask = token_mask(pair.shape[0], pair.shape[1], length)
    edges = make_edges(normed, proj_in, gate_in, mask)
    left_rows = lax.all_to_all(edges[:hidden], "row", split_axis=0, concat_axis=1, tiled=True)
    right_rows = lax.all_to_all(edges[hidden:], "row", split_axis=0, concat_axis=1, tiled=True)
    other_half = from_partner(left_rows, "col", 0)
    first_col = lax.axis_index("col") == 0
    left_full = jnp.where(
        first_col,
        jnp.concatenate([left_rows, other_half], axis=2),
        jnp.concatenate([other_half, left_rows], axis=2),
    )
    contracted = contract(left_full, right_rows).astype(jnp.bfloat16)
    returned = lax.all_to_all(contracted, "row", split_axis=1, concat_axis=0, tiled=True)
    return finish(returned, normed, gate_out, norm_out_gain, norm_out_bias, proj_out)


in_smem = pl.BlockSpec(memory_space=pltpu.SMEM)
in_any = pl.BlockSpec(memory_space=pl.ANY)
in_vmem = pl.BlockSpec(memory_space=pltpu.VMEM)
matmul_tn = (((0,), (0,)), ((), ()))
matmul_nt = (((1,), (1,)), ((), ()))


def call(kernel, outputs, scratch, specs, out_specs, name, limit=vmem_part):
    return pl.pallas_call(
        kernel,
        out_shape=outputs,
        in_specs=specs,
        out_specs=out_specs,
        scratch_shapes=scratch,
        compiler_params=pltpu.CompilerParams(vmem_limit_bytes=limit),
        name=name,
    )


def array(shape, dtype=jnp.bfloat16):
    return jax.ShapeDtypeStruct(shape, dtype)


def load(source, target, sem):
    copy = pltpu.make_async_copy(source, target, sem)
    copy.start()
    return copy


def chosen_weights(start, size, slots, row, proj, gate):
    width = proj.shape[1]
    first_slot, slot_count = slots
    count = 2 * slot_count * size
    at = lax.broadcasted_iota(jnp.int32, (count, width), 0)
    side, inside = at // (slot_count * size), at % (slot_count * size)
    slot, channel = first_slot + inside // size, inside % size
    source = side * (width // 2) + start + ((row % 4) ^ slot) * size + channel
    one_hot = (lax.broadcasted_iota(jnp.int32, (count, width), 1) == source).astype(jnp.bfloat16)
    picked = [
        lax.dot_general(one_hot, weights, matmul_nt, preferred_element_type=jnp.float32)
        for weights in (proj, gate)
    ]
    return jnp.concatenate(picked, axis=0).astype(jnp.bfloat16)


def block_edges(length, normed, weights, at, row_start, col_start, outs):
    rows, tile_cols, channels = normed.shape
    size = outs[0].shape[0] // 2
    pairs = lax.dot_general(
        weights,
        normed.reshape(rows * tile_cols, channels),
        matmul_nt,
        preferred_element_type=jnp.float32,
    )
    count = pairs.shape[0] // 2
    values = jax.nn.sigmoid(pairs[count:]) * pairs[:count]
    cols = col_start + lax.broadcasted_iota(jnp.int32, (count, tile_cols), 1)
    masked = []
    for row in range(rows):
        limit = jnp.where(row_start + at + row < length, length, 0)
        piece = values[:, row * tile_cols : (row + 1) * tile_cols]
        masked.append(jnp.where(cols < limit, piece, 0.0))
    swapped = jnp.swapaxes(jnp.stack(masked, axis=0), 0, 1).astype(jnp.bfloat16)
    for slot, out in enumerate(outs):
        for side in range(2):
            first = (side * len(outs) + slot) * size
            out[side * size : (side + 1) * size, at : at + rows, :] = swapped[first : first + size]


def first_kernel(bounds, length, pair, gain, bias, proj, gate, normed, *rest):
    start, size, rows = bounds
    outs = rest[:3]
    pair_held, gain_held, bias_held, proj_held, gate_held, normed_held = rest[3:9]
    helds, sems = rest[9:12], rest[12]
    tile_rows, tile_cols, channels = pair.shape
    blocks = tile_rows // rows
    parts = [pl.ds(b * rows, rows) for b in range(blocks)]
    pieces = [load(pair.at[p], pair_held.at[p], sems.at[b, 0]) for b, p in enumerate(parts)]
    small = [
        load(source, target, sems.at[blocks, at])
        for at, (source, target) in enumerate(
            ((proj, proj_held), (gate, gate_held), (gain, gain_held), (bias, bias_held))
        )
    ]
    row = lax.axis_index("row")
    row_start = row * tile_rows
    col_start = lax.axis_index("col") * tile_cols
    for copy in small:
        copy.wait()
    weights = chosen_weights(start, size, (1, 3), row, proj_held[...], gate_held[...])
    mean = jnp.full((channels, channels), 1.0 / channels, jnp.bfloat16)
    stores = []
    for b, part in enumerate(parts):
        at = b * rows
        pieces[b].wait()
        tokens = pair_held[at : at + rows].reshape(rows * tile_cols, channels)
        average = jnp.dot(tokens, mean, preferred_element_type=jnp.float32)
        centered = tokens.astype(jnp.float32) - average
        spread = jnp.mean(centered * centered, axis=-1, keepdims=True)
        scaled = centered * lax.rsqrt(spread + epsilon) * gain_held[...] + bias_held[...]
        rounded = scaled.astype(jnp.bfloat16).reshape(rows, tile_cols, channels)
        normed_held[at : at + rows] = rounded
        stores.append(load(normed_held.at[part], normed.at[part], sems.at[b, 1]))
        block_edges(length[0], rounded, weights, at, row_start, col_start, helds)
        for slot, out in enumerate(outs):
            stores.append(load(helds[slot].at[:, part], out.at[:, part], sems.at[b, 2 + slot]))
    for copy in stores:
        copy.wait()


def later_kernel(bounds, length, normed, proj, gate, *outs):
    rows, *chunks = bounds
    tile_rows, tile_cols, _ = normed.shape
    row = lax.axis_index("row")
    row_start = row * tile_rows
    col_start = lax.axis_index("col") * tile_cols
    for start, size, slots in chunks:
        weights = chosen_weights(start, size, slots, row, proj[...], gate[...])
        for at in range(0, tile_rows, rows):
            tokens = normed[at : at + rows]
            targets = outs[: slots[1]]
            block_edges(length[0], tokens, weights, at, row_start, col_start, targets)
        outs = outs[slots[1] :]


def gate_kernel(rows, after, normed, weights, out):
    tile_rows, tile_cols, channels = normed.shape
    for at in range(0, tile_rows, rows):
        gating = jnp.dot(
            normed[at : at + rows].reshape(rows * tile_cols, channels),
            weights[...],
            preferred_element_type=jnp.float32,
        )
        out[at : at + rows] = jax.nn.sigmoid(gating).reshape(rows, tile_cols, channels)


def pack_kernel(after, a, b, c, d, *rest):
    outs, sems = rest[:-1], rest[-1]
    copies, start = [], 0
    for piece, out in enumerate(outs):
        size, count, _ = out.shape
        part = count // 4
        for at, ref in enumerate((a, b, c, d)):
            rows = out.at[:, pl.ds(at * part, part), :]
            copies.append(load(ref.at[pl.ds(start, size)], rows, sems.at[piece, at]))
        start += size
    for copy in copies:
        copy.wait()


def contractions(lefts, parts, store):
    size = parts[0].shape[0] // 2
    places = [(at, u) for at in range(0, len(lefts), 2) for u in range(lefts[at].shape[0])]
    low = lax.axis_index("row") < 4
    own_away = (lax.axis_index("col") == 1) == low

    def both(first):
        for u in range(size):
            right = jnp.concatenate([part[size + u] for part in parts], axis=0)
            for side in range(2):
                left = lefts[places[u][0] + (first ^ side)][places[u][1]]
                product = lax.dot_general(
                    left, right, matmul_tn, preferred_element_type=jnp.float32
                )
                store(u, side, product)

    pl.when(own_away)(functools.partial(both, 0))
    pl.when(jnp.logical_not(own_away))(functools.partial(both, 1))


def contract_kernel(count, *refs):
    lefts, parts = refs[:count], refs[count : count + 4]
    outs = refs[count + 4 :]

    def store(u, side, product):
        outs[side][u] = product.astype(outs[side].dtype)

    contractions(lefts, parts, store)


def last_contract_kernel(count, *refs):
    lefts, parts = refs[:count], refs[count : count + 4]
    outs = refs[count + 4 : count + 8], refs[count + 8 : count + 12]
    held = refs[count + 12]
    part = outs[0][0].shape[1]
    row = lax.axis_index("row")

    def store(u, side, product):
        held[u, side] = product.astype(jnp.bfloat16)
        for slot, out in enumerate(outs[side]):
            rows = pl.ds(pl.multiple_of(((row % 4) ^ slot) * part, part), part)
            out[u] = held[u, side, rows, :]

    contractions(lefts, parts, store)


def add_kernel(keep, arrived, *refs):
    lasts, outs = refs[:4], refs[4:8]
    keep_held, arrived_held, sems = refs[8:]
    size, part = keep.shape[0], outs[0].shape[1]
    row = lax.axis_index("row")
    loads = [load(keep, keep_held, sems.at[0]), load(arrived, arrived_held, sems.at[1])]
    stores = [
        load(last, out.at[pl.ds(size, last.shape[0])], sems.at[2 + at])
        for at, (last, out) in enumerate(zip(lasts, outs, strict=True))
    ]
    for copy in loads:
        copy.wait()
    for u in range(size):
        total = keep_held[u] + arrived_held[u].astype(jnp.float32)
        arrived_held[u] = total.astype(jnp.bfloat16)
    for slot, out in enumerate(outs):
        rows = pl.ds(pl.multiple_of(((row % 4) ^ slot) * part, part), part)
        stores.append(
            load(arrived_held.at[:, rows, :], out.at[pl.ds(0, size)], sems.at[6 + slot])
        )
    for copy in stores:
        copy.wait()


def finish_kernel(rows, sizes, *refs):
    aways, totals = refs[:4], refs[4:8]
    opened, gain, bias, proj, out, out_held, sems = refs[8:]
    early, late = sizes
    tile_rows = out.shape[0]
    hidden, per = proj.shape[0], early + late
    row = lax.axis_index("row")
    at = lax.broadcasted_iota(jnp.int32, (hidden, hidden), 0)
    slot, place = at // per, at % per
    owner = (row % 4) ^ slot
    channel = jnp.where(
        place < early, owner * early + place, 4 * early + owner * late + place - early
    )
    picked = lax.broadcasted_iota(jnp.int32, (hidden, hidden), 1) == channel

    def down(values):
        column = jnp.sum(jnp.where(picked, values, 0.0), axis=1, keepdims=True)
        return jnp.broadcast_to(column, (hidden, hidden))[None]

    gain_rows, bias_rows = down(gain[...]), down(bias[...])
    ordered = jnp.dot(
        picked.astype(jnp.bfloat16), proj[...], preferred_element_type=jnp.float32
    ).astype(jnp.bfloat16)
    stores = []
    for b in range(tile_rows // rows):
        own = slice(b * rows, (b + 1) * rows)
        pieces = []
        for total, away in zip(totals, aways, strict=True):
            pieces.append(total[:early, own, :].astype(jnp.float32))
            kept = total[early:, own, :].astype(jnp.float32)
            pieces.append(kept + away[:, own, :].astype(jnp.float32))
        values = jnp.concatenate(pieces, axis=0)
        centered = values - jnp.sum(values, axis=0, keepdims=True) * (1.0 / hidden)
        spread = jnp.sum(centered * centered, axis=0, keepdims=True) * (1.0 / hidden)
        swapped = jnp.swapaxes(centered * lax.rsqrt(spread + epsilon), 0, 1)
        scaled = (swapped * gain_rows + bias_rows).astype(jnp.bfloat16)
        for step in range(rows):
            projected = lax.dot_general(
                scaled[step], ordered, matmul_tn, preferred_element_type=jnp.float32
            )
            at_row = b * rows + step
            out_held[at_row] = (opened[at_row] * projected).astype(jnp.bfloat16)
        part = pl.ds(b * rows, rows)
        stores.append(load(out_held.at[part], out.at[part], sems.at[b]))
    for copy in stores:
        copy.wait()


def shards_by_halves(
    pair,
    length,
    norm_in_gain,
    norm_in_bias,
    proj_in,
    gate_in,
    gate_out,
    norm_out_gain,
    norm_out_bias,
    proj_out,
):
    tile_rows, tile_cols, channels = pair.shape
    rows = lax.axis_size("row")
    block = min(16, tile_rows)
    blocks = tile_rows // block
    early, late = chunk_sizes
    vmem, semaphores = pltpu.VMEM, pltpu.SemaphoreType.DMA
    small = jnp.bfloat16
    depth = 4 * tile_rows

    def exchanged(value, mask):
        return lax.ppermute(value, "row", [(source, source ^ mask) for source in range(rows)])

    def edge_shape(size):
        return (2 * size, tile_rows, tile_cols)

    def received(pieces):
        return [pieces[0], *[exchanged(pieces[mask], mask) for mask in (3, 2, 1)]]

    def swapped_left(at, after, pieces):
        sizes = swap_pieces[at]
        lefts = call(
            pack_kernel,
            [array((size, depth, tile_cols)) for size in sizes],
            [semaphores((len(sizes), 4))],
            [in_any] * 5,
            [in_any] * len(sizes),
            "pack_left",
        )(after, *pieces)
        return [side for left in lefts for side in (left, from_partner(left, "col", 0))]

    normed, *sent = call(
        functools.partial(first_kernel, (0, early, block)),
        [array(pair.shape), *[array(edge_shape(early))] * 3],
        [
            vmem(pair.shape, small),
            vmem((1, channels), jnp.float32),
            vmem((1, channels), jnp.float32),
            vmem(proj_in.shape, small),
            vmem(gate_in.shape, small),
            vmem(pair.shape, small),
            *[vmem(edge_shape(early), small)] * 3,
            semaphores((blocks + 1, 5)),
        ],
        [in_smem] + [in_any] * 5,
        [in_any] * 4,
        "norm_and_first_edges",
        vmem_all,
    )(length, pair, norm_in_gain[None], norm_in_bias[None], proj_in, gate_in)
    own, *second = call(
        functools.partial(later_kernel, (block, (0, early, (0, 1)), (4 * early, late, (0, 4)))),
        [array(edge_shape(early)), *[array(edge_shape(late))] * 4],
        [],
        [in_smem] + [in_vmem] * 3,
        [in_vmem] * 5,
        "later_edges",
    )(length, normed, proj_in, gate_in)
    first = received([own, *sent])
    lefts = swapped_left(0, second[0], first)
    shape = (early, depth, tile_cols)
    away, keep = call(
        functools.partial(contract_kernel, len(lefts)),
        [array(shape), array(shape, jnp.float32)],
        [],
        [in_vmem] * (len(lefts) + 4),
        [in_vmem] * 2,
        "contract",
    )(*lefts, *first)
    arrived = exchanged(away, 4)
    second = received(second)
    (opened,) = call(
        functools.partial(gate_kernel, block),
        [array(pair.shape, jnp.float32)],
        [],
        [in_any] + [in_vmem] * 2,
        [in_vmem],
        "output_gate",
    )(away, normed, gate_out)
    lefts = swapped_left(1, opened, second)
    last = call(
        functools.partial(last_contract_kernel, len(lefts)),
        [array((late, tile_rows, tile_cols))] * 8,
        [vmem((late, 2, depth, tile_cols), small)],
        [in_vmem] * (len(lefts) + 4),
        [in_vmem] * 8,
        "contract",
    )(*lefts, *second)
    aways = [exchanged(last[mask], 4 ^ mask) for mask in range(4)]
    totals = call(
        add_kernel,
        [array((early + late, tile_rows, tile_cols))] * 4,
        [
            vmem((early, depth, tile_cols), jnp.float32),
            vmem((early, depth, tile_cols), small),
            semaphores((10,)),
        ],
        [in_any] * 6,
        [in_any] * 4,
        "add_halves",
    )(keep, arrived, *last[4:])
    totals = [totals[0], *[exchanged(totals[mask], mask) for mask in (1, 2, 3)]]
    (update,) = call(
        functools.partial(finish_kernel, 8, chunk_sizes),
        [array(pair.shape)],
        [vmem(pair.shape, small), semaphores((tile_rows // 8,))],
        [in_vmem] * 12,
        [in_any],
        "norm_and_project_out",
    )(*aways, *totals, opened, norm_out_gain[None], norm_out_bias[None], proj_out)
    return update


def solution(mesh):
    placed = (P(("grp", "row"), "col", None), P("grp"), P(), P(), P(), P(), P(), P(), P(), P())
    return jax.shard_map(
        shards_by_halves if mesh.shape["row"] == 8 else shards_by_exchange,
        mesh=mesh,
        in_specs=placed,
        out_specs=P(("grp", "row"), "col", None),
        check_vma=False,
    )
```

time: 113 us -> 78.4 us (0.69)
  waiting for transfers between devices: 72.4 us -> 39.3 us
  Pallas kernels: 0 us -> 11.4 us
  matrix products: 10.4 us -> 0 us
  starting transfers between devices: 14.5 us -> 23.7 us
  local copies, waits for them, and re-layouts: 8.66 us -> 2.93 us
  other arithmetic: 5.37 us -> 0 us
    all_to_all x3 -> x0, waiting for transfers between devices: 72.4 us -> none  [the longest x1 24.9 us: shards(): lax.all_to_all(right_half, 'row', split_axis=0, concat_axis=1, tiled=True)]
    ppermute x0 -> x14, waiting for transfers between devices: none -> 36.5 us  [exchanged(): lax.ppermute(value, 'row', [(source, source ^ mask) for source in range(r...]
    ppermute x0 -> x14, starting transfers between devices: none -> 22.6 us  [exchanged(): lax.ppermute(value, 'row', [(source, source ^ mask) for source in range(r...]
    all_to_all x3 -> x0, starting transfers between devices: 14.5 us -> none  [the longest x1 7.29 us: shards(): lax.all_to_all(left_half, 'row', split_axis=0, concat_axis=1, tiled=True)]
    pallas_call x0 -> x9, Pallas kernels: none -> 11.4 us  [the longest x1 3.81 us: shards_by_halves(): call(functools.partial(first_kernel, (0, early, block)), [array(pair.shap...]
    dot_general x5 -> x0, matrix products: 10.4 us -> none  [the longest x1 2.52 us: shards(): jnp.einsum('ijc,cd->ijd', normed, gate_out, preferred_element_type=jnp.fl...]
    reduce_sum x4 -> x0, other arithmetic: 4.53 us -> none  [the longest x1 2.33 us: shards(): spread = jnp.mean(centered * centered, axis=-1, keepdims=True)]
    slice x3 -> x0, local copies, waits for them, and re-layouts: 3.98 us -> none  [the longest x2 2.31 us: shards(): left_half = edges[:hidden]]
  transfers between devices with their start and end apart: 4 -> 18, of which waited for: 3 -> 13; matrix products, arithmetic and copies ran while one was open for 5% -> 0% of each run, Pallas kernels for 0% -> 6%
where the time goes in v3:
time: 78.4 us; the launch traced here: 78.1 us
  waiting for transfers between devices  39.3 us (50%)
  starting transfers between devices  23.7 us (30%)
  Pallas kernels  11.4 us (15%)
  local copies, waits for them, and re-layouts  2.93 us (4%)
  between operations  0.8 us (1%)
    ppermute x14, waiting for transfers between devices, exchanged(): lax.ppermute(value, 'row', [(source, source ^ mask) for source in range(r...  36.5 us
    ppermute x14, starting transfers between devices, exchanged(): lax.ppermute(value, 'row', [(source, source ^ mask) for source in range(r...  22.6 us
    pallas_call x1, Pallas kernels, shards_by_halves(): call(functools.partial(first_kernel, (0, early, block)), [array(pair.shap...  3.81 us
    unnamed x16, local copies, waits for them, and re-layouts  2.93 us
    ppermute x4, waiting for transfers between devices, from_partner(): return lax.ppermute(value, axis, pairs)  2.79 us
    pallas_call x1, Pallas kernels, shards_by_halves(): call(functools.partial(finish_kernel, 8, chunk_sizes), [array(pair.shape)...  2.5 us
    pallas_call x1, Pallas kernels, shards_by_halves(): call(functools.partial(later_kernel, (block, (0, early, (0, 1)), (4 * ear...  1.93 us
  transfers between devices with their start and end apart: 18, of which 13 were waited for; matrix products, arithmetic and copies ran while one was open for 0% of the time, Pallas kernels for 6%

profile of v3, /device:TPU:0, one launch (start us, length us, event | category | flops | bytes accessed | tf_op | source)
XLA Modules:
  0.0 78.1 jit_solution(16590947385311878961)
XLA Ops:
  0.7 3.8 %norm_and_first_edges.1 = (bf16[32,128,128]{2,1,0:T(8,128)(2,1)}, bf16[24,32,128]{2,1,0:T(8,128)(2,1)}, bf16[24,32,128]{2,1,0:T(8,128)(2,1)}, bf16[24,32,128]{2,1,0:T(8,128)(2,1)}) custom-call(s32[1]{0:T(128)S(6)} %copy.11.length, bf16[32,128,128]{2,1,0:T(8,128)(2,1)} %pair.1, f32[1,128]{1,0:T(1,128)} %bitcast.6, f32[1,128]{1,0:T(1,128)} %bitcast.7, ...), custom_call_target="tpu_custom_call" | custom-call | tf_op jit(solution)/shard_map/norm_and_first_edges/pallas_call | solution.py:405
  4.5 4.0 %collective-permute-start = (bf16[24,32,128]{2,1,0:T(8,128)(2,1)}, bf16[24,32,128]{2,1,0:T(8,128)(2,1)S(1)}, u32[]{:S(2)}, u32[]{:S(2)}) collective-permute-start(bf16[24,32,128]{2,1,0:T(8,128)(2,1)} %get-tuple-element.35), channel_id=1, source_target_pairs={{0,6},{2,4},{4,2},{6,0},{8,14},{10,12},{12,10},{14,8},{1,7},{3,5},... | collective-permute-start | bytes 589832 | tf_op jit(solution)/shard_map/ppermute | solution.py:385
  8.5 0.5 collective-permute-start.1
  9.2 1.2 %copy-done = bf16[32,128,128]{2,1,0:T(8,128)(2,1)S(1)} copy-done((bf16[32,128,128]{2,1,0:T(8,128)(2,1)S(1)}, bf16[32,128,128]{2,1,0:T(8,128)(2,1)}, u32[]{:S(2)}) %copy-start) | copy-done | bytes 1048600
  10.4 0.8 %copy-done.2 = bf16[128,256]{1,0:T(8,128)(2,1)S(1)} copy-done((bf16[128,256]{1,0:T(8,128)(2,1)S(1)}, bf16[128,256]{1,0:T(8,128)(2,1)}, u32[]{:S(2)}) %copy-start.2) | copy-done | bytes 65560
  11.2 0.8 %copy-done.3 = bf16[128,256]{1,0:T(8,128)(2,1)S(1)} copy-done((bf16[128,256]{1,0:T(8,128)(2,1)S(1)}, bf16[128,256]{1,0:T(8,128)(2,1)}, u32[]{:S(2)}) %copy-start.3) | copy-done | bytes 65560
  12.1 1.9 %later_edges.1 = (bf16[24,32,128]{2,1,0:T(8,128)(2,1)S(1)}, bf16[40,32,128]{2,1,0:T(8,128)(2,1)S(1)}, bf16[40,32,128]{2,1,0:T(8,128)(2,1)S(1)}, bf16[40,32,128]{2,1,0:T(8,128)(2,1)S(1)}, bf16[40,32,128]{2,1,0:T(8,128)(2,1)S(1)}) custom-call(s32[1]{0:T(128)S(6)} %copy.11.length, bf16[32,128,128]{2,1,0:T(8,128)(2,1)S(1)} %copy-done, ...), custom_call_target="tpu_custom_call" | custom-call | tf_op jit(solution)/shard_map/later_edges/pallas_call | solution.py:423
  14.0 2.9 %collective-permute-start.5 = (bf16[40,32,128]{2,1,0:T(8,128)(2,1)S(1)}, bf16[40,32,128]{2,1,0:T(8,128)(2,1)S(1)}, u32[]{:S(2)}, u32[]{:S(2)}) collective-permute-start(bf16[40,32,128]{2,1,0:T(8,128)(2,1)S(1)} %get-tuple-element.41), channel_id=1, source_target_pairs={{0,6},{2,4},{4,2},{6,0},{8,14},{10,12},{12,10},{14,8},{1,7},{3,5},... | collective-permute-start | bytes 983048 | tf_op jit(solution)/shard_map/ppermute | solution.py:385
  16.9 0.4 collective-permute-start.6
  17.6 1.5 %collective-permute-done.1.c.refs_6_ = bf16[24,32,128]{2,1,0:T(8,128)(2,1)S(1)} collective-permute-done((bf16[24,32,128]{2,1,0:T(8,128)(2,1)}, bf16[24,32,128]{2,1,0:T(8,128)(2,1)S(1)}, u32[]{:S(2)}, u32[]{:S(2)}) %collective-permute-start.1) | collective-permute-done | bytes 196640 | tf_op jit(solution)/shard_map/ppermute | solution.py:385
  19.4 0.5 collective-permute-start.4
  19.9 0.9 %collective-permute-done.3.refs_1_ = bf16[6,128,128]{2,1,0:T(8,128)(2,1)S(1)} collective-permute-done((bf16[6,128,128]{2,1,0:T(8,128)(2,1)S(1)}, bf16[6,128,128]{2,1,0:T(8,128)(2,1)S(1)}, u32[]{:S(2)}, u32[]{:S(2)}) %collective-permute-start.3) | collective-permute-done | bytes 196640 | tf_op jit(solution)/shard_map/ppermute | solution.py:20
  21.5 2.7 %collective-permute-start.14 = (bf16[12,128,128]{2,1,0:T(8,128)(2,1)S(1)}, bf16[12,128,128]{2,1,0:T(8,128)(2,1)S(1)}, u32[]{:S(2)}, u32[]{:S(2)}) collective-permute-start(bf16[12,128,128]{2,1,0:T(8,128)(2,1)S(1)} %get-tuple-element.40.after), channel_id=1, source_target_pairs={{0,8},{2,10},{4,12},{6,14},{8,0},{10,2},{12,4},{14,6},{1,9},{3,11}... | collective-permute-start | bytes 1179656 | tf_op jit(solution)/shard_map/ppermute | solution.py:385
  24.6 1.2 %collective-permute-done.5.b.refs_5_ = bf16[40,32,128]{2,1,0:T(8,128)(2,1)S(1)} collective-permute-done((bf16[40,32,128]{2,1,0:T(8,128)(2,1)S(1)}, bf16[40,32,128]{2,1,0:T(8,128)(2,1)S(1)}, u32[]{:S(2)}, u32[]{:S(2)}) %collective-permute-start.5) | collective-permute-done | bytes 327712 | tf_op jit(solution)/shard_map/ppermute | solution.py:385
  25.8 14.8 %collective-permute-done.6.c.refs_6_ = bf16[40,32,128]{2,1,0:T(8,128)(2,1)S(1)} collective-permute-done((bf16[40,32,128]{2,1,0:T(8,128)(2,1)S(1)}, bf16[40,32,128]{2,1,0:T(8,128)(2,1)S(1)}, u32[]{:S(2)}, u32[]{:S(2)}) %collective-permute-start.6) | collective-permute-done | bytes 327712 | tf_op jit(solution)/shard_map/ppermute | solution.py:385
  40.9 0.5 collective-permute-start.9
  41.3 1.1 %collective-permute-done.8.refs_1_ = bf16[10,128,128]{2,1,0:T(8,128)(2,1)S(1)} collective-permute-done((bf16[10,128,128]{2,1,0:T(8,128)(2,1)S(1)}, bf16[10,128,128]{2,1,0:T(8,128)(2,1)S(1)}, u32[]{:S(2)}, u32[]{:S(2)}) %collective-permute-start.8) | collective-permute-done | bytes 327712 | tf_op jit(solution)/shard_map/ppermute | solution.py:20
  42.4 0.5 collective-permute-done.9.refs_3_
  42.9 0.7 contract.3
  43.7 2.2 %collective-permute-start.11 = (bf16[20,32,128]{2,1,0:T(8,128)(2,1)S(1)}, bf16[20,32,128]{2,1,0:T(8,128)(2,1)S(1)}, u32[]{:S(2)}, u32[]{:S(2)}) collective-permute-start(bf16[20,32,128]{2,1,0:T(8,128)(2,1)S(1)} %get-tuple-element.47), channel_id=1, source_target_pairs={{0,10},{2,8},{4,14},{6,12},{8,2},{10,0},{12,6},{14,4},{1,11},{3,9}... | collective-permute-start | bytes 491528 | tf_op jit(solution)/shard_map/ppermute | solution.py:385
  45.9 1.3 %add_halves.1 = (bf16[32,32,128]{2,1,0:T(8,128)(2,1)S(1)}, bf16[32,32,128]{2,1,0:T(8,128)(2,1)S(1)}, bf16[32,32,128]{2,1,0:T(8,128)(2,1)S(1)}, bf16[32,32,128]{2,1,0:T(8,128)(2,1)S(1)}) custom-call(f32[12,128,128]{2,1,0:T(8,128)S(1)} %get-tuple-element.50.keep, bf16[12,128,128]{2,1,0:T(8,128)(2,1)S(1)} %collective-permute-done.14.arrived, ...), custom_call_target="tpu_custom_call" | custom-call | tf_op jit(solution)/shard_map/add_halves/pallas_call | solution.py:462
  47.2 2.2 %collective-permute-start.15 = (bf16[32,32,128]{2,1,0:T(8,128)(2,1)S(1)}, bf16[32,32,128]{2,1,0:T(8,128)(2,1)S(1)}, u32[]{:S(2)}, u32[]{:S(2)}) collective-permute-start(bf16[32,32,128]{2,1,0:T(8,128)(2,1)S(1)} %get-tuple-element.56), channel_id=1, source_target_pairs={{0,2},{2,0},{4,6},{6,4},{8,10},{10,8},{12,14},{14,12},{1,3},{3,1},... | collective-permute-start | bytes 786440 | tf_op jit(solution)/shard_map/ppermute | solution.py:385
  49.4 1.5 %collective-permute-start.17 = (bf16[32,32,128]{2,1,0:T(8,128)(2,1)S(1)}, bf16[32,32,128]{2,1,0:T(8,128)(2,1)S(1)}, u32[]{:S(2)}, u32[]{:S(2)}) collective-permute-start(bf16[32,32,128]{2,1,0:T(8,128)(2,1)S(1)} %get-tuple-element.58), channel_id=1, source_target_pairs={{0,6},{2,4},{4,2},{6,0},{8,14},{10,12},{12,10},{14,8},{1,7},{3,5},... | collective-permute-start | bytes 786440 | tf_op jit(solution)/shard_map/ppermute | solution.py:385
  51.0 6.3 %collective-permute-done.10.refs_0_ = bf16[20,32,128]{2,1,0:T(8,128)(2,1)S(1)} collective-permute-done((bf16[20,32,128]{2,1,0:T(8,128)(2,1)S(1)}, bf16[20,32,128]{2,1,0:T(8,128)(2,1)S(1)}, u32[]{:S(2)}, u32[]{:S(2)}) %collective-permute-start.10) | collective-permute-done | bytes 163872 | tf_op jit(solution)/shard_map/ppermute | solution.py:385
  57.3 1.9 %collective-permute-start.12 = (bf16[20,32,128]{2,1,0:T(8,128)(2,1)S(1)}, bf16[20,32,128]{2,1,0:T(8,128)(2,1)S(1)}, u32[]{:S(2)}, u32[]{:S(2)}) collective-permute-start(bf16[20,32,128]{2,1,0:T(8,128)(2,1)S(1)} %get-tuple-element.48), channel_id=1, source_target_pairs={{0,12},{2,14},{4,8},{6,10},{8,4},{10,6},{12,0},{14,2},{1,13},{3,15... | collective-permute-start | bytes 491528 | tf_op jit(solution)/shard_map/ppermute | solution.py:385
  59.2 0.6 collective-permute-done.11.refs_1_
  59.8 3.8 %collective-permute-start.13 = (bf16[20,32,128]{2,1,0:T(8,128)(2,1)S(1)}, bf16[20,32,128]{2,1,0:T(8,128)(2,1)S(1)}, u32[]{:S(2)}, u32[]{:S(2)}) collective-permute-start(bf16[20,32,128]{2,1,0:T(8,128)(2,1)S(1)} %get-tuple-element.49), channel_id=1, source_target_pairs={{0,14},{2,12},{4,10},{6,8},{8,6},{10,4},{12,2},{14,0},{1,15},{3,13... | collective-permute-start | bytes 491528 | tf_op jit(solution)/shard_map/ppermute | solution.py:385
  63.5 5.5 %collective-permute-done.12.refs_2_ = bf16[20,32,128]{2,1,0:T(8,128)(2,1)S(1)} collective-permute-done((bf16[20,32,128]{2,1,0:T(8,128)(2,1)S(1)}, bf16[20,32,128]{2,1,0:T(8,128)(2,1)S(1)}, u32[]{:S(2)}, u32[]{:S(2)}) %collective-permute-start.12) | collective-permute-done | bytes 163872 | tf_op jit(solution)/shard_map/ppermute | solution.py:385
  69.0 2.7 %collective-permute-done.13.refs_3_ = bf16[20,32,128]{2,1,0:T(8,128)(2,1)S(1)} collective-permute-done((bf16[20,32,128]{2,1,0:T(8,128)(2,1)S(1)}, bf16[20,32,128]{2,1,0:T(8,128)(2,1)S(1)}, u32[]{:S(2)}, u32[]{:S(2)}) %collective-permute-start.13) | collective-permute-done | bytes 163872 | tf_op jit(solution)/shard_map/ppermute | solution.py:385
  71.7 0.8 %collective-permute-done.16.refs_6_ = bf16[32,32,128]{2,1,0:T(8,128)(2,1)S(1)} collective-permute-done((bf16[32,32,128]{2,1,0:T(8,128)(2,1)S(1)}, bf16[32,32,128]{2,1,0:T(8,128)(2,1)S(1)}, u32[]{:S(2)}, u32[]{:S(2)}) %collective-permute-start.16) | collective-permute-done | bytes 262176 | tf_op jit(solution)/shard_map/ppermute | solution.py:385
  72.6 3.0 %collective-permute-done.17.refs_7_ = bf16[32,32,128]{2,1,0:T(8,128)(2,1)S(1)} collective-permute-done((bf16[32,32,128]{2,1,0:T(8,128)(2,1)S(1)}, bf16[32,32,128]{2,1,0:T(8,128)(2,1)S(1)}, u32[]{:S(2)}, u32[]{:S(2)}) %collective-permute-start.17) | collective-permute-done | bytes 262176 | tf_op jit(solution)/shard_map/ppermute | solution.py:385
  75.6 2.5 %norm_and_project_out.1 = bf16[32,128,128]{2,1,0:T(8,128)(2,1)} custom-call(bf16[20,32,128]{2,1,0:T(8,128)(2,1)S(1)} %collective-permute-done.10.refs_0_, bf16[20,32,128]{2,1,0:T(8,128)(2,1)S(1)} %collective-permute-done.11.refs_1_, bf16[20,32,128]{2,1,0:T(8,128)(2,1)S(1)} %collective-permute-done.12.refs_2_, ...), custom_call_target="tpu_custom_call" | custom-call | tf_op jit(solution)/shard_map/norm_and_project_out/pallas_call | solution.py:475
  (29 shorter events, 2.1 us)
Async XLA Ops:
  0.7 23.5 %copy-start.4 = (bf16[128,128]{1,0:T(8,128)(2,1)S(1)}, bf16[128,128]{1,0:T(8,128)(2,1)}, u32[]{:S(2)}) copy-start(bf16[128,128]{1,0:T(8,128)(2,1)} %weights.1) | copy-start | bytes 98308
  4.5 12.9 %collective-permute-start = (bf16[24,32,128]{2,1,0:T(8,128)(2,1)}, bf16[24,32,128]{2,1,0:T(8,128)(2,1)S(1)}, u32[]{:S(2)}, u32[]{:S(2)}) collective-permute-start(bf16[24,32,128]{2,1,0:T(8,128)(2,1)} %get-tuple-element.35), channel_id=1, source_target_pairs={{0,6},{2,4},{4,2},{6,0},{8,14},{10,12},{12,10},{14,8},{1,7},{3,5},... | collective-permute-start | bytes 589832 | tf_op jit(solution)/shard_map/ppermute | solution.py:385
  8.5 10.6 %collective-permute-start.1 = (bf16[24,32,128]{2,1,0:T(8,128)(2,1)}, bf16[24,32,128]{2,1,0:T(8,128)(2,1)S(1)}, u32[]{:S(2)}, u32[]{:S(2)}) collective-permute-start(bf16[24,32,128]{2,1,0:T(8,128)(2,1)} %get-tuple-element.36), channel_id=1, source_target_pairs={{0,4},{2,6},{4,0},{6,2},{8,12},{10,14},{12,8},{14,10},{1,5},{3,7},... | collective-permute-start | bytes 589832 | tf_op jit(solution)/shard_map/ppermute | solution.py:385
  9.0 10.1 %collective-permute-start.2 = (bf16[24,32,128]{2,1,0:T(8,128)(2,1)}, bf16[24,32,128]{2,1,0:T(8,128)(2,1)S(1)}, u32[]{:S(2)}, u32[]{:S(2)}) collective-permute-start(bf16[24,32,128]{2,1,0:T(8,128)(2,1)} %get-tuple-element.37), channel_id=1, source_target_pairs={{0,2},{2,0},{4,6},{6,4},{8,10},{10,8},{12,14},{14,12},{1,3},{3,1},... | collective-permute-start | bytes 589832 | tf_op jit(solution)/shard_map/ppermute | solution.py:385
  9.2 1.2 %copy-start = (bf16[32,128,128]{2,1,0:T(8,128)(2,1)S(1)}, bf16[32,128,128]{2,1,0:T(8,128)(2,1)}, u32[]{:S(2)}) copy-start(bf16[32,128,128]{2,1,0:T(8,128)(2,1)} %get-tuple-element.32.normed) | copy-start | bytes 3145732
  10.4 0.8 %copy-start.2 = (bf16[128,256]{1,0:T(8,128)(2,1)S(1)}, bf16[128,256]{1,0:T(8,128)(2,1)}, u32[]{:S(2)}) copy-start(bf16[128,256]{1,0:T(8,128)(2,1)} %proj.3) | copy-start | bytes 196612
  11.2 0.8 %copy-start.3 = (bf16[128,256]{1,0:T(8,128)(2,1)S(1)}, bf16[128,256]{1,0:T(8,128)(2,1)}, u32[]{:S(2)}) copy-start(bf16[128,256]{1,0:T(8,128)(2,1)} %gate.3) | copy-start | bytes 196612
  12.1 12.1 %copy-start.1 = (bf16[32,128,128]{2,1,0:T(8,128)(2,1)S(1)}, bf16[32,128,128]{2,1,0:T(8,128)(2,1)}, u32[]{:S(2)}) copy-start(bf16[32,128,128]{2,1,0:T(8,128)(2,1)} %get-tuple-element.32.normed) | copy-start | bytes 3145732
  14.0 11.8 %collective-permute-start.5 = (bf16[40,32,128]{2,1,0:T(8,128)(2,1)S(1)}, bf16[40,32,128]{2,1,0:T(8,128)(2,1)S(1)}, u32[]{:S(2)}, u32[]{:S(2)}) collective-permute-start(bf16[40,32,128]{2,1,0:T(8,128)(2,1)S(1)} %get-tuple-element.41), channel_id=1, source_target_pairs={{0,6},{2,4},{4,2},{6,0},{8,14},{10,12},{12,10},{14,8},{1,7},{3,5},... | collective-permute-start | bytes 983048 | tf_op jit(solution)/shard_map/ppermute | solution.py:385
  16.9 23.7 %collective-permute-start.6 = (bf16[40,32,128]{2,1,0:T(8,128)(2,1)S(1)}, bf16[40,32,128]{2,1,0:T(8,128)(2,1)S(1)}, u32[]{:S(2)}, u32[]{:S(2)}) collective-permute-start(bf16[40,32,128]{2,1,0:T(8,128)(2,1)S(1)} %get-tuple-element.42), channel_id=1, source_target_pairs={{0,4},{2,6},{4,0},{6,2},{8,12},{10,14},{12,8},{14,10},{1,5},{3,7},... | collective-permute-start | bytes 983048 | tf_op jit(solution)/shard_map/ppermute | solution.py:385
  17.4 23.2 %collective-permute-start.7 = (bf16[40,32,128]{2,1,0:T(8,128)(2,1)S(1)}, bf16[40,32,128]{2,1,0:T(8,128)(2,1)S(1)}, u32[]{:S(2)}, u32[]{:S(2)}) collective-permute-start(bf16[40,32,128]{2,1,0:T(8,128)(2,1)S(1)} %get-tuple-element.43), channel_id=1, source_target_pairs={{0,2},{2,0},{4,6},{6,4},{8,10},{10,8},{12,14},{14,12},{1,3},{3,1},... | collective-permute-start | bytes 983048 | tf_op jit(solution)/shard_map/ppermute | solution.py:385
  19.3 1.5 %collective-permute-start.3 = (bf16[6,128,128]{2,1,0:T(8,128)(2,1)S(1)}, bf16[6,128,128]{2,1,0:T(8,128)(2,1)S(1)}, u32[]{:S(2)}, u32[]{:S(2)}) collective-permute-start(bf16[6,128,128]{2,1,0:T(8,128)(2,1)S(1)} %get-tuple-element.38.refs_0_), channel_id=1, source_target_pairs={{0,1},{1,0},{2,3},{3,2},{4,5},{5,4},{6,7},{7,6},{8,9},{9,8},{10,11... | collective-permute-start | bytes 589832 | tf_op jit(solution)/shard_map/ppermute | solution.py:20
  19.4 1.7 %collective-permute-start.4 = (bf16[6,128,128]{2,1,0:T(8,128)(2,1)S(1)}, bf16[6,128,128]{2,1,0:T(8,128)(2,1)S(1)}, u32[]{:S(2)}, u32[]{:S(2)}) collective-permute-start(bf16[6,128,128]{2,1,0:T(8,128)(2,1)S(1)} %get-tuple-element.39.refs_2_), channel_id=1, source_target_pairs={{0,1},{1,0},{2,3},{3,2},{4,5},{5,4},{6,7},{7,6},{8,9},{9,8},{10,11... | collective-permute-start | bytes 589832 | tf_op jit(solution)/shard_map/ppermute | solution.py:20
  21.5 24.4 %collective-permute-start.14 = (bf16[12,128,128]{2,1,0:T(8,128)(2,1)S(1)}, bf16[12,128,128]{2,1,0:T(8,128)(2,1)S(1)}, u32[]{:S(2)}, u32[]{:S(2)}) collective-permute-start(bf16[12,128,128]{2,1,0:T(8,128)(2,1)S(1)} %get-tuple-element.40.after), channel_id=1, source_target_pairs={{0,8},{2,10},{4,12},{6,14},{8,0},{10,2},{12,4},{14,6},{1,9},{3,11}... | collective-permute-start | bytes 1179656 | tf_op jit(solution)/shard_map/ppermute | solution.py:385
  40.7 1.7 %collective-permute-start.8 = (bf16[10,128,128]{2,1,0:T(8,128)(2,1)S(1)}, bf16[10,128,128]{2,1,0:T(8,128)(2,1)S(1)}, u32[]{:S(2)}, u32[]{:S(2)}) collective-permute-start(bf16[10,128,128]{2,1,0:T(8,128)(2,1)S(1)} %get-tuple-element.44.refs_0_), channel_id=1, source_target_pairs={{0,1},{1,0},{2,3},{3,2},{4,5},{5,4},{6,7},{7,6},{8,9},{9,8},{10,11... | collective-permute-start | bytes 983048 | tf_op jit(solution)/shard_map/ppermute | solution.py:20
  40.8 34.8 %copy-start.5 = (bf16[128,128]{1,0:T(8,128)(2,1)S(1)}, bf16[128,128]{1,0:T(8,128)(2,1)}, u32[]{:S(2)}) copy-start(bf16[128,128]{1,0:T(8,128)(2,1)} %refs_11_.1) | copy-start | bytes 98308
  40.8 34.8 %copy-start.6 = (f32[128]{0:T(128)S(1)}, f32[128]{0:T(128)}, u32[]{:S(2)}) copy-start(f32[128]{0:T(128)} %param.17) | copy-start | bytes 1540
  40.9 34.7 %copy-start.7 = (f32[128]{0:T(128)S(1)}, f32[128]{0:T(128)}, u32[]{:S(2)}) copy-start(f32[128]{0:T(128)} %param.18) | copy-start | bytes 1540
  40.9 2.0 %collective-permute-start.9 = (bf16[10,128,128]{2,1,0:T(8,128)(2,1)S(1)}, bf16[10,128,128]{2,1,0:T(8,128)(2,1)S(1)}, u32[]{:S(2)}, u32[]{:S(2)}) collective-permute-start(bf16[10,128,128]{2,1,0:T(8,128)(2,1)S(1)} %get-tuple-element.45.refs_2_), channel_id=1, source_target_pairs={{0,1},{1,0},{2,3},{3,2},{4,5},{5,4},{6,7},{7,6},{8,9},{9,8},{10,11... | collective-permute-start | bytes 983048 | tf_op jit(solution)/shard_map/ppermute | solution.py:20
  43.6 13.7 %collective-permute-start.10 = (bf16[20,32,128]{2,1,0:T(8,128)(2,1)S(1)}, bf16[20,32,128]{2,1,0:T(8,128)(2,1)S(1)}, u32[]{:S(2)}, u32[]{:S(2)}) collective-permute-start(bf16[20,32,128]{2,1,0:T(8,128)(2,1)S(1)} %get-tuple-element.46), channel_id=1, source_target_pairs={{0,8},{2,10},{4,12},{6,14},{8,0},{10,2},{12,4},{14,6},{1,9},{3,11}... | collective-permute-start | bytes 491528 | tf_op jit(solution)/shard_map/ppermute | solution.py:385
  43.7 16.1 %collective-permute-start.11 = (bf16[20,32,128]{2,1,0:T(8,128)(2,1)S(1)}, bf16[20,32,128]{2,1,0:T(8,128)(2,1)S(1)}, u32[]{:S(2)}, u32[]{:S(2)}) collective-permute-start(bf16[20,32,128]{2,1,0:T(8,128)(2,1)S(1)} %get-tuple-element.47), channel_id=1, source_target_pairs={{0,10},{2,8},{4,14},{6,12},{8,2},{10,0},{12,6},{14,4},{1,11},{3,9}... | collective-permute-start | bytes 491528 | tf_op jit(solution)/shard_map/ppermute | solution.py:385
  47.2 24.5 %collective-permute-start.15 = (bf16[32,32,128]{2,1,0:T(8,128)(2,1)S(1)}, bf16[32,32,128]{2,1,0:T(8,128)(2,1)S(1)}, u32[]{:S(2)}, u32[]{:S(2)}) collective-permute-start(bf16[32,32,128]{2,1,0:T(8,128)(2,1)S(1)} %get-tuple-element.56), channel_id=1, source_target_pairs={{0,2},{2,0},{4,6},{6,4},{8,10},{10,8},{12,14},{14,12},{1,3},{3,1},... | collective-permute-start | bytes 786440 | tf_op jit(solution)/shard_map/ppermute | solution.py:385
  49.4 23.1 %collective-permute-start.16 = (bf16[32,32,128]{2,1,0:T(8,128)(2,1)S(1)}, bf16[32,32,128]{2,1,0:T(8,128)(2,1)S(1)}, u32[]{:S(2)}, u32[]{:S(2)}) collective-permute-start(bf16[32,32,128]{2,1,0:T(8,128)(2,1)S(1)} %get-tuple-element.57), channel_id=1, source_target_pairs={{0,4},{2,6},{4,0},{6,2},{8,12},{10,14},{12,8},{14,10},{1,5},{3,7},... | collective-permute-start | bytes 786440 | tf_op jit(solution)/shard_map/ppermute | solution.py:385
  49.4 26.2 %collective-permute-start.17 = (bf16[32,32,128]{2,1,0:T(8,128)(2,1)S(1)}, bf16[32,32,128]{2,1,0:T(8,128)(2,1)S(1)}, u32[]{:S(2)}, u32[]{:S(2)}) collective-permute-start(bf16[32,32,128]{2,1,0:T(8,128)(2,1)S(1)} %get-tuple-element.58), channel_id=1, source_target_pairs={{0,6},{2,4},{4,2},{6,0},{8,14},{10,12},{12,10},{14,8},{1,7},{3,5},... | collective-permute-start | bytes 786440 | tf_op jit(solution)/shard_map/ppermute | solution.py:385
  57.3 11.8 %collective-permute-start.12 = (bf16[20,32,128]{2,1,0:T(8,128)(2,1)S(1)}, bf16[20,32,128]{2,1,0:T(8,128)(2,1)S(1)}, u32[]{:S(2)}, u32[]{:S(2)}) collective-permute-start(bf16[20,32,128]{2,1,0:T(8,128)(2,1)S(1)} %get-tuple-element.48), channel_id=1, source_target_pairs={{0,12},{2,14},{4,8},{6,10},{8,4},{10,6},{12,0},{14,2},{1,13},{3,15... | collective-permute-start | bytes 491528 | tf_op jit(solution)/shard_map/ppermute | solution.py:385
  59.8 12.0 %collective-permute-start.13 = (bf16[20,32,128]{2,1,0:T(8,128)(2,1)S(1)}, bf16[20,32,128]{2,1,0:T(8,128)(2,1)S(1)}, u32[]{:S(2)}, u32[]{:S(2)}) collective-permute-start(bf16[20,32,128]{2,1,0:T(8,128)(2,1)S(1)} %get-tuple-element.49), channel_id=1, source_target_pairs={{0,14},{2,12},{4,10},{6,8},{8,6},{10,4},{12,2},{14,0},{1,15},{3,13... | collective-permute-start | bytes 491528 | tf_op jit(solution)/shard_map/ppermute | solution.py:385

commit v4 on v3

--- a/solution.py
+++ b/solution.py
@@ -8,8 +8,7 @@
 from jax.sharding import PartitionSpec as P
 
 epsilon = 1e-05
-chunk_sizes = (12, 20)
-swap_pieces = ((6, 6), (10, 10))
+chunk_sizes = (13, 19)
 vmem_all = 60 * 1024 * 1024
 vmem_part = 28 * 1024 * 1024
 
@@ -228,31 +227,29 @@
         out[at : at + rows] = jax.nn.sigmoid(gating).reshape(rows, tile_cols, channels)
 
 
-def pack_kernel(after, a, b, c, d, *rest):
-    outs, sems = rest[:-1], rest[-1]
-    copies, start = [], 0
-    for piece, out in enumerate(outs):
-        size, count, _ = out.shape
-        part = count // 4
-        for at, ref in enumerate((a, b, c, d)):
-            rows = out.at[:, pl.ds(at * part, part), :]
-            copies.append(load(ref.at[pl.ds(start, size)], rows, sems.at[piece, at]))
-        start += size
+def pack_kernel(after, a, b, out, sems):
+    size, count, _ = out.shape
+    part = count // 2
+    copies = [
+        load(ref.at[pl.ds(0, size)], out.at[:, pl.ds(at * part, part), :], sems.at[at])
+        for at, ref in enumerate((a, b))
+    ]
     for copy in copies:
         copy.wait()
 
 
-def contractions(lefts, parts, store):
+def contractions(partners, parts, store):
     size = parts[0].shape[0] // 2
-    places = [(at, u) for at in range(0, len(lefts), 2) for u in range(lefts[at].shape[0])]
     low = lax.axis_index("row") < 4
     own_away = (lax.axis_index("col") == 1) == low
 
     def both(first):
         for u in range(size):
             right = jnp.concatenate([part[size + u] for part in parts], axis=0)
+            own = jnp.concatenate([part[u] for part in parts], axis=0)
+            theirs = jnp.concatenate([partner[u] for partner in partners], axis=0)
             for side in range(2):
-                left = lefts[places[u][0] + (first ^ side)][places[u][1]]
+                left = theirs if first ^ side else own
                 product = lax.dot_general(
                     left, right, matmul_tn, preferred_element_type=jnp.float32
                 )
@@ -262,20 +259,18 @@
     pl.when(jnp.logical_not(own_away))(functools.partial(both, 1))
 
 
-def contract_kernel(count, *refs):
-    lefts, parts = refs[:count], refs[count : count + 4]
-    outs = refs[count + 4 :]
+def contract_kernel(*refs):
+    partners, parts, outs = refs[:2], refs[2:6], refs[6:]
 
     def store(u, side, product):
         outs[side][u] = product.astype(outs[side].dtype)
 
-    contractions(lefts, parts, store)
-
-
-def last_contract_kernel(count, *refs):
-    lefts, parts = refs[:count], refs[count : count + 4]
-    outs = refs[count + 4 : count + 8], refs[count + 8 : count + 12]
-    held = refs[count + 12]
+    contractions(partners, parts, store)
+
+
+def last_contract_kernel(*refs):
+    partners, parts = refs[:2], refs[2:6]
+    outs, held = (refs[6:10], refs[10:14]), refs[14]
     part = outs[0][0].shape[1]
     row = lax.axis_index("row")
 
@@ -285,31 +280,18 @@
             rows = pl.ds(pl.multiple_of(((row % 4) ^ slot) * part, part), part)
             out[u] = held[u, side, rows, :]
 
-    contractions(lefts, parts, store)
+    contractions(partners, parts, store)
 
 
 def add_kernel(keep, arrived, *refs):
-    lasts, outs = refs[:4], refs[4:8]
-    keep_held, arrived_held, sems = refs[8:]
+    lasts, outs, held = refs[:4], refs[4:8], refs[8]
     size, part = keep.shape[0], outs[0].shape[1]
     row = lax.axis_index("row")
-    loads = [load(keep, keep_held, sems.at[0]), load(arrived, arrived_held, sems.at[1])]
-    stores = [
-        load(last, out.at[pl.ds(size, last.shape[0])], sems.at[2 + at])
-        for at, (last, out) in enumerate(zip(lasts, outs, strict=True))
-    ]
-    for copy in loads:
-        copy.wait()
-    for u in range(size):
-        total = keep_held[u] + arrived_held[u].astype(jnp.float32)
-        arrived_held[u] = total.astype(jnp.bfloat16)
-    for slot, out in enumerate(outs):
+    held[...] = (keep[...] + arrived[...].astype(jnp.float32)).astype(jnp.bfloat16)
+    for slot, (last, out) in enumerate(zip(lasts, outs, strict=True)):
         rows = pl.ds(pl.multiple_of(((row % 4) ^ slot) * part, part), part)
-        stores.append(
-            load(arrived_held.at[:, rows, :], out.at[pl.ds(0, size)], sems.at[6 + slot])
-        )
-    for copy in stores:
-        copy.wait()
+        out[:size] = held[:, rows, :]
+        out[size:] = last[...]
 
 
 def finish_kernel(rows, sizes, *refs):
@@ -321,7 +303,7 @@
     row = lax.axis_index("row")
     at = lax.broadcasted_iota(jnp.int32, (hidden, hidden), 0)
     slot, place = at // per, at % per
-    owner = (row % 4) ^ slot
+    owner = (row % 4) ^ ((4 - slot) % 4)
     channel = jnp.where(
         place < early, owner * early + place, 4 * early + owner * late + place - early
     )
@@ -387,20 +369,19 @@
     def edge_shape(size):
         return (2 * size, tile_rows, tile_cols)
 
-    def received(pieces):
+    def spread(pieces):
         return [pieces[0], *[exchanged(pieces[mask], mask) for mask in (3, 2, 1)]]
 
-    def swapped_left(at, after, pieces):
-        sizes = swap_pieces[at]
-        lefts = call(
+    def swapped_left(after, a, b):
+        (left,) = call(
             pack_kernel,
-            [array((size, depth, tile_cols)) for size in sizes],
-            [semaphores((len(sizes), 4))],
-            [in_any] * 5,
-            [in_any] * len(sizes),
+            [array((a.shape[0] // 2, depth // 2, tile_cols))],
+            [semaphores((2,))],
+            [in_any] * 3,
+            [in_any],
             "pack_left",
-        )(after, *pieces)
-        return [side for left in lefts for side in (left, from_partner(left, "col", 0))]
+        )(after, a, b)
+        return from_partner(left, "col", 0)
 
     normed, *sent = call(
         functools.partial(first_kernel, (0, early, block)),
@@ -428,19 +409,20 @@
         [in_vmem] * 5,
         "later_edges",
     )(length, normed, proj_in, gate_in)
-    first = received([own, *sent])
-    lefts = swapped_left(0, second[0], first)
+    first = spread([own, *sent])
+    partners = [swapped_left(second[0], first[0], first[3]), swapped_left(second[0], first[1], first[2])]
+    parts = [first[0], first[3], first[1], first[2]]
     shape = (early, depth, tile_cols)
     away, keep = call(
-        functools.partial(contract_kernel, len(lefts)),
+        contract_kernel,
         [array(shape), array(shape, jnp.float32)],
         [],
-        [in_vmem] * (len(lefts) + 4),
+        [in_vmem] * 6,
         [in_vmem] * 2,
         "contract",
-    )(*lefts, *first)
+    )(*partners, *parts)
     arrived = exchanged(away, 4)
-    second = received(second)
+    second = spread(second)
     (opened,) = call(
         functools.partial(gate_kernel, block),
         [array(pair.shape, jnp.float32)],
@@ -449,29 +431,26 @@
         [in_vmem],
         "output_gate",
     )(away, normed, gate_out)
-    lefts = swapped_left(1, opened, second)
+    partners = [swapped_left(opened, second[0], second[3]), swapped_left(opened, second[1], second[2])]
+    parts = [second[0], second[3], second[1], second[2]]
     last = call(
-        functools.partial(last_contract_kernel, len(lefts)),
+        last_contract_kernel,
         [array((late, tile_rows, tile_cols))] * 8,
         [vmem((late, 2, depth, tile_cols), small)],
-        [in_vmem] * (len(lefts) + 4),
+        [in_vmem] * 6,
         [in_vmem] * 8,
         "contract",
-    )(*lefts, *second)
-    aways = [exchanged(last[mask], 4 ^ mask) for mask in range(4)]
+    )(*partners, *parts)
+    aways = [exchanged(last[mask], 4 ^ mask) for mask in (0, 3, 2, 1)]
     totals = call(
         add_kernel,
         [array((early + late, tile_rows, tile_cols))] * 4,
-        [
-            vmem((early, depth, tile_cols), jnp.float32),
-            vmem((early, depth, tile_cols), small),
-            semaphores((10,)),
-        ],
-        [in_any] * 6,
-        [in_any] * 4,
+        [vmem(shape, small)],
+        [in_vmem] * 6,
+        [in_vmem] * 4,
         "add_halves",
     )(keep, arrived, *last[4:])
-    totals = [totals[0], *[exchanged(totals[mask], mask) for mask in (1, 2, 3)]]
+    totals = spread(totals)
     (update,) = call(
         functools.partial(finish_kernel, 8, chunk_sizes),
         [array(pair.shape)],

time: 78.4 us -> 75.9 us (0.968)
  the two profiles are of different devices: /device:TPU:0 before, /device:TPU:4 now
where the time goes in v4:
time: 75.9 us; the launch traced here: 75.7 us
  starting transfers between devices  30.8 us (41%)
  waiting for transfers between devices  30.6 us (40%)
  Pallas kernels  10.4 us (14%)
  local copies, waits for them, and re-layouts  2.93 us (4%)
  between operations  0.85 us (1%)
    ppermute x14, starting transfers between devices, exchanged(): lax.ppermute(value, 'row', [(source, source ^ mask) for source in range(r...  30.6 us
    ppermute x14, waiting for transfers between devices, exchanged(): lax.ppermute(value, 'row', [(source, source ^ mask) for source in range(r...  27.6 us
    pallas_call x1, Pallas kernels, shards_by_halves(): call(functools.partial(first_kernel, (0, early, block)), [array(pair.shap...  3.99 us
    ppermute x4, waiting for transfers between devices, from_partner(): return lax.ppermute(value, axis, pairs)  3.03 us
    unnamed x16, local copies, waits for them, and re-layouts  2.93 us
    pallas_call x1, Pallas kernels, shards_by_halves(): call(functools.partial(finish_kernel, 8, chunk_sizes), [array(pair.shape)...  2.55 us
    pallas_call x1, Pallas kernels, shards_by_halves(): call(functools.partial(later_kernel, (block, (0, early, (0, 1)), (4 * ear...  1.95 us
  transfers between devices with their start and end apart: 18, of which 10 were waited for; matrix products, arithmetic and copies ran while one was open for 0% of the time, Pallas kernels for 5%

profile of v4, /device:TPU:4, one launch (start us, length us, event | category | flops | bytes accessed | tf_op | source)
XLA Modules:
  0.0 75.7 jit_solution(8581992577660508836)
XLA Ops:
  0.7 4.0 %norm_and_first_edges.1 = (bf16[32,128,128]{2,1,0:T(8,128)(2,1)}, bf16[26,32,128]{2,1,0:T(8,128)(2,1)}, bf16[26,32,128]{2,1,0:T(8,128)(2,1)}, bf16[26,32,128]{2,1,0:T(8,128)(2,1)}) custom-call(s32[1]{0:T(128)S(6)} %copy.11.length, bf16[32,128,128]{2,1,0:T(8,128)(2,1)} %pair.1, f32[1,128]{1,0:T(1,128)} %bitcast.6, f32[1,128]{1,0:T(1,128)} %bitcast.7, ...), custom_call_target="tpu_custom_call" | custom-call | tf_op jit(solution)/shard_map/norm_and_first_edges/pallas_call | solution.py:386
  4.6 1.6 %collective-permute-start.2 = (bf16[26,32,128]{2,1,0:T(8,128)(2,1)}, bf16[26,32,128]{2,1,0:T(8,128)(2,1)S(1)}, u32[]{:S(2)}, u32[]{:S(2)}) collective-permute-start(bf16[26,32,128]{2,1,0:T(8,128)(2,1)} %get-tuple-element.32), channel_id=1, source_target_pairs={{0,6},{2,4},{4,2},{6,0},{8,14},{10,12},{12,10},{14,8},{1,7},{3,5},... | collective-permute-start | bytes 638984 | tf_op jit(solution)/shard_map/ppermute | solution.py:367
  6.2 0.1 collective-permute-start.3
  6.4 1.8 %collective-permute-start = (bf16[26,32,128]{2,1,0:T(8,128)(2,1)}, bf16[26,32,128]{2,1,0:T(8,128)(2,1)S(1)}, u32[]{:S(2)}, u32[]{:S(2)}) collective-permute-start(bf16[26,32,128]{2,1,0:T(8,128)(2,1)} %get-tuple-element.31), channel_id=1, source_target_pairs={{0,2},{2,0},{4,6},{6,4},{8,10},{10,8},{12,14},{14,12},{1,3},{3,1},... | collective-permute-start | bytes 638984 | tf_op jit(solution)/shard_map/ppermute | solution.py:367
  8.2 1.2 %copy-done = bf16[32,128,128]{2,1,0:T(8,128)(2,1)S(1)} copy-done((bf16[32,128,128]{2,1,0:T(8,128)(2,1)S(1)}, bf16[32,128,128]{2,1,0:T(8,128)(2,1)}, u32[]{:S(2)}) %copy-start) | copy-done | bytes 1048600
  9.4 0.8 %copy-done.2 = bf16[128,256]{1,0:T(8,128)(2,1)S(1)} copy-done((bf16[128,256]{1,0:T(8,128)(2,1)S(1)}, bf16[128,256]{1,0:T(8,128)(2,1)}, u32[]{:S(2)}) %copy-start.2) | copy-done | bytes 65560
  10.3 0.8 %copy-done.3 = bf16[128,256]{1,0:T(8,128)(2,1)S(1)} copy-done((bf16[128,256]{1,0:T(8,128)(2,1)S(1)}, bf16[128,256]{1,0:T(8,128)(2,1)}, u32[]{:S(2)}) %copy-start.3) | copy-done | bytes 65560
  11.1 2.0 %later_edges.1 = (bf16[26,32,128]{2,1,0:T(8,128)(2,1)S(1)}, bf16[38,32,128]{2,1,0:T(8,128)(2,1)S(1)}, bf16[38,32,128]{2,1,0:T(8,128)(2,1)S(1)}, bf16[38,32,128]{2,1,0:T(8,128)(2,1)S(1)}, bf16[38,32,128]{2,1,0:T(8,128)(2,1)S(1)}) custom-call(s32[1]{0:T(128)S(6)} %copy.11.length, bf16[32,128,128]{2,1,0:T(8,128)(2,1)S(1)} %copy-done, ...), custom_call_target="tpu_custom_call" | custom-call | tf_op jit(solution)/shard_map/later_edges/pallas_call | solution.py:404
  13.1 0.3 collective-permute-start.5
  13.3 2.9 %collective-permute-start.7 = (bf16[38,32,128]{2,1,0:T(8,128)(2,1)S(1)}, bf16[38,32,128]{2,1,0:T(8,128)(2,1)S(1)}, u32[]{:S(2)}, u32[]{:S(2)}) collective-permute-start(bf16[38,32,128]{2,1,0:T(8,128)(2,1)S(1)} %get-tuple-element.36), channel_id=1, source_target_pairs={{0,6},{2,4},{4,2},{6,0},{8,14},{10,12},{12,10},{14,8},{1,7},{3,5},... | collective-permute-start | bytes 933896 | tf_op jit(solution)/shard_map/ppermute | solution.py:367
  16.2 0.4 collective-permute-start.8
  16.9 1.8 %collective-permute-done.b.refs_3_ = bf16[26,32,128]{2,1,0:T(8,128)(2,1)S(1)} collective-permute-done((bf16[26,32,128]{2,1,0:T(8,128)(2,1)}, bf16[26,32,128]{2,1,0:T(8,128)(2,1)S(1)}, u32[]{:S(2)}, u32[]{:S(2)}) %collective-permute-start) | collective-permute-done | bytes 213024 | tf_op jit(solution)/shard_map/ppermute | solution.py:367
  18.8 1.4 %collective-permute-done.1.refs_0_ = bf16[13,64,128]{2,1,0:T(8,128)(2,1)S(1)} collective-permute-done((bf16[13,64,128]{2,1,0:T(8,128)(2,1)S(1)}, bf16[13,64,128]{2,1,0:T(8,128)(2,1)S(1)}, u32[]{:S(2)}, u32[]{:S(2)}) %collective-permute-start.1) | collective-permute-done | bytes 213024 | tf_op jit(solution)/shard_map/ppermute | solution.py:19
  20.2 0.4 contract.2
  20.6 2.7 %collective-permute-start.14 = (bf16[13,128,128]{2,1,0:T(8,128)(2,1)S(1)}, bf16[13,128,128]{2,1,0:T(8,128)(2,1)S(1)}, u32[]{:S(2)}, u32[]{:S(2)}) collective-permute-start(bf16[13,128,128]{2,1,0:T(8,128)(2,1)S(1)} %get-tuple-element.34.after), channel_id=1, source_target_pairs={{0,8},{2,10},{4,12},{6,14},{8,0},{10,2},{12,4},{14,6},{1,9},{3,11}... | collective-permute-start | bytes 1277960 | tf_op jit(solution)/shard_map/ppermute | solution.py:367
  23.3 0.4 output_gate.1.after.refs_8_
  23.7 6.8 %collective-permute-done.5.b.refs_3_ = bf16[38,32,128]{2,1,0:T(8,128)(2,1)S(1)} collective-permute-done((bf16[38,32,128]{2,1,0:T(8,128)(2,1)S(1)}, bf16[38,32,128]{2,1,0:T(8,128)(2,1)S(1)}, u32[]{:S(2)}, u32[]{:S(2)}) %collective-permute-start.5) | collective-permute-done | bytes 311328 | tf_op jit(solution)/shard_map/ppermute | solution.py:367
  30.7 2.0 %collective-permute-done.7.a.refs_4_ = bf16[38,32,128]{2,1,0:T(8,128)(2,1)S(1)} collective-permute-done((bf16[38,32,128]{2,1,0:T(8,128)(2,1)S(1)}, bf16[38,32,128]{2,1,0:T(8,128)(2,1)S(1)}, u32[]{:S(2)}, u32[]{:S(2)}) %collective-permute-start.7) | collective-permute-done | bytes 311328 | tf_op jit(solution)/shard_map/ppermute | solution.py:367
  32.6 4.7 %collective-permute-done.8.b.refs_5_ = bf16[38,32,128]{2,1,0:T(8,128)(2,1)S(1)} collective-permute-done((bf16[38,32,128]{2,1,0:T(8,128)(2,1)S(1)}, bf16[38,32,128]{2,1,0:T(8,128)(2,1)S(1)}, u32[]{:S(2)}, u32[]{:S(2)}) %collective-permute-start.8) | collective-permute-done | bytes 311328 | tf_op jit(solution)/shard_map/ppermute | solution.py:367
  37.5 1.6 %collective-permute-done.9.refs_1_ = bf16[19,64,128]{2,1,0:T(8,128)(2,1)S(1)} collective-permute-done((bf16[19,64,128]{2,1,0:T(8,128)(2,1)S(1)}, bf16[19,64,128]{2,1,0:T(8,128)(2,1)S(1)}, u32[]{:S(2)}, u32[]{:S(2)}) %collective-permute-start.9) | collective-permute-done | bytes 311328 | tf_op jit(solution)/shard_map/ppermute | solution.py:19
  39.1 0.7 contract.3
  39.9 3.5 %collective-permute-start.11 = (bf16[19,32,128]{2,1,0:T(8,128)(2,1)S(1)}, bf16[19,32,128]{2,1,0:T(8,128)(2,1)S(1)}, u32[]{:S(2)}, u32[]{:S(2)}) collective-permute-start(bf16[19,32,128]{2,1,0:T(8,128)(2,1)S(1)} %get-tuple-element.39), channel_id=1, source_target_pairs={{0,14},{2,12},{4,10},{6,8},{8,6},{10,4},{12,2},{14,0},{1,15},{3,13... | collective-permute-start | bytes 466952 | tf_op jit(solution)/shard_map/ppermute | solution.py:367
  43.4 2.6 %collective-permute-done.14.arrived = bf16[13,128,128]{2,1,0:T(8,128)(2,1)S(1)} collective-permute-done((bf16[13,128,128]{2,1,0:T(8,128)(2,1)S(1)}, bf16[13,128,128]{2,1,0:T(8,128)(2,1)S(1)}, u32[]{:S(2)}, u32[]{:S(2)}) %collective-permute-start.14) | collective-permute-done | bytes 426016 | tf_op jit(solution)/shard_map/ppermute | solution.py:367
  46.0 0.2 add_halves.1
  46.2 4.8 %collective-permute-start.15 = (bf16[32,32,128]{2,1,0:T(8,128)(2,1)S(1)}, bf16[32,32,128]{2,1,0:T(8,128)(2,1)S(1)}, u32[]{:S(2)}, u32[]{:S(2)}) collective-permute-start(bf16[32,32,128]{2,1,0:T(8,128)(2,1)S(1)} %get-tuple-element.48), channel_id=1, source_target_pairs={{0,6},{2,4},{4,2},{6,0},{8,14},{10,12},{12,10},{14,8},{1,7},{3,5},... | collective-permute-start | bytes 786440 | tf_op jit(solution)/shard_map/ppermute | solution.py:367
  51.0 0.3 collective-permute-start.16
  51.3 1.4 %collective-permute-start.17 = (bf16[32,32,128]{2,1,0:T(8,128)(2,1)S(1)}, bf16[32,32,128]{2,1,0:T(8,128)(2,1)S(1)}, u32[]{:S(2)}, u32[]{:S(2)}) collective-permute-start(bf16[32,32,128]{2,1,0:T(8,128)(2,1)S(1)} %get-tuple-element.50), channel_id=1, source_target_pairs={{0,2},{2,0},{4,6},{6,4},{8,10},{10,8},{12,14},{14,12},{1,3},{3,1},... | collective-permute-start | bytes 786440 | tf_op jit(solution)/shard_map/ppermute | solution.py:367
  52.7 4.9 %collective-permute-start.12 = (bf16[19,32,128]{2,1,0:T(8,128)(2,1)S(1)}, bf16[19,32,128]{2,1,0:T(8,128)(2,1)S(1)}, u32[]{:S(2)}, u32[]{:S(2)}) collective-permute-start(bf16[19,32,128]{2,1,0:T(8,128)(2,1)S(1)} %get-tuple-element.40), channel_id=1, source_target_pairs={{0,12},{2,14},{4,8},{6,10},{8,4},{10,6},{12,0},{14,2},{1,13},{3,15... | collective-permute-start | bytes 466952 | tf_op jit(solution)/shard_map/ppermute | solution.py:367
  57.6 5.9 %collective-permute-start.13 = (bf16[19,32,128]{2,1,0:T(8,128)(2,1)S(1)}, bf16[19,32,128]{2,1,0:T(8,128)(2,1)S(1)}, u32[]{:S(2)}, u32[]{:S(2)}) collective-permute-start(bf16[19,32,128]{2,1,0:T(8,128)(2,1)S(1)} %get-tuple-element.41), channel_id=1, source_target_pairs={{0,10},{2,8},{4,14},{6,12},{8,2},{10,0},{12,6},{14,4},{1,11},{3,9}... | collective-permute-start | bytes 466952 | tf_op jit(solution)/shard_map/ppermute | solution.py:367
  63.5 7.7 %collective-permute-done.12.refs_2_ = bf16[19,32,128]{2,1,0:T(8,128)(2,1)S(1)} collective-permute-done((bf16[19,32,128]{2,1,0:T(8,128)(2,1)S(1)}, bf16[19,32,128]{2,1,0:T(8,128)(2,1)S(1)}, u32[]{:S(2)}, u32[]{:S(2)}) %collective-permute-start.12) | collective-permute-done | bytes 155680 | tf_op jit(solution)/shard_map/ppermute | solution.py:367
  71.2 1.9 %collective-permute-done.13.refs_3_ = bf16[19,32,128]{2,1,0:T(8,128)(2,1)S(1)} collective-permute-done((bf16[19,32,128]{2,1,0:T(8,128)(2,1)S(1)}, bf16[19,32,128]{2,1,0:T(8,128)(2,1)S(1)}, u32[]{:S(2)}, u32[]{:S(2)}) %collective-permute-start.13) | collective-permute-done | bytes 155680 | tf_op jit(solution)/shard_map/ppermute | solution.py:367
  73.1 2.6 %norm_and_project_out.1 = bf16[32,128,128]{2,1,0:T(8,128)(2,1)} custom-call(bf16[19,32,128]{2,1,0:T(8,128)(2,1)S(1)} %collective-permute-done.10.refs_0_, bf16[19,32,128]{2,1,0:T(8,128)(2,1)S(1)} %collective-permute-done.11.refs_1_, bf16[19,32,128]{2,1,0:T(8,128)(2,1)S(1)} %collective-permute-done.12.refs_2_, ...), custom_call_target="tpu_custom_call" | custom-call | tf_op jit(solution)/shard_map/norm_and_project_out/pallas_call | solution.py:454
  (31 shorter events, 0.8 us)
Async XLA Ops:
  4.6 11.5 %collective-permute-start.2 = (bf16[26,32,128]{2,1,0:T(8,128)(2,1)}, bf16[26,32,128]{2,1,0:T(8,128)(2,1)S(1)}, u32[]{:S(2)}, u32[]{:S(2)}) collective-permute-start(bf16[26,32,128]{2,1,0:T(8,128)(2,1)} %get-tuple-element.32), channel_id=1, source_target_pairs={{0,6},{2,4},{4,2},{6,0},{8,14},{10,12},{12,10},{14,8},{1,7},{3,5},... | collective-permute-start | bytes 638984 | tf_op jit(solution)/shard_map/ppermute | solution.py:367
  6.2 10.5 %collective-permute-start.3 = (bf16[26,32,128]{2,1,0:T(8,128)(2,1)}, bf16[26,32,128]{2,1,0:T(8,128)(2,1)S(1)}, u32[]{:S(2)}, u32[]{:S(2)}) collective-permute-start(bf16[26,32,128]{2,1,0:T(8,128)(2,1)} %get-tuple-element.33), channel_id=1, source_target_pairs={{0,4},{2,6},{4,0},{6,2},{8,12},{10,14},{12,8},{14,10},{1,5},{3,7},... | collective-permute-start | bytes 638984 | tf_op jit(solution)/shard_map/ppermute | solution.py:367
  6.4 12.3 %collective-permute-start = (bf16[26,32,128]{2,1,0:T(8,128)(2,1)}, bf16[26,32,128]{2,1,0:T(8,128)(2,1)S(1)}, u32[]{:S(2)}, u32[]{:S(2)}) collective-permute-start(bf16[26,32,128]{2,1,0:T(8,128)(2,1)} %get-tuple-element.31), channel_id=1, source_target_pairs={{0,2},{2,0},{4,6},{6,4},{8,10},{10,8},{12,14},{14,12},{1,3},{3,1},... | collective-permute-start | bytes 638984 | tf_op jit(solution)/shard_map/ppermute | solution.py:367
  8.2 1.2 %copy-start = (bf16[32,128,128]{2,1,0:T(8,128)(2,1)S(1)}, bf16[32,128,128]{2,1,0:T(8,128)(2,1)}, u32[]{:S(2)}) copy-start(bf16[32,128,128]{2,1,0:T(8,128)(2,1)} %get-tuple-element.28.normed) | copy-start | bytes 3145732
  9.4 0.8 %copy-start.2 = (bf16[128,256]{1,0:T(8,128)(2,1)S(1)}, bf16[128,256]{1,0:T(8,128)(2,1)}, u32[]{:S(2)}) copy-start(bf16[128,256]{1,0:T(8,128)(2,1)} %proj.3) | copy-start | bytes 196612
  10.3 0.8 %copy-start.3 = (bf16[128,256]{1,0:T(8,128)(2,1)S(1)}, bf16[128,256]{1,0:T(8,128)(2,1)}, u32[]{:S(2)}) copy-start(bf16[128,256]{1,0:T(8,128)(2,1)} %gate.3) | copy-start | bytes 196612
  11.1 12.2 %copy-start.1 = (bf16[32,128,128]{2,1,0:T(8,128)(2,1)S(1)}, bf16[32,128,128]{2,1,0:T(8,128)(2,1)}, u32[]{:S(2)}) copy-start(bf16[32,128,128]{2,1,0:T(8,128)(2,1)} %get-tuple-element.28.normed) | copy-start | bytes 3145732
  11.1 12.2 %copy-start.4 = (bf16[128,128]{1,0:T(8,128)(2,1)S(1)}, bf16[128,128]{1,0:T(8,128)(2,1)}, u32[]{:S(2)}) copy-start(bf16[128,128]{1,0:T(8,128)(2,1)} %weights.1) | copy-start | bytes 98308
  13.1 17.4 %collective-permute-start.5 = (bf16[38,32,128]{2,1,0:T(8,128)(2,1)S(1)}, bf16[38,32,128]{2,1,0:T(8,128)(2,1)S(1)}, u32[]{:S(2)}, u32[]{:S(2)}) collective-permute-start(bf16[38,32,128]{2,1,0:T(8,128)(2,1)S(1)} %get-tuple-element.35), channel_id=1, source_target_pairs={{0,2},{2,0},{4,6},{6,4},{8,10},{10,8},{12,14},{14,12},{1,3},{3,1},... | collective-permute-start | bytes 933896 | tf_op jit(solution)/shard_map/ppermute | solution.py:367
  13.3 19.3 %collective-permute-start.7 = (bf16[38,32,128]{2,1,0:T(8,128)(2,1)S(1)}, bf16[38,32,128]{2,1,0:T(8,128)(2,1)S(1)}, u32[]{:S(2)}, u32[]{:S(2)}) collective-permute-start(bf16[38,32,128]{2,1,0:T(8,128)(2,1)S(1)} %get-tuple-element.36), channel_id=1, source_target_pairs={{0,6},{2,4},{4,2},{6,0},{8,14},{10,12},{12,10},{14,8},{1,7},{3,5},... | collective-permute-start | bytes 933896 | tf_op jit(solution)/shard_map/ppermute | solution.py:367
  16.2 21.2 %collective-permute-start.8 = (bf16[38,32,128]{2,1,0:T(8,128)(2,1)S(1)}, bf16[38,32,128]{2,1,0:T(8,128)(2,1)S(1)}, u32[]{:S(2)}, u32[]{:S(2)}) collective-permute-start(bf16[38,32,128]{2,1,0:T(8,128)(2,1)S(1)} %get-tuple-element.37), channel_id=1, source_target_pairs={{0,4},{2,6},{4,0},{6,2},{8,12},{10,14},{12,8},{14,10},{1,5},{3,7},... | collective-permute-start | bytes 933896 | tf_op jit(solution)/shard_map/ppermute | solution.py:367
  16.8 2.0 %collective-permute-start.4 = (bf16[13,64,128]{2,1,0:T(8,128)(2,1)S(1)}, bf16[13,64,128]{2,1,0:T(8,128)(2,1)S(1)}, u32[]{:S(2)}, u32[]{:S(2)}) collective-permute-start(bf16[13,64,128]{2,1,0:T(8,128)(2,1)S(1)} %pack_left.5), channel_id=1, source_target_pairs={{0,1},{1,0},{2,3},{3,2},{4,5},{5,4},{6,7},{7,6},{8,9},{9,8},{10,11... | collective-permute-start | bytes 638984 | tf_op jit(solution)/shard_map/ppermute | solution.py:19
  18.7 1.5 %collective-permute-start.1 = (bf16[13,64,128]{2,1,0:T(8,128)(2,1)S(1)}, bf16[13,64,128]{2,1,0:T(8,128)(2,1)S(1)}, u32[]{:S(2)}, u32[]{:S(2)}) collective-permute-start(bf16[13,64,128]{2,1,0:T(8,128)(2,1)S(1)} %pack_left.4), channel_id=1, source_target_pairs={{0,1},{1,0},{2,3},{3,2},{4,5},{5,4},{6,7},{7,6},{8,9},{9,8},{10,11... | collective-permute-start | bytes 638984 | tf_op jit(solution)/shard_map/ppermute | solution.py:19
  20.6 25.3 %collective-permute-start.14 = (bf16[13,128,128]{2,1,0:T(8,128)(2,1)S(1)}, bf16[13,128,128]{2,1,0:T(8,128)(2,1)S(1)}, u32[]{:S(2)}, u32[]{:S(2)}) collective-permute-start(bf16[13,128,128]{2,1,0:T(8,128)(2,1)S(1)} %get-tuple-element.34.after), channel_id=1, source_target_pairs={{0,8},{2,10},{4,12},{6,14},{8,0},{10,2},{12,4},{14,6},{1,9},{3,11}... | collective-permute-start | bytes 1277960 | tf_op jit(solution)/shard_map/ppermute | solution.py:367
  30.6 6.9 %collective-permute-start.6 = (bf16[19,64,128]{2,1,0:T(8,128)(2,1)S(1)}, bf16[19,64,128]{2,1,0:T(8,128)(2,1)S(1)}, u32[]{:S(2)}, u32[]{:S(2)}) collective-permute-start(bf16[19,64,128]{2,1,0:T(8,128)(2,1)S(1)} %pack_left.6), channel_id=1, source_target_pairs={{0,1},{1,0},{2,3},{3,2},{4,5},{5,4},{6,7},{7,6},{8,9},{9,8},{10,11... | collective-permute-start | bytes 933896 | tf_op jit(solution)/shard_map/ppermute | solution.py:19
  37.4 35.7 %copy-start.5 = (bf16[128,128]{1,0:T(8,128)(2,1)S(1)}, bf16[128,128]{1,0:T(8,128)(2,1)}, u32[]{:S(2)}) copy-start(bf16[128,128]{1,0:T(8,128)(2,1)} %refs_11_.1) | copy-start | bytes 98308
  37.4 35.7 %copy-start.6 = (f32[128]{0:T(128)S(1)}, f32[128]{0:T(128)}, u32[]{:S(2)}) copy-start(f32[128]{0:T(128)} %param.17) | copy-start | bytes 1540
  37.4 35.7 %copy-start.7 = (f32[128]{0:T(128)S(1)}, f32[128]{0:T(128)}, u32[]{:S(2)}) copy-start(f32[128]{0:T(128)} %param.18) | copy-start | bytes 1540
  37.4 1.7 %collective-permute-start.9 = (bf16[19,64,128]{2,1,0:T(8,128)(2,1)S(1)}, bf16[19,64,128]{2,1,0:T(8,128)(2,1)S(1)}, u32[]{:S(2)}, u32[]{:S(2)}) collective-permute-start(bf16[19,64,128]{2,1,0:T(8,128)(2,1)S(1)} %pack_left.7), channel_id=1, source_target_pairs={{0,1},{1,0},{2,3},{3,2},{4,5},{5,4},{6,7},{7,6},{8,9},{9,8},{10,11... | collective-permute-start | bytes 933896 | tf_op jit(solution)/shard_map/ppermute | solution.py:19
  39.8 12.9 %collective-permute-start.10 = (bf16[19,32,128]{2,1,0:T(8,128)(2,1)S(1)}, bf16[19,32,128]{2,1,0:T(8,128)(2,1)S(1)}, u32[]{:S(2)}, u32[]{:S(2)}) collective-permute-start(bf16[19,32,128]{2,1,0:T(8,128)(2,1)S(1)} %get-tuple-element.38), channel_id=1, source_target_pairs={{0,8},{2,10},{4,12},{6,14},{8,0},{10,2},{12,4},{14,6},{1,9},{3,11}... | collective-permute-start | bytes 466952 | tf_op jit(solution)/shard_map/ppermute | solution.py:367
  39.9 17.7 %collective-permute-start.11 = (bf16[19,32,128]{2,1,0:T(8,128)(2,1)S(1)}, bf16[19,32,128]{2,1,0:T(8,128)(2,1)S(1)}, u32[]{:S(2)}, u32[]{:S(2)}) collective-permute-start(bf16[19,32,128]{2,1,0:T(8,128)(2,1)S(1)} %get-tuple-element.39), channel_id=1, source_target_pairs={{0,14},{2,12},{4,10},{6,8},{8,6},{10,4},{12,2},{14,0},{1,15},{3,13... | collective-permute-start | bytes 466952 | tf_op jit(solution)/shard_map/ppermute | solution.py:367
  46.2 26.9 %collective-permute-start.15 = (bf16[32,32,128]{2,1,0:T(8,128)(2,1)S(1)}, bf16[32,32,128]{2,1,0:T(8,128)(2,1)S(1)}, u32[]{:S(2)}, u32[]{:S(2)}) collective-permute-start(bf16[32,32,128]{2,1,0:T(8,128)(2,1)S(1)} %get-tuple-element.48), channel_id=1, source_target_pairs={{0,6},{2,4},{4,2},{6,0},{8,14},{10,12},{12,10},{14,8},{1,7},{3,5},... | collective-permute-start | bytes 786440 | tf_op jit(solution)/shard_map/ppermute | solution.py:367
  51.0 22.1 %collective-permute-start.16 = (bf16[32,32,128]{2,1,0:T(8,128)(2,1)S(1)}, bf16[32,32,128]{2,1,0:T(8,128)(2,1)S(1)}, u32[]{:S(2)}, u32[]{:S(2)}) collective-permute-start(bf16[32,32,128]{2,1,0:T(8,128)(2,1)S(1)} %get-tuple-element.49), channel_id=1, source_target_pairs={{0,4},{2,6},{4,0},{6,2},{8,12},{10,14},{12,8},{14,10},{1,5},{3,7},... | collective-permute-start | bytes 786440 | tf_op jit(solution)/shard_map/ppermute | solution.py:367
  51.3 21.8 %collective-permute-start.17 = (bf16[32,32,128]{2,1,0:T(8,128)(2,1)S(1)}, bf16[32,32,128]{2,1,0:T(8,128)(2,1)S(1)}, u32[]{:S(2)}, u32[]{:S(2)}) collective-permute-start(bf16[32,32,128]{2,1,0:T(8,128)(2,1)S(1)} %get-tuple-element.50), channel_id=1, source_target_pairs={{0,2},{2,0},{4,6},{6,4},{8,10},{10,8},{12,14},{14,12},{1,3},{3,1},... | collective-permute-start | bytes 786440 | tf_op jit(solution)/shard_map/ppermute | solution.py:367
  52.7 18.5 %collective-permute-start.12 = (bf16[19,32,128]{2,1,0:T(8,128)(2,1)S(1)}, bf16[19,32,128]{2,1,0:T(8,128)(2,1)S(1)}, u32[]{:S(2)}, u32[]{:S(2)}) collective-permute-start(bf16[19,32,128]{2,1,0:T(8,128)(2,1)S(1)} %get-tuple-element.40), channel_id=1, source_target_pairs={{0,12},{2,14},{4,8},{6,10},{8,4},{10,6},{12,0},{14,2},{1,13},{3,15... | collective-permute-start | bytes 466952 | tf_op jit(solution)/shard_map/ppermute | solution.py:367
  57.6 15.5 %collective-permute-start.13 = (bf16[19,32,128]{2,1,0:T(8,128)(2,1)S(1)}, bf16[19,32,128]{2,1,0:T(8,128)(2,1)S(1)}, u32[]{:S(2)}, u32[]{:S(2)}) collective-permute-start(bf16[19,32,128]{2,1,0:T(8,128)(2,1)S(1)} %get-tuple-element.41), channel_id=1, source_target_pairs={{0,10},{2,8},{4,14},{6,12},{8,2},{10,0},{12,6},{14,4},{1,11},{3,9}... | collective-permute-start | bytes 466952 | tf_op jit(solution)/shard_map/ppermute | solution.py:367

commit v5 on v4

--- a/solution.py
+++ b/solution.py
@@ -9,6 +9,8 @@
 
 epsilon = 1e-05
 chunk_sizes = (13, 19)
+away_masks = (3, 2, 1, 0)
+return_masks = (0, 3, 2, 1)
 vmem_all = 60 * 1024 * 1024
 vmem_part = 28 * 1024 * 1024
 
@@ -295,7 +297,8 @@
 
 
 def finish_kernel(rows, sizes, *refs):
-    aways, totals = refs[:4], refs[4:8]
+    aways = [refs[away_masks.index(apart)] for apart in return_masks]
+    totals = refs[4:8]
     opened, gain, bias, proj, out, out_held, sems = refs[8:]
     early, late = sizes
     tile_rows = out.shape[0]
@@ -303,7 +306,8 @@
     row = lax.axis_index("row")
     at = lax.broadcasted_iota(jnp.int32, (hidden, hidden), 0)
     slot, place = at // per, at % per
-    owner = (row % 4) ^ ((4 - slot) % 4)
+    mask = sum(jnp.where(slot == place, apart, 0) for place, apart in enumerate(return_masks))
+    owner = (row % 4) ^ mask
     channel = jnp.where(
         place < early, owner * early + place, 4 * early + owner * late + place - early
     )
@@ -441,7 +445,7 @@
         [in_vmem] * 8,
         "contract",
     )(*partners, *parts)
-    aways = [exchanged(last[mask], 4 ^ mask) for mask in (0, 3, 2, 1)]
+    aways = [exchanged(last[mask], 4 ^ mask) for mask in away_masks]
     totals = call(
         add_kernel,
         [array((early + late, tile_rows, tile_cols))] * 4,
@@ -450,7 +454,7 @@
         [in_vmem] * 4,
         "add_halves",
     )(keep, arrived, *last[4:])
-    totals = spread(totals)
+    totals = [totals[0], *[exchanged(totals[mask], mask) for mask in return_masks[1:]]]
     (update,) = call(
         functools.partial(finish_kernel, 8, chunk_sizes),
         [array(pair.shape)],

time: 75.9 us -> 74.3 us (0.979)
  the two profiles are of different devices: /device:TPU:4 before, /device:TPU:0 now
where the time goes in v5:
time: 74.3 us; the launch traced here: 74.1 us
  starting transfers between devices  30.7 us (41%)
  waiting for transfers between devices  29.2 us (39%)
  Pallas kernels  10.4 us (14%)
  local copies, waits for them, and re-layouts  2.93 us (4%)
  between operations  0.82 us (1%)
    ppermute x14, starting transfers between devices, exchanged(): lax.ppermute(value, 'row', [(source, source ^ mask) for source in range(r...  29.9 us
    ppermute x14, waiting for transfers between devices, exchanged(): lax.ppermute(value, 'row', [(source, source ^ mask) for source in range(r...  26.5 us
    pallas_call x1, Pallas kernels, shards_by_halves(): call(functools.partial(first_kernel, (0, early, block)), [array(pair.shap...  3.99 us
    unnamed x16, local copies, waits for them, and re-layouts  2.93 us
    ppermute x4, waiting for transfers between devices, from_partner(): return lax.ppermute(value, axis, pairs)  2.72 us
    pallas_call x1, Pallas kernels, shards_by_halves(): call(functools.partial(finish_kernel, 8, chunk_sizes), [array(pair.shape)...  2.54 us
    pallas_call x1, Pallas kernels, shards_by_halves(): call(functools.partial(later_kernel, (block, (0, early, (0, 1)), (4 * ear...  1.95 us
  transfers between devices with their start and end apart: 18, of which 10 were waited for; matrix products, arithmetic and copies ran while one was open for 0% of the time, Pallas kernels for 5%

profile of v5, /device:TPU:0, one launch (start us, length us, event | category | flops | bytes accessed | tf_op | source)
XLA Modules:
  0.0 74.1 jit_solution(15094973016238380814)
XLA Ops:
  0.7 4.0 %norm_and_first_edges.1 = (bf16[32,128,128]{2,1,0:T(8,128)(2,1)}, bf16[26,32,128]{2,1,0:T(8,128)(2,1)}, bf16[26,32,128]{2,1,0:T(8,128)(2,1)}, bf16[26,32,128]{2,1,0:T(8,128)(2,1)}) custom-call(s32[1]{0:T(128)S(6)} %copy.11.length, bf16[32,128,128]{2,1,0:T(8,128)(2,1)} %pair.1, f32[1,128]{1,0:T(1,128)} %bitcast.6, f32[1,128]{1,0:T(1,128)} %bitcast.7, ...), custom_call_target="tpu_custom_call" | custom-call | tf_op jit(solution)/shard_map/norm_and_first_edges/pallas_call | solution.py:390
  4.6 4.0 %collective-permute-start.2 = (bf16[26,32,128]{2,1,0:T(8,128)(2,1)}, bf16[26,32,128]{2,1,0:T(8,128)(2,1)S(1)}, u32[]{:S(2)}, u32[]{:S(2)}) collective-permute-start(bf16[26,32,128]{2,1,0:T(8,128)(2,1)} %get-tuple-element.32), channel_id=1, source_target_pairs={{0,6},{2,4},{4,2},{6,0},{8,14},{10,12},{12,10},{14,8},{1,7},{3,5},... | collective-permute-start | bytes 638984 | tf_op jit(solution)/shard_map/ppermute | solution.py:371
  8.7 0.4 collective-permute-start.3
  9.3 1.2 %copy-done = bf16[32,128,128]{2,1,0:T(8,128)(2,1)S(1)} copy-done((bf16[32,128,128]{2,1,0:T(8,128)(2,1)S(1)}, bf16[32,128,128]{2,1,0:T(8,128)(2,1)}, u32[]{:S(2)}) %copy-start) | copy-done | bytes 1048600
  10.6 0.8 %copy-done.2 = bf16[128,256]{1,0:T(8,128)(2,1)S(1)} copy-done((bf16[128,256]{1,0:T(8,128)(2,1)S(1)}, bf16[128,256]{1,0:T(8,128)(2,1)}, u32[]{:S(2)}) %copy-start.2) | copy-done | bytes 65560
  11.4 0.8 %copy-done.3 = bf16[128,256]{1,0:T(8,128)(2,1)S(1)} copy-done((bf16[128,256]{1,0:T(8,128)(2,1)S(1)}, bf16[128,256]{1,0:T(8,128)(2,1)}, u32[]{:S(2)}) %copy-start.3) | copy-done | bytes 65560
  12.2 1.9 %later_edges.1 = (bf16[26,32,128]{2,1,0:T(8,128)(2,1)S(1)}, bf16[38,32,128]{2,1,0:T(8,128)(2,1)S(1)}, bf16[38,32,128]{2,1,0:T(8,128)(2,1)S(1)}, bf16[38,32,128]{2,1,0:T(8,128)(2,1)S(1)}, bf16[38,32,128]{2,1,0:T(8,128)(2,1)S(1)}) custom-call(s32[1]{0:T(128)S(6)} %copy.11.length, bf16[32,128,128]{2,1,0:T(8,128)(2,1)S(1)} %copy-done, ...), custom_call_target="tpu_custom_call" | custom-call | tf_op jit(solution)/shard_map/later_edges/pallas_call | solution.py:408
  14.2 1.9 %collective-permute-start.5 = (bf16[38,32,128]{2,1,0:T(8,128)(2,1)S(1)}, bf16[38,32,128]{2,1,0:T(8,128)(2,1)S(1)}, u32[]{:S(2)}, u32[]{:S(2)}) collective-permute-start(bf16[38,32,128]{2,1,0:T(8,128)(2,1)S(1)} %get-tuple-element.35), channel_id=1, source_target_pairs={{0,2},{2,0},{4,6},{6,4},{8,10},{10,8},{12,14},{14,12},{1,3},{3,1},... | collective-permute-start | bytes 933896 | tf_op jit(solution)/shard_map/ppermute | solution.py:371
  16.1 1.5 %collective-permute-start.7 = (bf16[38,32,128]{2,1,0:T(8,128)(2,1)S(1)}, bf16[38,32,128]{2,1,0:T(8,128)(2,1)S(1)}, u32[]{:S(2)}, u32[]{:S(2)}) collective-permute-start(bf16[38,32,128]{2,1,0:T(8,128)(2,1)S(1)} %get-tuple-element.36), channel_id=1, source_target_pairs={{0,6},{2,4},{4,2},{6,0},{8,14},{10,12},{12,10},{14,8},{1,7},{3,5},... | collective-permute-start | bytes 933896 | tf_op jit(solution)/shard_map/ppermute | solution.py:371
  17.8 2.3 %collective-permute-done.3.b.refs_5_ = bf16[26,32,128]{2,1,0:T(8,128)(2,1)S(1)} collective-permute-done((bf16[26,32,128]{2,1,0:T(8,128)(2,1)}, bf16[26,32,128]{2,1,0:T(8,128)(2,1)S(1)}, u32[]{:S(2)}, u32[]{:S(2)}) %collective-permute-start.3) | collective-permute-done | bytes 213024 | tf_op jit(solution)/shard_map/ppermute | solution.py:371
  20.3 0.6 collective-permute-start.1
  20.8 0.8 %collective-permute-done.4.refs_1_ = bf16[13,64,128]{2,1,0:T(8,128)(2,1)S(1)} collective-permute-done((bf16[13,64,128]{2,1,0:T(8,128)(2,1)S(1)}, bf16[13,64,128]{2,1,0:T(8,128)(2,1)S(1)}, u32[]{:S(2)}, u32[]{:S(2)}) %collective-permute-start.4) | collective-permute-done | bytes 213024 | tf_op jit(solution)/shard_map/ppermute | solution.py:21
  21.7 0.3 collective-permute-done.1.refs_0_
  22.0 0.4 contract.2
  22.4 2.7 %collective-permute-start.14 = (bf16[13,128,128]{2,1,0:T(8,128)(2,1)S(1)}, bf16[13,128,128]{2,1,0:T(8,128)(2,1)S(1)}, u32[]{:S(2)}, u32[]{:S(2)}) collective-permute-start(bf16[13,128,128]{2,1,0:T(8,128)(2,1)S(1)} %get-tuple-element.34.after), channel_id=1, source_target_pairs={{0,8},{2,10},{4,12},{6,14},{8,0},{10,2},{12,4},{14,6},{1,9},{3,11}... | collective-permute-start | bytes 1277960 | tf_op jit(solution)/shard_map/ppermute | solution.py:371
  25.1 0.4 output_gate.1.after.refs_8_
  25.5 6.4 %collective-permute-done.5.b.refs_3_ = bf16[38,32,128]{2,1,0:T(8,128)(2,1)S(1)} collective-permute-done((bf16[38,32,128]{2,1,0:T(8,128)(2,1)S(1)}, bf16[38,32,128]{2,1,0:T(8,128)(2,1)S(1)}, u32[]{:S(2)}, u32[]{:S(2)}) %collective-permute-start.5) | collective-permute-done | bytes 311328 | tf_op jit(solution)/shard_map/ppermute | solution.py:371
  32.0 1.6 %collective-permute-done.7.a.refs_4_ = bf16[38,32,128]{2,1,0:T(8,128)(2,1)S(1)} collective-permute-done((bf16[38,32,128]{2,1,0:T(8,128)(2,1)S(1)}, bf16[38,32,128]{2,1,0:T(8,128)(2,1)S(1)}, u32[]{:S(2)}, u32[]{:S(2)}) %collective-permute-start.7) | collective-permute-done | bytes 311328 | tf_op jit(solution)/shard_map/ppermute | solution.py:371
  33.6 6.8 %collective-permute-done.8.b.refs_5_ = bf16[38,32,128]{2,1,0:T(8,128)(2,1)S(1)} collective-permute-done((bf16[38,32,128]{2,1,0:T(8,128)(2,1)S(1)}, bf16[38,32,128]{2,1,0:T(8,128)(2,1)S(1)}, u32[]{:S(2)}, u32[]{:S(2)}) %collective-permute-start.8) | collective-permute-done | bytes 311328 | tf_op jit(solution)/shard_map/ppermute | solution.py:371
  40.6 1.6 %collective-permute-done.9.refs_1_ = bf16[19,64,128]{2,1,0:T(8,128)(2,1)S(1)} collective-permute-done((bf16[19,64,128]{2,1,0:T(8,128)(2,1)S(1)}, bf16[19,64,128]{2,1,0:T(8,128)(2,1)S(1)}, u32[]{:S(2)}, u32[]{:S(2)}) %collective-permute-start.9) | collective-permute-done | bytes 311328 | tf_op jit(solution)/shard_map/ppermute | solution.py:21
  42.2 0.7 contract.3
  42.9 0.9 %collective-permute-start.10 = (bf16[19,32,128]{2,1,0:T(8,128)(2,1)S(1)}, bf16[19,32,128]{2,1,0:T(8,128)(2,1)S(1)}, u32[]{:S(2)}, u32[]{:S(2)}) collective-permute-start(bf16[19,32,128]{2,1,0:T(8,128)(2,1)S(1)} %get-tuple-element.38), channel_id=1, source_target_pairs={{0,14},{2,12},{4,10},{6,8},{8,6},{10,4},{12,2},{14,0},{1,15},{3,13... | collective-permute-start | bytes 466952 | tf_op jit(solution)/shard_map/ppermute | solution.py:371
  43.7 2.3 %collective-permute-start.11 = (bf16[19,32,128]{2,1,0:T(8,128)(2,1)S(1)}, bf16[19,32,128]{2,1,0:T(8,128)(2,1)S(1)}, u32[]{:S(2)}, u32[]{:S(2)}) collective-permute-start(bf16[19,32,128]{2,1,0:T(8,128)(2,1)S(1)} %get-tuple-element.39), channel_id=1, source_target_pairs={{0,12},{2,14},{4,8},{6,10},{8,4},{10,6},{12,0},{14,2},{1,13},{3,15... | collective-permute-start | bytes 466952 | tf_op jit(solution)/shard_map/ppermute | solution.py:371
  46.3 0.6 collective-permute-start.15
  46.9 5.2 %collective-permute-start.16 = (bf16[32,32,128]{2,1,0:T(8,128)(2,1)S(1)}, bf16[32,32,128]{2,1,0:T(8,128)(2,1)S(1)}, u32[]{:S(2)}, u32[]{:S(2)}) collective-permute-start(bf16[32,32,128]{2,1,0:T(8,128)(2,1)S(1)} %get-tuple-element.49), channel_id=1, source_target_pairs={{0,4},{2,6},{4,0},{6,2},{8,12},{10,14},{12,8},{14,10},{1,5},{3,7},... | collective-permute-start | bytes 786440 | tf_op jit(solution)/shard_map/ppermute | solution.py:371
  52.2 1.4 %collective-permute-start.17 = (bf16[32,32,128]{2,1,0:T(8,128)(2,1)S(1)}, bf16[32,32,128]{2,1,0:T(8,128)(2,1)S(1)}, u32[]{:S(2)}, u32[]{:S(2)}) collective-permute-start(bf16[32,32,128]{2,1,0:T(8,128)(2,1)S(1)} %get-tuple-element.50), channel_id=1, source_target_pairs={{0,2},{2,0},{4,6},{6,4},{8,10},{10,8},{12,14},{14,12},{1,3},{3,1},... | collective-permute-start | bytes 786440 | tf_op jit(solution)/shard_map/ppermute | solution.py:371
  53.6 7.2 %collective-permute-start.12 = (bf16[19,32,128]{2,1,0:T(8,128)(2,1)S(1)}, bf16[19,32,128]{2,1,0:T(8,128)(2,1)S(1)}, u32[]{:S(2)}, u32[]{:S(2)}) collective-permute-start(bf16[19,32,128]{2,1,0:T(8,128)(2,1)S(1)} %get-tuple-element.40), channel_id=1, source_target_pairs={{0,10},{2,8},{4,14},{6,12},{8,2},{10,0},{12,6},{14,4},{1,11},{3,9}... | collective-permute-start | bytes 466952 | tf_op jit(solution)/shard_map/ppermute | solution.py:371
  60.7 1.4 %collective-permute-start.13 = (bf16[19,32,128]{2,1,0:T(8,128)(2,1)S(1)}, bf16[19,32,128]{2,1,0:T(8,128)(2,1)S(1)}, u32[]{:S(2)}, u32[]{:S(2)}) collective-permute-start(bf16[19,32,128]{2,1,0:T(8,128)(2,1)S(1)} %get-tuple-element.41), channel_id=1, source_target_pairs={{0,8},{2,10},{4,12},{6,14},{8,0},{10,2},{12,4},{14,6},{1,9},{3,11}... | collective-permute-start | bytes 466952 | tf_op jit(solution)/shard_map/ppermute | solution.py:371
  62.1 4.7 %collective-permute-done.12.refs_2_ = bf16[19,32,128]{2,1,0:T(8,128)(2,1)S(1)} collective-permute-done((bf16[19,32,128]{2,1,0:T(8,128)(2,1)S(1)}, bf16[19,32,128]{2,1,0:T(8,128)(2,1)S(1)}, u32[]{:S(2)}, u32[]{:S(2)}) %collective-permute-start.12) | collective-permute-done | bytes 155680 | tf_op jit(solution)/shard_map/ppermute | solution.py:371
  66.8 2.5 %collective-permute-done.13.refs_3_ = bf16[19,32,128]{2,1,0:T(8,128)(2,1)S(1)} collective-permute-done((bf16[19,32,128]{2,1,0:T(8,128)(2,1)S(1)}, bf16[19,32,128]{2,1,0:T(8,128)(2,1)S(1)}, u32[]{:S(2)}, u32[]{:S(2)}) %collective-permute-start.13) | collective-permute-done | bytes 155680 | tf_op jit(solution)/shard_map/ppermute | solution.py:371
  69.4 2.1 %collective-permute-done.16.refs_6_ = bf16[32,32,128]{2,1,0:T(8,128)(2,1)S(1)} collective-permute-done((bf16[32,32,128]{2,1,0:T(8,128)(2,1)S(1)}, bf16[32,32,128]{2,1,0:T(8,128)(2,1)S(1)}, u32[]{:S(2)}, u32[]{:S(2)}) %collective-permute-start.16) | collective-permute-done | bytes 262176 | tf_op jit(solution)/shard_map/ppermute | solution.py:371
  71.5 2.5 %norm_and_project_out.1 = bf16[32,128,128]{2,1,0:T(8,128)(2,1)} custom-call(bf16[19,32,128]{2,1,0:T(8,128)(2,1)S(1)} %collective-permute-done.10.refs_0_, bf16[19,32,128]{2,1,0:T(8,128)(2,1)S(1)} %collective-permute-done.11.refs_1_, bf16[19,32,128]{2,1,0:T(8,128)(2,1)S(1)} %collective-permute-done.12.refs_2_, ...), custom_call_target="tpu_custom_call" | custom-call | tf_op jit(solution)/shard_map/norm_and_project_out/pallas_call | solution.py:458
  (31 shorter events, 1.0 us)
Async XLA Ops:
  4.6 13.0 %collective-permute-start.2 = (bf16[26,32,128]{2,1,0:T(8,128)(2,1)}, bf16[26,32,128]{2,1,0:T(8,128)(2,1)S(1)}, u32[]{:S(2)}, u32[]{:S(2)}) collective-permute-start(bf16[26,32,128]{2,1,0:T(8,128)(2,1)} %get-tuple-element.32), channel_id=1, source_target_pairs={{0,6},{2,4},{4,2},{6,0},{8,14},{10,12},{12,10},{14,8},{1,7},{3,5},... | collective-permute-start | bytes 638984 | tf_op jit(solution)/shard_map/ppermute | solution.py:371
  8.7 11.4 %collective-permute-start.3 = (bf16[26,32,128]{2,1,0:T(8,128)(2,1)}, bf16[26,32,128]{2,1,0:T(8,128)(2,1)S(1)}, u32[]{:S(2)}, u32[]{:S(2)}) collective-permute-start(bf16[26,32,128]{2,1,0:T(8,128)(2,1)} %get-tuple-element.33), channel_id=1, source_target_pairs={{0,4},{2,6},{4,0},{6,2},{8,12},{10,14},{12,8},{14,10},{1,5},{3,7},... | collective-permute-start | bytes 638984 | tf_op jit(solution)/shard_map/ppermute | solution.py:371
  9.1 11.1 %collective-permute-start = (bf16[26,32,128]{2,1,0:T(8,128)(2,1)}, bf16[26,32,128]{2,1,0:T(8,128)(2,1)S(1)}, u32[]{:S(2)}, u32[]{:S(2)}) collective-permute-start(bf16[26,32,128]{2,1,0:T(8,128)(2,1)} %get-tuple-element.31), channel_id=1, source_target_pairs={{0,2},{2,0},{4,6},{6,4},{8,10},{10,8},{12,14},{14,12},{1,3},{3,1},... | collective-permute-start | bytes 638984 | tf_op jit(solution)/shard_map/ppermute | solution.py:371
  9.3 1.2 %copy-start = (bf16[32,128,128]{2,1,0:T(8,128)(2,1)S(1)}, bf16[32,128,128]{2,1,0:T(8,128)(2,1)}, u32[]{:S(2)}) copy-start(bf16[32,128,128]{2,1,0:T(8,128)(2,1)} %get-tuple-element.28.normed) | copy-start | bytes 3145732
  10.6 0.8 %copy-start.2 = (bf16[128,256]{1,0:T(8,128)(2,1)S(1)}, bf16[128,256]{1,0:T(8,128)(2,1)}, u32[]{:S(2)}) copy-start(bf16[128,256]{1,0:T(8,128)(2,1)} %proj.3) | copy-start | bytes 196612
  11.4 0.8 %copy-start.3 = (bf16[128,256]{1,0:T(8,128)(2,1)S(1)}, bf16[128,256]{1,0:T(8,128)(2,1)}, u32[]{:S(2)}) copy-start(bf16[128,256]{1,0:T(8,128)(2,1)} %gate.3) | copy-start | bytes 196612
  12.2 12.8 %copy-start.1 = (bf16[32,128,128]{2,1,0:T(8,128)(2,1)S(1)}, bf16[32,128,128]{2,1,0:T(8,128)(2,1)}, u32[]{:S(2)}) copy-start(bf16[32,128,128]{2,1,0:T(8,128)(2,1)} %get-tuple-element.28.normed) | copy-start | bytes 3145732
  12.2 12.8 %copy-start.4 = (bf16[128,128]{1,0:T(8,128)(2,1)S(1)}, bf16[128,128]{1,0:T(8,128)(2,1)}, u32[]{:S(2)}) copy-start(bf16[128,128]{1,0:T(8,128)(2,1)} %weights.1) | copy-start | bytes 98308
  14.2 17.6 %collective-permute-start.5 = (bf16[38,32,128]{2,1,0:T(8,128)(2,1)S(1)}, bf16[38,32,128]{2,1,0:T(8,128)(2,1)S(1)}, u32[]{:S(2)}, u32[]{:S(2)}) collective-permute-start(bf16[38,32,128]{2,1,0:T(8,128)(2,1)S(1)} %get-tuple-element.35), channel_id=1, source_target_pairs={{0,2},{2,0},{4,6},{6,4},{8,10},{10,8},{12,14},{14,12},{1,3},{3,1},... | collective-permute-start | bytes 933896 | tf_op jit(solution)/shard_map/ppermute | solution.py:371
  16.1 17.5 %collective-permute-start.7 = (bf16[38,32,128]{2,1,0:T(8,128)(2,1)S(1)}, bf16[38,32,128]{2,1,0:T(8,128)(2,1)S(1)}, u32[]{:S(2)}, u32[]{:S(2)}) collective-permute-start(bf16[38,32,128]{2,1,0:T(8,128)(2,1)S(1)} %get-tuple-element.36), channel_id=1, source_target_pairs={{0,6},{2,4},{4,2},{6,0},{8,14},{10,12},{12,10},{14,8},{1,7},{3,5},... | collective-permute-start | bytes 933896 | tf_op jit(solution)/shard_map/ppermute | solution.py:371
  17.6 22.8 %collective-permute-start.8 = (bf16[38,32,128]{2,1,0:T(8,128)(2,1)S(1)}, bf16[38,32,128]{2,1,0:T(8,128)(2,1)S(1)}, u32[]{:S(2)}, u32[]{:S(2)}) collective-permute-start(bf16[38,32,128]{2,1,0:T(8,128)(2,1)S(1)} %get-tuple-element.37), channel_id=1, source_target_pairs={{0,4},{2,6},{4,0},{6,2},{8,12},{10,14},{12,8},{14,10},{1,5},{3,7},... | collective-permute-start | bytes 933896 | tf_op jit(solution)/shard_map/ppermute | solution.py:371
  20.1 1.5 %collective-permute-start.4 = (bf16[13,64,128]{2,1,0:T(8,128)(2,1)S(1)}, bf16[13,64,128]{2,1,0:T(8,128)(2,1)S(1)}, u32[]{:S(2)}, u32[]{:S(2)}) collective-permute-start(bf16[13,64,128]{2,1,0:T(8,128)(2,1)S(1)} %pack_left.5), channel_id=1, source_target_pairs={{0,1},{1,0},{2,3},{3,2},{4,5},{5,4},{6,7},{7,6},{8,9},{9,8},{10,11... | collective-permute-start | bytes 638984 | tf_op jit(solution)/shard_map/ppermute | solution.py:21
  20.3 1.7 %collective-permute-start.1 = (bf16[13,64,128]{2,1,0:T(8,128)(2,1)S(1)}, bf16[13,64,128]{2,1,0:T(8,128)(2,1)S(1)}, u32[]{:S(2)}, u32[]{:S(2)}) collective-permute-start(bf16[13,64,128]{2,1,0:T(8,128)(2,1)S(1)} %pack_left.4), channel_id=1, source_target_pairs={{0,1},{1,0},{2,3},{3,2},{4,5},{5,4},{6,7},{7,6},{8,9},{9,8},{10,11... | collective-permute-start | bytes 638984 | tf_op jit(solution)/shard_map/ppermute | solution.py:21
  22.4 23.7 %collective-permute-start.14 = (bf16[13,128,128]{2,1,0:T(8,128)(2,1)S(1)}, bf16[13,128,128]{2,1,0:T(8,128)(2,1)S(1)}, u32[]{:S(2)}, u32[]{:S(2)}) collective-permute-start(bf16[13,128,128]{2,1,0:T(8,128)(2,1)S(1)} %get-tuple-element.34.after), channel_id=1, source_target_pairs={{0,8},{2,10},{4,12},{6,14},{8,0},{10,2},{12,4},{14,6},{1,9},{3,11}... | collective-permute-start | bytes 1277960 | tf_op jit(solution)/shard_map/ppermute | solution.py:371
  31.9 8.7 %collective-permute-start.6 = (bf16[19,64,128]{2,1,0:T(8,128)(2,1)S(1)}, bf16[19,64,128]{2,1,0:T(8,128)(2,1)S(1)}, u32[]{:S(2)}, u32[]{:S(2)}) collective-permute-start(bf16[19,64,128]{2,1,0:T(8,128)(2,1)S(1)} %pack_left.6), channel_id=1, source_target_pairs={{0,1},{1,0},{2,3},{3,2},{4,5},{5,4},{6,7},{7,6},{8,9},{9,8},{10,11... | collective-permute-start | bytes 933896 | tf_op jit(solution)/shard_map/ppermute | solution.py:21
  40.5 31.0 %copy-start.5 = (bf16[128,128]{1,0:T(8,128)(2,1)S(1)}, bf16[128,128]{1,0:T(8,128)(2,1)}, u32[]{:S(2)}) copy-start(bf16[128,128]{1,0:T(8,128)(2,1)} %refs_11_.1) | copy-start | bytes 98308
  40.5 31.0 %copy-start.6 = (f32[128]{0:T(128)S(1)}, f32[128]{0:T(128)}, u32[]{:S(2)}) copy-start(f32[128]{0:T(128)} %param.17) | copy-start | bytes 1540
  40.5 31.0 %copy-start.7 = (f32[128]{0:T(128)S(1)}, f32[128]{0:T(128)}, u32[]{:S(2)}) copy-start(f32[128]{0:T(128)} %param.18) | copy-start | bytes 1540
  40.5 1.7 %collective-permute-start.9 = (bf16[19,64,128]{2,1,0:T(8,128)(2,1)S(1)}, bf16[19,64,128]{2,1,0:T(8,128)(2,1)S(1)}, u32[]{:S(2)}, u32[]{:S(2)}) collective-permute-start(bf16[19,64,128]{2,1,0:T(8,128)(2,1)S(1)} %pack_left.7), channel_id=1, source_target_pairs={{0,1},{1,0},{2,3},{3,2},{4,5},{5,4},{6,7},{7,6},{8,9},{9,8},{10,11... | collective-permute-start | bytes 933896 | tf_op jit(solution)/shard_map/ppermute | solution.py:21
  42.9 10.7 %collective-permute-start.10 = (bf16[19,32,128]{2,1,0:T(8,128)(2,1)S(1)}, bf16[19,32,128]{2,1,0:T(8,128)(2,1)S(1)}, u32[]{:S(2)}, u32[]{:S(2)}) collective-permute-start(bf16[19,32,128]{2,1,0:T(8,128)(2,1)S(1)} %get-tuple-element.38), channel_id=1, source_target_pairs={{0,14},{2,12},{4,10},{6,8},{8,6},{10,4},{12,2},{14,0},{1,15},{3,13... | collective-permute-start | bytes 466952 | tf_op jit(solution)/shard_map/ppermute | solution.py:371
  43.7 17.0 %collective-permute-start.11 = (bf16[19,32,128]{2,1,0:T(8,128)(2,1)S(1)}, bf16[19,32,128]{2,1,0:T(8,128)(2,1)S(1)}, u32[]{:S(2)}, u32[]{:S(2)}) collective-permute-start(bf16[19,32,128]{2,1,0:T(8,128)(2,1)S(1)} %get-tuple-element.39), channel_id=1, source_target_pairs={{0,12},{2,14},{4,8},{6,10},{8,4},{10,6},{12,0},{14,2},{1,13},{3,15... | collective-permute-start | bytes 466952 | tf_op jit(solution)/shard_map/ppermute | solution.py:371
  46.3 23.1 %collective-permute-start.15 = (bf16[32,32,128]{2,1,0:T(8,128)(2,1)S(1)}, bf16[32,32,128]{2,1,0:T(8,128)(2,1)S(1)}, u32[]{:S(2)}, u32[]{:S(2)}) collective-permute-start(bf16[32,32,128]{2,1,0:T(8,128)(2,1)S(1)} %get-tuple-element.48), channel_id=1, source_target_pairs={{0,6},{2,4},{4,2},{6,0},{8,14},{10,12},{12,10},{14,8},{1,7},{3,5},... | collective-permute-start | bytes 786440 | tf_op jit(solution)/shard_map/ppermute | solution.py:371
  46.9 24.6 %collective-permute-start.16 = (bf16[32,32,128]{2,1,0:T(8,128)(2,1)S(1)}, bf16[32,32,128]{2,1,0:T(8,128)(2,1)S(1)}, u32[]{:S(2)}, u32[]{:S(2)}) collective-permute-start(bf16[32,32,128]{2,1,0:T(8,128)(2,1)S(1)} %get-tuple-element.49), channel_id=1, source_target_pairs={{0,4},{2,6},{4,0},{6,2},{8,12},{10,14},{12,8},{14,10},{1,5},{3,7},... | collective-permute-start | bytes 786440 | tf_op jit(solution)/shard_map/ppermute | solution.py:371
  52.2 19.3 %collective-permute-start.17 = (bf16[32,32,128]{2,1,0:T(8,128)(2,1)S(1)}, bf16[32,32,128]{2,1,0:T(8,128)(2,1)S(1)}, u32[]{:S(2)}, u32[]{:S(2)}) collective-permute-start(bf16[32,32,128]{2,1,0:T(8,128)(2,1)S(1)} %get-tuple-element.50), channel_id=1, source_target_pairs={{0,2},{2,0},{4,6},{6,4},{8,10},{10,8},{12,14},{14,12},{1,3},{3,1},... | collective-permute-start | bytes 786440 | tf_op jit(solution)/shard_map/ppermute | solution.py:371
  53.6 13.3 %collective-permute-start.12 = (bf16[19,32,128]{2,1,0:T(8,128)(2,1)S(1)}, bf16[19,32,128]{2,1,0:T(8,128)(2,1)S(1)}, u32[]{:S(2)}, u32[]{:S(2)}) collective-permute-start(bf16[19,32,128]{2,1,0:T(8,128)(2,1)S(1)} %get-tuple-element.40), channel_id=1, source_target_pairs={{0,10},{2,8},{4,14},{6,12},{8,2},{10,0},{12,6},{14,4},{1,11},{3,9}... | collective-permute-start | bytes 466952 | tf_op jit(solution)/shard_map/ppermute | solution.py:371
  60.7 8.7 %collective-permute-start.13 = (bf16[19,32,128]{2,1,0:T(8,128)(2,1)S(1)}, bf16[19,32,128]{2,1,0:T(8,128)(2,1)S(1)}, u32[]{:S(2)}, u32[]{:S(2)}) collective-permute-start(bf16[19,32,128]{2,1,0:T(8,128)(2,1)S(1)} %get-tuple-element.41), channel_id=1, source_target_pairs={{0,8},{2,10},{4,12},{6,14},{8,0},{10,2},{12,4},{14,6},{1,9},{3,11}... | collective-permute-start | bytes 466952 | tf_op jit(solution)/shard_map/ppermute | solution.py:371

commit v6 on v5

--- a/solution.py
+++ b/solution.py
@@ -435,8 +435,8 @@
         [in_vmem],
         "output_gate",
     )(away, normed, gate_out)
-    partners = [swapped_left(opened, second[0], second[3]), swapped_left(opened, second[1], second[2])]
-    parts = [second[0], second[3], second[1], second[2]]
+    partners = [swapped_left(opened, second[0], second[1]), swapped_left(opened, second[2], second[3])]
+    parts = [second[0], second[1], second[2], second[3]]
     last = call(
         last_contract_kernel,
         [array((late, tile_rows, tile_cols))] * 8,

time: 74.3 us -> 74.3 us (level)
  transfers between devices with their start and end apart: 18 -> 18, of which waited for: 10 -> 9; matrix products, arithmetic and copies ran while one was open for 0% -> 0% of each run, Pallas kernels for 5% -> 5%
where the time goes in v6:
time: 74.3 us; the launch traced here: 74.1 us
  starting transfers between devices  30.7 us (41%)
  waiting for transfers between devices  29.2 us (39%)
  Pallas kernels  10.4 us (14%)
  local copies, waits for them, and re-layouts  2.93 us (4%)
  between operations  0.83 us (1%)
    ppermute x14, starting transfers between devices, exchanged(): lax.ppermute(value, 'row', [(source, source ^ mask) for source in range(r...  30 us
    ppermute x14, waiting for transfers between devices, exchanged(): lax.ppermute(value, 'row', [(source, source ^ mask) for source in range(r...  26.5 us
    pallas_call x1, Pallas kernels, shards_by_halves(): call(functools.partial(first_kernel, (0, early, block)), [array(pair.shap...  3.99 us
    unnamed x16, local copies, waits for them, and re-layouts  2.93 us
    ppermute x4, waiting for transfers between devices, from_partner(): return lax.ppermute(value, axis, pairs)  2.72 us
    pallas_call x1, Pallas kernels, shards_by_halves(): call(functools.partial(finish_kernel, 8, chunk_sizes), [array(pair.shape)...  2.54 us
    pallas_call x1, Pallas kernels, shards_by_halves(): call(functools.partial(later_kernel, (block, (0, early, (0, 1)), (4 * ear...  1.95 us
  transfers between devices with their start and end apart: 18, of which 9 were waited for; matrix products, arithmetic and copies ran while one was open for 0% of the time, Pallas kernels for 5%

profile of v6, /device:TPU:0, one launch (start us, length us, event | category | flops | bytes accessed | tf_op | source)
XLA Modules:
  0.0 74.1 jit_solution(7691376059177600196)
XLA Ops:
  0.7 4.0 %norm_and_first_edges.1 = (bf16[32,128,128]{2,1,0:T(8,128)(2,1)}, bf16[26,32,128]{2,1,0:T(8,128)(2,1)}, bf16[26,32,128]{2,1,0:T(8,128)(2,1)}, bf16[26,32,128]{2,1,0:T(8,128)(2,1)}) custom-call(s32[1]{0:T(128)S(6)} %copy.11.length, bf16[32,128,128]{2,1,0:T(8,128)(2,1)} %pair.1, f32[1,128]{1,0:T(1,128)} %bitcast.6, f32[1,128]{1,0:T(1,128)} %bitcast.7, ...), custom_call_target="tpu_custom_call" | custom-call | tf_op jit(solution)/shard_map/norm_and_first_edges/pallas_call | solution.py:390
  4.6 4.0 %collective-permute-start.2 = (bf16[26,32,128]{2,1,0:T(8,128)(2,1)}, bf16[26,32,128]{2,1,0:T(8,128)(2,1)S(1)}, u32[]{:S(2)}, u32[]{:S(2)}) collective-permute-start(bf16[26,32,128]{2,1,0:T(8,128)(2,1)} %get-tuple-element.32), channel_id=1, source_target_pairs={{0,6},{2,4},{4,2},{6,0},{8,14},{10,12},{12,10},{14,8},{1,7},{3,5},... | collective-permute-start | bytes 638984 | tf_op jit(solution)/shard_map/ppermute | solution.py:371
  8.7 0.4 collective-permute-start.3
  9.3 1.2 %copy-done = bf16[32,128,128]{2,1,0:T(8,128)(2,1)S(1)} copy-done((bf16[32,128,128]{2,1,0:T(8,128)(2,1)S(1)}, bf16[32,128,128]{2,1,0:T(8,128)(2,1)}, u32[]{:S(2)}) %copy-start) | copy-done | bytes 1048600
  10.6 0.8 %copy-done.2 = bf16[128,256]{1,0:T(8,128)(2,1)S(1)} copy-done((bf16[128,256]{1,0:T(8,128)(2,1)S(1)}, bf16[128,256]{1,0:T(8,128)(2,1)}, u32[]{:S(2)}) %copy-start.2) | copy-done | bytes 65560
  11.4 0.8 %copy-done.3 = bf16[128,256]{1,0:T(8,128)(2,1)S(1)} copy-done((bf16[128,256]{1,0:T(8,128)(2,1)S(1)}, bf16[128,256]{1,0:T(8,128)(2,1)}, u32[]{:S(2)}) %copy-start.3) | copy-done | bytes 65560
  12.2 1.9 %later_edges.1 = (bf16[26,32,128]{2,1,0:T(8,128)(2,1)S(1)}, bf16[38,32,128]{2,1,0:T(8,128)(2,1)S(1)}, bf16[38,32,128]{2,1,0:T(8,128)(2,1)S(1)}, bf16[38,32,128]{2,1,0:T(8,128)(2,1)S(1)}, bf16[38,32,128]{2,1,0:T(8,128)(2,1)S(1)}) custom-call(s32[1]{0:T(128)S(6)} %copy.11.length, bf16[32,128,128]{2,1,0:T(8,128)(2,1)S(1)} %copy-done, ...), custom_call_target="tpu_custom_call" | custom-call | tf_op jit(solution)/shard_map/later_edges/pallas_call | solution.py:408
  14.2 2.9 %collective-permute-start.5 = (bf16[38,32,128]{2,1,0:T(8,128)(2,1)S(1)}, bf16[38,32,128]{2,1,0:T(8,128)(2,1)S(1)}, u32[]{:S(2)}, u32[]{:S(2)}) collective-permute-start(bf16[38,32,128]{2,1,0:T(8,128)(2,1)S(1)} %get-tuple-element.35), channel_id=1, source_target_pairs={{0,6},{2,4},{4,2},{6,0},{8,14},{10,12},{12,10},{14,8},{1,7},{3,5},... | collective-permute-start | bytes 933896 | tf_op jit(solution)/shard_map/ppermute | solution.py:371
  17.1 0.4 collective-permute-start.7
  17.8 2.3 %collective-permute-done.3.b.refs_5_ = bf16[26,32,128]{2,1,0:T(8,128)(2,1)S(1)} collective-permute-done((bf16[26,32,128]{2,1,0:T(8,128)(2,1)}, bf16[26,32,128]{2,1,0:T(8,128)(2,1)S(1)}, u32[]{:S(2)}, u32[]{:S(2)}) %collective-permute-start.3) | collective-permute-done | bytes 213024 | tf_op jit(solution)/shard_map/ppermute | solution.py:371
  20.3 0.6 collective-permute-start.1
  20.8 0.8 %collective-permute-done.4.refs_1_ = bf16[13,64,128]{2,1,0:T(8,128)(2,1)S(1)} collective-permute-done((bf16[13,64,128]{2,1,0:T(8,128)(2,1)S(1)}, bf16[13,64,128]{2,1,0:T(8,128)(2,1)S(1)}, u32[]{:S(2)}, u32[]{:S(2)}) %collective-permute-start.4) | collective-permute-done | bytes 213024 | tf_op jit(solution)/shard_map/ppermute | solution.py:21
  21.7 0.3 collective-permute-done.1.refs_0_
  22.0 0.4 contract.2
  22.4 2.7 %collective-permute-start.14 = (bf16[13,128,128]{2,1,0:T(8,128)(2,1)S(1)}, bf16[13,128,128]{2,1,0:T(8,128)(2,1)S(1)}, u32[]{:S(2)}, u32[]{:S(2)}) collective-permute-start(bf16[13,128,128]{2,1,0:T(8,128)(2,1)S(1)} %get-tuple-element.34.after), channel_id=1, source_target_pairs={{0,8},{2,10},{4,12},{6,14},{8,0},{10,2},{12,4},{14,6},{1,9},{3,11}... | collective-permute-start | bytes 1277960 | tf_op jit(solution)/shard_map/ppermute | solution.py:371
  25.1 0.4 output_gate.1.after.refs_8_
  25.5 0.8 %collective-permute-done.5.b.refs_3_ = bf16[38,32,128]{2,1,0:T(8,128)(2,1)S(1)} collective-permute-done((bf16[38,32,128]{2,1,0:T(8,128)(2,1)S(1)}, bf16[38,32,128]{2,1,0:T(8,128)(2,1)S(1)}, u32[]{:S(2)}, u32[]{:S(2)}) %collective-permute-start.5) | collective-permute-done | bytes 311328 | tf_op jit(solution)/shard_map/ppermute | solution.py:371
  26.5 14.0 %collective-permute-done.7.a.refs_4_ = bf16[38,32,128]{2,1,0:T(8,128)(2,1)S(1)} collective-permute-done((bf16[38,32,128]{2,1,0:T(8,128)(2,1)S(1)}, bf16[38,32,128]{2,1,0:T(8,128)(2,1)S(1)}, u32[]{:S(2)}, u32[]{:S(2)}) %collective-permute-start.7) | collective-permute-done | bytes 311328 | tf_op jit(solution)/shard_map/ppermute | solution.py:371
  40.6 1.6 %collective-permute-done.9.refs_1_ = bf16[19,64,128]{2,1,0:T(8,128)(2,1)S(1)} collective-permute-done((bf16[19,64,128]{2,1,0:T(8,128)(2,1)S(1)}, bf16[19,64,128]{2,1,0:T(8,128)(2,1)S(1)}, u32[]{:S(2)}, u32[]{:S(2)}) %collective-permute-start.9) | collective-permute-done | bytes 311328 | tf_op jit(solution)/shard_map/ppermute | solution.py:21
  42.2 0.6 contract.3
  42.9 0.9 %collective-permute-start.10 = (bf16[19,32,128]{2,1,0:T(8,128)(2,1)S(1)}, bf16[19,32,128]{2,1,0:T(8,128)(2,1)S(1)}, u32[]{:S(2)}, u32[]{:S(2)}) collective-permute-start(bf16[19,32,128]{2,1,0:T(8,128)(2,1)S(1)} %get-tuple-element.38), channel_id=1, source_target_pairs={{0,14},{2,12},{4,10},{6,8},{8,6},{10,4},{12,2},{14,0},{1,15},{3,13... | collective-permute-start | bytes 466952 | tf_op jit(solution)/shard_map/ppermute | solution.py:371
  43.7 2.4 %collective-permute-start.11 = (bf16[19,32,128]{2,1,0:T(8,128)(2,1)S(1)}, bf16[19,32,128]{2,1,0:T(8,128)(2,1)S(1)}, u32[]{:S(2)}, u32[]{:S(2)}) collective-permute-start(bf16[19,32,128]{2,1,0:T(8,128)(2,1)S(1)} %get-tuple-element.39), channel_id=1, source_target_pairs={{0,12},{2,14},{4,8},{6,10},{8,4},{10,6},{12,0},{14,2},{1,13},{3,15... | collective-permute-start | bytes 466952 | tf_op jit(solution)/shard_map/ppermute | solution.py:371
  46.1 0.2 add_halves.1
  46.3 0.6 collective-permute-start.15
  46.9 5.3 %collective-permute-start.16 = (bf16[32,32,128]{2,1,0:T(8,128)(2,1)S(1)}, bf16[32,32,128]{2,1,0:T(8,128)(2,1)S(1)}, u32[]{:S(2)}, u32[]{:S(2)}) collective-permute-start(bf16[32,32,128]{2,1,0:T(8,128)(2,1)S(1)} %get-tuple-element.49), channel_id=1, source_target_pairs={{0,4},{2,6},{4,0},{6,2},{8,12},{10,14},{12,8},{14,10},{1,5},{3,7},... | collective-permute-start | bytes 786440 | tf_op jit(solution)/shard_map/ppermute | solution.py:371
  52.2 1.4 %collective-permute-start.17 = (bf16[32,32,128]{2,1,0:T(8,128)(2,1)S(1)}, bf16[32,32,128]{2,1,0:T(8,128)(2,1)S(1)}, u32[]{:S(2)}, u32[]{:S(2)}) collective-permute-start(bf16[32,32,128]{2,1,0:T(8,128)(2,1)S(1)} %get-tuple-element.50), channel_id=1, source_target_pairs={{0,2},{2,0},{4,6},{6,4},{8,10},{10,8},{12,14},{14,12},{1,3},{3,1},... | collective-permute-start | bytes 786440 | tf_op jit(solution)/shard_map/ppermute | solution.py:371
  53.6 7.2 %collective-permute-start.12 = (bf16[19,32,128]{2,1,0:T(8,128)(2,1)S(1)}, bf16[19,32,128]{2,1,0:T(8,128)(2,1)S(1)}, u32[]{:S(2)}, u32[]{:S(2)}) collective-permute-start(bf16[19,32,128]{2,1,0:T(8,128)(2,1)S(1)} %get-tuple-element.40), channel_id=1, source_target_pairs={{0,10},{2,8},{4,14},{6,12},{8,2},{10,0},{12,6},{14,4},{1,11},{3,9}... | collective-permute-start | bytes 466952 | tf_op jit(solution)/shard_map/ppermute | solution.py:371
  60.7 1.4 %collective-permute-start.13 = (bf16[19,32,128]{2,1,0:T(8,128)(2,1)S(1)}, bf16[19,32,128]{2,1,0:T(8,128)(2,1)S(1)}, u32[]{:S(2)}, u32[]{:S(2)}) collective-permute-start(bf16[19,32,128]{2,1,0:T(8,128)(2,1)S(1)} %get-tuple-element.41), channel_id=1, source_target_pairs={{0,8},{2,10},{4,12},{6,14},{8,0},{10,2},{12,4},{14,6},{1,9},{3,11}... | collective-permute-start | bytes 466952 | tf_op jit(solution)/shard_map/ppermute | solution.py:371
  62.1 4.7 %collective-permute-done.12.refs_2_ = bf16[19,32,128]{2,1,0:T(8,128)(2,1)S(1)} collective-permute-done((bf16[19,32,128]{2,1,0:T(8,128)(2,1)S(1)}, bf16[19,32,128]{2,1,0:T(8,128)(2,1)S(1)}, u32[]{:S(2)}, u32[]{:S(2)}) %collective-permute-start.12) | collective-permute-done | bytes 155680 | tf_op jit(solution)/shard_map/ppermute | solution.py:371
  66.8 2.5 %collective-permute-done.13.refs_3_ = bf16[19,32,128]{2,1,0:T(8,128)(2,1)S(1)} collective-permute-done((bf16[19,32,128]{2,1,0:T(8,128)(2,1)S(1)}, bf16[19,32,128]{2,1,0:T(8,128)(2,1)S(1)}, u32[]{:S(2)}, u32[]{:S(2)}) %collective-permute-start.13) | collective-permute-done | bytes 155680 | tf_op jit(solution)/shard_map/ppermute | solution.py:371
  69.4 2.1 %collective-permute-done.16.refs_6_ = bf16[32,32,128]{2,1,0:T(8,128)(2,1)S(1)} collective-permute-done((bf16[32,32,128]{2,1,0:T(8,128)(2,1)S(1)}, bf16[32,32,128]{2,1,0:T(8,128)(2,1)S(1)}, u32[]{:S(2)}, u32[]{:S(2)}) %collective-permute-start.16) | collective-permute-done | bytes 262176 | tf_op jit(solution)/shard_map/ppermute | solution.py:371
  71.5 2.5 %norm_and_project_out.1 = bf16[32,128,128]{2,1,0:T(8,128)(2,1)} custom-call(bf16[19,32,128]{2,1,0:T(8,128)(2,1)S(1)} %collective-permute-done.10.refs_0_, bf16[19,32,128]{2,1,0:T(8,128)(2,1)S(1)} %collective-permute-done.11.refs_1_, bf16[19,32,128]{2,1,0:T(8,128)(2,1)S(1)} %collective-permute-done.12.refs_2_, ...), custom_call_target="tpu_custom_call" | custom-call | tf_op jit(solution)/shard_map/norm_and_project_out/pallas_call | solution.py:458
  (31 shorter events, 0.9 us)
Async XLA Ops:
  4.6 12.9 %collective-permute-start.2 = (bf16[26,32,128]{2,1,0:T(8,128)(2,1)}, bf16[26,32,128]{2,1,0:T(8,128)(2,1)S(1)}, u32[]{:S(2)}, u32[]{:S(2)}) collective-permute-start(bf16[26,32,128]{2,1,0:T(8,128)(2,1)} %get-tuple-element.32), channel_id=1, source_target_pairs={{0,6},{2,4},{4,2},{6,0},{8,14},{10,12},{12,10},{14,8},{1,7},{3,5},... | collective-permute-start | bytes 638984 | tf_op jit(solution)/shard_map/ppermute | solution.py:371
  8.7 11.4 %collective-permute-start.3 = (bf16[26,32,128]{2,1,0:T(8,128)(2,1)}, bf16[26,32,128]{2,1,0:T(8,128)(2,1)S(1)}, u32[]{:S(2)}, u32[]{:S(2)}) collective-permute-start(bf16[26,32,128]{2,1,0:T(8,128)(2,1)} %get-tuple-element.33), channel_id=1, source_target_pairs={{0,4},{2,6},{4,0},{6,2},{8,12},{10,14},{12,8},{14,10},{1,5},{3,7},... | collective-permute-start | bytes 638984 | tf_op jit(solution)/shard_map/ppermute | solution.py:371
  9.1 11.1 %collective-permute-start = (bf16[26,32,128]{2,1,0:T(8,128)(2,1)}, bf16[26,32,128]{2,1,0:T(8,128)(2,1)S(1)}, u32[]{:S(2)}, u32[]{:S(2)}) collective-permute-start(bf16[26,32,128]{2,1,0:T(8,128)(2,1)} %get-tuple-element.31), channel_id=1, source_target_pairs={{0,2},{2,0},{4,6},{6,4},{8,10},{10,8},{12,14},{14,12},{1,3},{3,1},... | collective-permute-start | bytes 638984 | tf_op jit(solution)/shard_map/ppermute | solution.py:371
  9.3 1.2 %copy-start = (bf16[32,128,128]{2,1,0:T(8,128)(2,1)S(1)}, bf16[32,128,128]{2,1,0:T(8,128)(2,1)}, u32[]{:S(2)}) copy-start(bf16[32,128,128]{2,1,0:T(8,128)(2,1)} %get-tuple-element.28.normed) | copy-start | bytes 3145732
  10.6 0.8 %copy-start.2 = (bf16[128,256]{1,0:T(8,128)(2,1)S(1)}, bf16[128,256]{1,0:T(8,128)(2,1)}, u32[]{:S(2)}) copy-start(bf16[128,256]{1,0:T(8,128)(2,1)} %proj.3) | copy-start | bytes 196612
  11.4 0.8 %copy-start.3 = (bf16[128,256]{1,0:T(8,128)(2,1)S(1)}, bf16[128,256]{1,0:T(8,128)(2,1)}, u32[]{:S(2)}) copy-start(bf16[128,256]{1,0:T(8,128)(2,1)} %gate.3) | copy-start | bytes 196612
  12.2 12.8 %copy-start.1 = (bf16[32,128,128]{2,1,0:T(8,128)(2,1)S(1)}, bf16[32,128,128]{2,1,0:T(8,128)(2,1)}, u32[]{:S(2)}) copy-start(bf16[32,128,128]{2,1,0:T(8,128)(2,1)} %get-tuple-element.28.normed) | copy-start | bytes 3145732
  12.2 12.8 %copy-start.4 = (bf16[128,128]{1,0:T(8,128)(2,1)S(1)}, bf16[128,128]{1,0:T(8,128)(2,1)}, u32[]{:S(2)}) copy-start(bf16[128,128]{1,0:T(8,128)(2,1)} %weights.1) | copy-start | bytes 98308
  14.2 12.1 %collective-permute-start.5 = (bf16[38,32,128]{2,1,0:T(8,128)(2,1)S(1)}, bf16[38,32,128]{2,1,0:T(8,128)(2,1)S(1)}, u32[]{:S(2)}, u32[]{:S(2)}) collective-permute-start(bf16[38,32,128]{2,1,0:T(8,128)(2,1)S(1)} %get-tuple-element.35), channel_id=1, source_target_pairs={{0,6},{2,4},{4,2},{6,0},{8,14},{10,12},{12,10},{14,8},{1,7},{3,5},... | collective-permute-start | bytes 933896 | tf_op jit(solution)/shard_map/ppermute | solution.py:371
  17.1 23.3 %collective-permute-start.7 = (bf16[38,32,128]{2,1,0:T(8,128)(2,1)S(1)}, bf16[38,32,128]{2,1,0:T(8,128)(2,1)S(1)}, u32[]{:S(2)}, u32[]{:S(2)}) collective-permute-start(bf16[38,32,128]{2,1,0:T(8,128)(2,1)S(1)} %get-tuple-element.36), channel_id=1, source_target_pairs={{0,4},{2,6},{4,0},{6,2},{8,12},{10,14},{12,8},{14,10},{1,5},{3,7},... | collective-permute-start | bytes 933896 | tf_op jit(solution)/shard_map/ppermute | solution.py:371
  17.6 22.9 %collective-permute-start.8 = (bf16[38,32,128]{2,1,0:T(8,128)(2,1)S(1)}, bf16[38,32,128]{2,1,0:T(8,128)(2,1)S(1)}, u32[]{:S(2)}, u32[]{:S(2)}) collective-permute-start(bf16[38,32,128]{2,1,0:T(8,128)(2,1)S(1)} %get-tuple-element.37), channel_id=1, source_target_pairs={{0,2},{2,0},{4,6},{6,4},{8,10},{10,8},{12,14},{14,12},{1,3},{3,1},... | collective-permute-start | bytes 933896 | tf_op jit(solution)/shard_map/ppermute | solution.py:371
  20.1 1.5 %collective-permute-start.4 = (bf16[13,64,128]{2,1,0:T(8,128)(2,1)S(1)}, bf16[13,64,128]{2,1,0:T(8,128)(2,1)S(1)}, u32[]{:S(2)}, u32[]{:S(2)}) collective-permute-start(bf16[13,64,128]{2,1,0:T(8,128)(2,1)S(1)} %pack_left.5), channel_id=1, source_target_pairs={{0,1},{1,0},{2,3},{3,2},{4,5},{5,4},{6,7},{7,6},{8,9},{9,8},{10,11... | collective-permute-start | bytes 638984 | tf_op jit(solution)/shard_map/ppermute | solution.py:21
  20.3 1.7 %collective-permute-start.1 = (bf16[13,64,128]{2,1,0:T(8,128)(2,1)S(1)}, bf16[13,64,128]{2,1,0:T(8,128)(2,1)S(1)}, u32[]{:S(2)}, u32[]{:S(2)}) collective-permute-start(bf16[13,64,128]{2,1,0:T(8,128)(2,1)S(1)} %pack_left.4), channel_id=1, source_target_pairs={{0,1},{1,0},{2,3},{3,2},{4,5},{5,4},{6,7},{7,6},{8,9},{9,8},{10,11... | collective-permute-start | bytes 638984 | tf_op jit(solution)/shard_map/ppermute | solution.py:21
  22.4 23.7 %collective-permute-start.14 = (bf16[13,128,128]{2,1,0:T(8,128)(2,1)S(1)}, bf16[13,128,128]{2,1,0:T(8,128)(2,1)S(1)}, u32[]{:S(2)}, u32[]{:S(2)}) collective-permute-start(bf16[13,128,128]{2,1,0:T(8,128)(2,1)S(1)} %get-tuple-element.34.after), channel_id=1, source_target_pairs={{0,8},{2,10},{4,12},{6,14},{8,0},{10,2},{12,4},{14,6},{1,9},{3,11}... | collective-permute-start | bytes 1277960 | tf_op jit(solution)/shard_map/ppermute | solution.py:371
  26.4 14.2 %collective-permute-start.6 = (bf16[19,64,128]{2,1,0:T(8,128)(2,1)S(1)}, bf16[19,64,128]{2,1,0:T(8,128)(2,1)S(1)}, u32[]{:S(2)}, u32[]{:S(2)}) collective-permute-start(bf16[19,64,128]{2,1,0:T(8,128)(2,1)S(1)} %pack_left.6), channel_id=1, source_target_pairs={{0,1},{1,0},{2,3},{3,2},{4,5},{5,4},{6,7},{7,6},{8,9},{9,8},{10,11... | collective-permute-start | bytes 933896 | tf_op jit(solution)/shard_map/ppermute | solution.py:21
  40.5 31.0 %copy-start.5 = (bf16[128,128]{1,0:T(8,128)(2,1)S(1)}, bf16[128,128]{1,0:T(8,128)(2,1)}, u32[]{:S(2)}) copy-start(bf16[128,128]{1,0:T(8,128)(2,1)} %refs_11_.1) | copy-start | bytes 98308
  40.5 31.0 %copy-start.6 = (f32[128]{0:T(128)S(1)}, f32[128]{0:T(128)}, u32[]{:S(2)}) copy-start(f32[128]{0:T(128)} %param.17) | copy-start | bytes 1540
  40.5 31.0 %copy-start.7 = (f32[128]{0:T(128)S(1)}, f32[128]{0:T(128)}, u32[]{:S(2)}) copy-start(f32[128]{0:T(128)} %param.18) | copy-start | bytes 1540
  40.5 1.7 %collective-permute-start.9 = (bf16[19,64,128]{2,1,0:T(8,128)(2,1)S(1)}, bf16[19,64,128]{2,1,0:T(8,128)(2,1)S(1)}, u32[]{:S(2)}, u32[]{:S(2)}) collective-permute-start(bf16[19,64,128]{2,1,0:T(8,128)(2,1)S(1)} %pack_left.7), channel_id=1, source_target_pairs={{0,1},{1,0},{2,3},{3,2},{4,5},{5,4},{6,7},{7,6},{8,9},{9,8},{10,11... | collective-permute-start | bytes 933896 | tf_op jit(solution)/shard_map/ppermute | solution.py:21
  42.9 10.7 %collective-permute-start.10 = (bf16[19,32,128]{2,1,0:T(8,128)(2,1)S(1)}, bf16[19,32,128]{2,1,0:T(8,128)(2,1)S(1)}, u32[]{:S(2)}, u32[]{:S(2)}) collective-permute-start(bf16[19,32,128]{2,1,0:T(8,128)(2,1)S(1)} %get-tuple-element.38), channel_id=1, source_target_pairs={{0,14},{2,12},{4,10},{6,8},{8,6},{10,4},{12,2},{14,0},{1,15},{3,13... | collective-permute-start | bytes 466952 | tf_op jit(solution)/shard_map/ppermute | solution.py:371
  43.7 17.0 %collective-permute-start.11 = (bf16[19,32,128]{2,1,0:T(8,128)(2,1)S(1)}, bf16[19,32,128]{2,1,0:T(8,128)(2,1)S(1)}, u32[]{:S(2)}, u32[]{:S(2)}) collective-permute-start(bf16[19,32,128]{2,1,0:T(8,128)(2,1)S(1)} %get-tuple-element.39), channel_id=1, source_target_pairs={{0,12},{2,14},{4,8},{6,10},{8,4},{10,6},{12,0},{14,2},{1,13},{3,15... | collective-permute-start | bytes 466952 | tf_op jit(solution)/shard_map/ppermute | solution.py:371
  46.3 23.1 %collective-permute-start.15 = (bf16[32,32,128]{2,1,0:T(8,128)(2,1)S(1)}, bf16[32,32,128]{2,1,0:T(8,128)(2,1)S(1)}, u32[]{:S(2)}, u32[]{:S(2)}) collective-permute-start(bf16[32,32,128]{2,1,0:T(8,128)(2,1)S(1)} %get-tuple-element.48), channel_id=1, source_target_pairs={{0,6},{2,4},{4,2},{6,0},{8,14},{10,12},{12,10},{14,8},{1,7},{3,5},... | collective-permute-start | bytes 786440 | tf_op jit(solution)/shard_map/ppermute | solution.py:371
  46.9 24.6 %collective-permute-start.16 = (bf16[32,32,128]{2,1,0:T(8,128)(2,1)S(1)}, bf16[32,32,128]{2,1,0:T(8,128)(2,1)S(1)}, u32[]{:S(2)}, u32[]{:S(2)}) collective-permute-start(bf16[32,32,128]{2,1,0:T(8,128)(2,1)S(1)} %get-tuple-element.49), channel_id=1, source_target_pairs={{0,4},{2,6},{4,0},{6,2},{8,12},{10,14},{12,8},{14,10},{1,5},{3,7},... | collective-permute-start | bytes 786440 | tf_op jit(solution)/shard_map/ppermute | solution.py:371
  52.2 19.3 %collective-permute-start.17 = (bf16[32,32,128]{2,1,0:T(8,128)(2,1)S(1)}, bf16[32,32,128]{2,1,0:T(8,128)(2,1)S(1)}, u32[]{:S(2)}, u32[]{:S(2)}) collective-permute-start(bf16[32,32,128]{2,1,0:T(8,128)(2,1)S(1)} %get-tuple-element.50), channel_id=1, source_target_pairs={{0,2},{2,0},{4,6},{6,4},{8,10},{10,8},{12,14},{14,12},{1,3},{3,1},... | collective-permute-start | bytes 786440 | tf_op jit(solution)/shard_map/ppermute | solution.py:371
  53.6 13.3 %collective-permute-start.12 = (bf16[19,32,128]{2,1,0:T(8,128)(2,1)S(1)}, bf16[19,32,128]{2,1,0:T(8,128)(2,1)S(1)}, u32[]{:S(2)}, u32[]{:S(2)}) collective-permute-start(bf16[19,32,128]{2,1,0:T(8,128)(2,1)S(1)} %get-tuple-element.40), channel_id=1, source_target_pairs={{0,10},{2,8},{4,14},{6,12},{8,2},{10,0},{12,6},{14,4},{1,11},{3,9}... | collective-permute-start | bytes 466952 | tf_op jit(solution)/shard_map/ppermute | solution.py:371
  60.7 8.7 %collective-permute-start.13 = (bf16[19,32,128]{2,1,0:T(8,128)(2,1)S(1)}, bf16[19,32,128]{2,1,0:T(8,128)(2,1)S(1)}, u32[]{:S(2)}, u32[]{:S(2)}) collective-permute-start(bf16[19,32,128]{2,1,0:T(8,128)(2,1)S(1)} %get-tuple-element.41), channel_id=1, source_target_pairs={{0,8},{2,10},{4,12},{6,14},{8,0},{10,2},{12,4},{14,6},{1,9},{3,11}... | collective-permute-start | bytes 466952 | tf_op jit(solution)/shard_map/ppermute | solution.py:371

commit v7 on v6

--- a/solution.py
+++ b/solution.py
@@ -434,6 +434,7 @@
         [in_any] + [in_vmem] * 2,
         [in_vmem],
         "output_gate",
+        vmem_all,
     )(away, normed, gate_out)
     partners = [swapped_left(opened, second[0], second[1]), swapped_left(opened, second[2], second[3])]
     parts = [second[0], second[1], second[2], second[3]]

time: 74.3 us -> 74.4 us (level)
  waiting for transfers between devices: 29.2 us -> 25 us
  Pallas kernels: 10.4 us -> 13 us
  local copies, waits for them, and re-layouts: 2.93 us -> 4.52 us
    ppermute x14, waiting for transfers between devices: 26.5 us -> 22.2 us  [exchanged(): lax.ppermute(value, 'row', [(source, source ^ mask) for source in range(r...]
    pallas_call x1, Pallas kernels: 0.42 us -> 3 us  [shards_by_halves(): call(functools.partial(gate_kernel, block), [array(pair.shape, jnp.float3...]
    unnamed x16 -> x18, local copies, waits for them, and re-layouts: 2.93 us -> 4.52 us
  transfers between devices with their start and end apart: 18 -> 18, of which waited for: 9 -> 8; matrix products, arithmetic and copies ran while one was open for 0% -> 0% of each run, Pallas kernels for 5% -> 9%
where the time goes in v7:
time: 74.4 us; the launch traced here: 74 us
  starting transfers between devices  30.8 us (41%)
  waiting for transfers between devices  25 us (34%)
  Pallas kernels  13 us (17%)
  local copies, waits for them, and re-layouts  4.52 us (6%)
  between operations  0.82 us (1%)
    ppermute x14, starting transfers between devices, exchanged(): lax.ppermute(value, 'row', [(source, source ^ mask) for source in range(r...  30 us
    ppermute x14, waiting for transfers between devices, exchanged(): lax.ppermute(value, 'row', [(source, source ^ mask) for source in range(r...  22.2 us
    unnamed x18, local copies, waits for them, and re-layouts  4.52 us
    pallas_call x1, Pallas kernels, shards_by_halves(): call(functools.partial(first_kernel, (0, early, block)), [array(pair.shap...  3.99 us
    pallas_call x1, Pallas kernels, shards_by_halves(): call(functools.partial(gate_kernel, block), [array(pair.shape, jnp.float3...  3 us
    ppermute x4, waiting for transfers between devices, from_partner(): return lax.ppermute(value, axis, pairs)  2.72 us
    pallas_call x1, Pallas kernels, shards_by_halves(): call(functools.partial(finish_kernel, 8, chunk_sizes), [array(pair.shape)...  2.54 us
    pallas_call x1, Pallas kernels, shards_by_halves(): call(functools.partial(later_kernel, (block, (0, early, (0, 1)), (4 * ear...  1.95 us
  transfers between devices with their start and end apart: 18, of which 8 were waited for; matrix products, arithmetic and copies ran while one was open for 0% of the time, Pallas kernels for 9%

profile of v7, /device:TPU:0, one launch (start us, length us, event | category | flops | bytes accessed | tf_op | source)
XLA Modules:
  0.0 74.0 jit_solution(6103937939617237701)
XLA Ops:
  0.7 4.0 %norm_and_first_edges.1 = (bf16[32,128,128]{2,1,0:T(8,128)(2,1)}, bf16[26,32,128]{2,1,0:T(8,128)(2,1)}, bf16[26,32,128]{2,1,0:T(8,128)(2,1)}, bf16[26,32,128]{2,1,0:T(8,128)(2,1)}) custom-call(s32[1]{0:T(128)S(6)} %copy.11.length, bf16[32,128,128]{2,1,0:T(8,128)(2,1)} %pair.1, f32[1,128]{1,0:T(1,128)} %bitcast.6, f32[1,128]{1,0:T(1,128)} %bitcast.7, ...), custom_call_target="tpu_custom_call" | custom-call | tf_op jit(solution)/shard_map/norm_and_first_edges/pallas_call | solution.py:390
  4.6 4.0 %collective-permute-start.2 = (bf16[26,32,128]{2,1,0:T(8,128)(2,1)}, bf16[26,32,128]{2,1,0:T(8,128)(2,1)S(1)}, u32[]{:S(2)}, u32[]{:S(2)}) collective-permute-start(bf16[26,32,128]{2,1,0:T(8,128)(2,1)} %get-tuple-element.32), channel_id=1, source_target_pairs={{0,6},{2,4},{4,2},{6,0},{8,14},{10,12},{12,10},{14,8},{1,7},{3,5},... | collective-permute-start | bytes 638984 | tf_op jit(solution)/shard_map/ppermute | solution.py:371
  8.7 0.4 collective-permute-start.3
  9.3 1.2 %copy-done.2 = bf16[32,128,128]{2,1,0:T(8,128)(2,1)S(1)} copy-done((bf16[32,128,128]{2,1,0:T(8,128)(2,1)S(1)}, bf16[32,128,128]{2,1,0:T(8,128)(2,1)}, u32[]{:S(2)}) %copy-start.2) | copy-done | bytes 1048600
  10.6 0.8 %copy-done.4 = bf16[128,256]{1,0:T(8,128)(2,1)S(1)} copy-done((bf16[128,256]{1,0:T(8,128)(2,1)S(1)}, bf16[128,256]{1,0:T(8,128)(2,1)}, u32[]{:S(2)}) %copy-start.4) | copy-done | bytes 65560
  11.4 0.8 %copy-done.5 = bf16[128,256]{1,0:T(8,128)(2,1)S(1)} copy-done((bf16[128,256]{1,0:T(8,128)(2,1)S(1)}, bf16[128,256]{1,0:T(8,128)(2,1)}, u32[]{:S(2)}) %copy-start.5) | copy-done | bytes 65560
  12.2 2.0 %later_edges.1 = (bf16[26,32,128]{2,1,0:T(8,128)(2,1)S(1)}, bf16[38,32,128]{2,1,0:T(8,128)(2,1)S(1)}, bf16[38,32,128]{2,1,0:T(8,128)(2,1)S(1)}, bf16[38,32,128]{2,1,0:T(8,128)(2,1)S(1)}, bf16[38,32,128]{2,1,0:T(8,128)(2,1)S(1)}) custom-call(s32[1]{0:T(128)S(6)} %copy.11.length, bf16[32,128,128]{2,1,0:T(8,128)(2,1)S(1)} %copy-done.2, ...), custom_call_target="tpu_custom_call" | custom-call | tf_op jit(solution)/shard_map/later_edges/pallas_call | solution.py:408
  14.2 2.9 %collective-permute-start.5 = (bf16[38,32,128]{2,1,0:T(8,128)(2,1)S(1)}, bf16[38,32,128]{2,1,0:T(8,128)(2,1)S(1)}, u32[]{:S(2)}, u32[]{:S(2)}) collective-permute-start(bf16[38,32,128]{2,1,0:T(8,128)(2,1)S(1)} %get-tuple-element.35), channel_id=1, source_target_pairs={{0,6},{2,4},{4,2},{6,0},{8,14},{10,12},{12,10},{14,8},{1,7},{3,5},... | collective-permute-start | bytes 933896 | tf_op jit(solution)/shard_map/ppermute | solution.py:371
  17.1 0.4 collective-permute-start.7
  17.8 2.3 %collective-permute-done.3.b.refs_5_ = bf16[26,32,128]{2,1,0:T(8,128)(2,1)S(1)} collective-permute-done((bf16[26,32,128]{2,1,0:T(8,128)(2,1)}, bf16[26,32,128]{2,1,0:T(8,128)(2,1)S(1)}, u32[]{:S(2)}, u32[]{:S(2)}) %collective-permute-start.3) | collective-permute-done | bytes 213024 | tf_op jit(solution)/shard_map/ppermute | solution.py:371
  20.3 0.6 collective-permute-start.1
  20.8 0.8 %collective-permute-done.4.refs_1_ = bf16[13,64,128]{2,1,0:T(8,128)(2,1)S(1)} collective-permute-done((bf16[13,64,128]{2,1,0:T(8,128)(2,1)S(1)}, bf16[13,64,128]{2,1,0:T(8,128)(2,1)S(1)}, u32[]{:S(2)}, u32[]{:S(2)}) %collective-permute-start.4) | collective-permute-done | bytes 213024 | tf_op jit(solution)/shard_map/ppermute | solution.py:21
  21.7 0.3 collective-permute-done.1.refs_0_
  22.0 0.4 contract.2
  22.4 2.6 %collective-permute-start.14 = (bf16[13,128,128]{2,1,0:T(8,128)(2,1)S(1)}, bf16[13,128,128]{2,1,0:T(8,128)(2,1)S(1)}, u32[]{:S(2)}, u32[]{:S(2)}) collective-permute-start(bf16[13,128,128]{2,1,0:T(8,128)(2,1)S(1)} %get-tuple-element.34.after), channel_id=1, source_target_pairs={{0,8},{2,10},{4,12},{6,14},{8,0},{10,2},{12,4},{14,6},{1,9},{3,11}... | collective-permute-start | bytes 1277960 | tf_op jit(solution)/shard_map/ppermute | solution.py:371
  25.1 3.0 %output_gate.1.after.refs_8_ = f32[32,128,128]{2,1,0:T(8,128)} custom-call(bf16[13,128,128]{2,1,0:T(8,128)(2,1)} %copy-done.3, bf16[32,128,128]{2,1,0:T(8,128)(2,1)} %get-tuple-element.28.normed, bf16[128,128]{1,0:T(8,128)(2,1)} %weights.1), custom_call_target="tpu_custom_call" | custom-call | tf_op jit(solution)/shard_map/output_gate/pallas_call | solution.py:430
  28.1 1.6 %copy-done = f32[32,128,128]{2,1,0:T(8,128)S(1)} copy-done((f32[32,128,128]{2,1,0:T(8,128)S(1)}, f32[32,128,128]{2,1,0:T(8,128)}, u32[]{:S(2)}) %copy-start) | copy-done | bytes 2097176
  29.8 10.6 %collective-permute-done.7.a.refs_4_ = bf16[38,32,128]{2,1,0:T(8,128)(2,1)S(1)} collective-permute-done((bf16[38,32,128]{2,1,0:T(8,128)(2,1)S(1)}, bf16[38,32,128]{2,1,0:T(8,128)(2,1)S(1)}, u32[]{:S(2)}, u32[]{:S(2)}) %collective-permute-start.7) | collective-permute-done | bytes 311328 | tf_op jit(solution)/shard_map/ppermute | solution.py:371
  40.6 1.6 %collective-permute-done.9.refs_1_ = bf16[19,64,128]{2,1,0:T(8,128)(2,1)S(1)} collective-permute-done((bf16[19,64,128]{2,1,0:T(8,128)(2,1)S(1)}, bf16[19,64,128]{2,1,0:T(8,128)(2,1)S(1)}, u32[]{:S(2)}, u32[]{:S(2)}) %collective-permute-start.9) | collective-permute-done | bytes 311328 | tf_op jit(solution)/shard_map/ppermute | solution.py:21
  42.2 0.6 contract.3
  42.9 0.9 %collective-permute-start.10 = (bf16[19,32,128]{2,1,0:T(8,128)(2,1)S(1)}, bf16[19,32,128]{2,1,0:T(8,128)(2,1)S(1)}, u32[]{:S(2)}, u32[]{:S(2)}) collective-permute-start(bf16[19,32,128]{2,1,0:T(8,128)(2,1)S(1)} %get-tuple-element.38), channel_id=1, source_target_pairs={{0,14},{2,12},{4,10},{6,8},{8,6},{10,4},{12,2},{14,0},{1,15},{3,13... | collective-permute-start | bytes 466952 | tf_op jit(solution)/shard_map/ppermute | solution.py:371
  43.7 2.3 %collective-permute-start.11 = (bf16[19,32,128]{2,1,0:T(8,128)(2,1)S(1)}, bf16[19,32,128]{2,1,0:T(8,128)(2,1)S(1)}, u32[]{:S(2)}, u32[]{:S(2)}) collective-permute-start(bf16[19,32,128]{2,1,0:T(8,128)(2,1)S(1)} %get-tuple-element.39), channel_id=1, source_target_pairs={{0,12},{2,14},{4,8},{6,10},{8,4},{10,6},{12,0},{14,2},{1,13},{3,15... | collective-permute-start | bytes 466952 | tf_op jit(solution)/shard_map/ppermute | solution.py:371
  46.1 0.2 add_halves.1
  46.3 0.6 collective-permute-start.15
  46.9 5.3 %collective-permute-start.16 = (bf16[32,32,128]{2,1,0:T(8,128)(2,1)S(1)}, bf16[32,32,128]{2,1,0:T(8,128)(2,1)S(1)}, u32[]{:S(2)}, u32[]{:S(2)}) collective-permute-start(bf16[32,32,128]{2,1,0:T(8,128)(2,1)S(1)} %get-tuple-element.49), channel_id=1, source_target_pairs={{0,4},{2,6},{4,0},{6,2},{8,12},{10,14},{12,8},{14,10},{1,5},{3,7},... | collective-permute-start | bytes 786440 | tf_op jit(solution)/shard_map/ppermute | solution.py:371
  52.2 1.4 %collective-permute-start.17 = (bf16[32,32,128]{2,1,0:T(8,128)(2,1)S(1)}, bf16[32,32,128]{2,1,0:T(8,128)(2,1)S(1)}, u32[]{:S(2)}, u32[]{:S(2)}) collective-permute-start(bf16[32,32,128]{2,1,0:T(8,128)(2,1)S(1)} %get-tuple-element.50), channel_id=1, source_target_pairs={{0,2},{2,0},{4,6},{6,4},{8,10},{10,8},{12,14},{14,12},{1,3},{3,1},... | collective-permute-start | bytes 786440 | tf_op jit(solution)/shard_map/ppermute | solution.py:371
  53.6 7.1 %collective-permute-start.12 = (bf16[19,32,128]{2,1,0:T(8,128)(2,1)S(1)}, bf16[19,32,128]{2,1,0:T(8,128)(2,1)S(1)}, u32[]{:S(2)}, u32[]{:S(2)}) collective-permute-start(bf16[19,32,128]{2,1,0:T(8,128)(2,1)S(1)} %get-tuple-element.40), channel_id=1, source_target_pairs={{0,10},{2,8},{4,14},{6,12},{8,2},{10,0},{12,6},{14,4},{1,11},{3,9}... | collective-permute-start | bytes 466952 | tf_op jit(solution)/shard_map/ppermute | solution.py:371
  60.7 1.4 %collective-permute-start.13 = (bf16[19,32,128]{2,1,0:T(8,128)(2,1)S(1)}, bf16[19,32,128]{2,1,0:T(8,128)(2,1)S(1)}, u32[]{:S(2)}, u32[]{:S(2)}) collective-permute-start(bf16[19,32,128]{2,1,0:T(8,128)(2,1)S(1)} %get-tuple-element.41), channel_id=1, source_target_pairs={{0,8},{2,10},{4,12},{6,14},{8,0},{10,2},{12,4},{14,6},{1,9},{3,11}... | collective-permute-start | bytes 466952 | tf_op jit(solution)/shard_map/ppermute | solution.py:371
  62.2 4.7 %collective-permute-done.12.refs_2_ = bf16[19,32,128]{2,1,0:T(8,128)(2,1)S(1)} collective-permute-done((bf16[19,32,128]{2,1,0:T(8,128)(2,1)S(1)}, bf16[19,32,128]{2,1,0:T(8,128)(2,1)S(1)}, u32[]{:S(2)}, u32[]{:S(2)}) %collective-permute-start.12) | collective-permute-done | bytes 155680 | tf_op jit(solution)/shard_map/ppermute | solution.py:371
  66.9 2.5 %collective-permute-done.13.refs_3_ = bf16[19,32,128]{2,1,0:T(8,128)(2,1)S(1)} collective-permute-done((bf16[19,32,128]{2,1,0:T(8,128)(2,1)S(1)}, bf16[19,32,128]{2,1,0:T(8,128)(2,1)S(1)}, u32[]{:S(2)}, u32[]{:S(2)}) %collective-permute-start.13) | collective-permute-done | bytes 155680 | tf_op jit(solution)/shard_map/ppermute | solution.py:371
  69.4 2.1 %collective-permute-done.16.refs_6_ = bf16[32,32,128]{2,1,0:T(8,128)(2,1)S(1)} collective-permute-done((bf16[32,32,128]{2,1,0:T(8,128)(2,1)S(1)}, bf16[32,32,128]{2,1,0:T(8,128)(2,1)S(1)}, u32[]{:S(2)}, u32[]{:S(2)}) %collective-permute-start.16) | collective-permute-done | bytes 262176 | tf_op jit(solution)/shard_map/ppermute | solution.py:371
  71.5 2.5 %norm_and_project_out.1 = bf16[32,128,128]{2,1,0:T(8,128)(2,1)} custom-call(bf16[19,32,128]{2,1,0:T(8,128)(2,1)S(1)} %collective-permute-done.10.refs_0_, bf16[19,32,128]{2,1,0:T(8,128)(2,1)S(1)} %collective-permute-done.11.refs_1_, bf16[19,32,128]{2,1,0:T(8,128)(2,1)S(1)} %collective-permute-done.12.refs_2_, ...), custom_call_target="tpu_custom_call" | custom-call | tf_op jit(solution)/shard_map/norm_and_project_out/pallas_call | solution.py:459
  (33 shorter events, 0.9 us)
Async XLA Ops:
  4.6 12.9 %collective-permute-start.2 = (bf16[26,32,128]{2,1,0:T(8,128)(2,1)}, bf16[26,32,128]{2,1,0:T(8,128)(2,1)S(1)}, u32[]{:S(2)}, u32[]{:S(2)}) collective-permute-start(bf16[26,32,128]{2,1,0:T(8,128)(2,1)} %get-tuple-element.32), channel_id=1, source_target_pairs={{0,6},{2,4},{4,2},{6,0},{8,14},{10,12},{12,10},{14,8},{1,7},{3,5},... | collective-permute-start | bytes 638984 | tf_op jit(solution)/shard_map/ppermute | solution.py:371
  8.7 11.4 %collective-permute-start.3 = (bf16[26,32,128]{2,1,0:T(8,128)(2,1)}, bf16[26,32,128]{2,1,0:T(8,128)(2,1)S(1)}, u32[]{:S(2)}, u32[]{:S(2)}) collective-permute-start(bf16[26,32,128]{2,1,0:T(8,128)(2,1)} %get-tuple-element.33), channel_id=1, source_target_pairs={{0,4},{2,6},{4,0},{6,2},{8,12},{10,14},{12,8},{14,10},{1,5},{3,7},... | collective-permute-start | bytes 638984 | tf_op jit(solution)/shard_map/ppermute | solution.py:371
  9.1 11.1 %collective-permute-start = (bf16[26,32,128]{2,1,0:T(8,128)(2,1)}, bf16[26,32,128]{2,1,0:T(8,128)(2,1)S(1)}, u32[]{:S(2)}, u32[]{:S(2)}) collective-permute-start(bf16[26,32,128]{2,1,0:T(8,128)(2,1)} %get-tuple-element.31), channel_id=1, source_target_pairs={{0,2},{2,0},{4,6},{6,4},{8,10},{10,8},{12,14},{14,12},{1,3},{3,1},... | collective-permute-start | bytes 638984 | tf_op jit(solution)/shard_map/ppermute | solution.py:371
  9.3 1.2 %copy-start.2 = (bf16[32,128,128]{2,1,0:T(8,128)(2,1)S(1)}, bf16[32,128,128]{2,1,0:T(8,128)(2,1)}, u32[]{:S(2)}) copy-start(bf16[32,128,128]{2,1,0:T(8,128)(2,1)} %get-tuple-element.28.normed) | copy-start | bytes 3145732
  10.6 0.8 %copy-start.4 = (bf16[128,256]{1,0:T(8,128)(2,1)S(1)}, bf16[128,256]{1,0:T(8,128)(2,1)}, u32[]{:S(2)}) copy-start(bf16[128,256]{1,0:T(8,128)(2,1)} %proj.3) | copy-start | bytes 196612
  11.4 0.8 %copy-start.5 = (bf16[128,256]{1,0:T(8,128)(2,1)S(1)}, bf16[128,256]{1,0:T(8,128)(2,1)}, u32[]{:S(2)}) copy-start(bf16[128,256]{1,0:T(8,128)(2,1)} %gate.3) | copy-start | bytes 196612
  14.2 13.9 %collective-permute-start.5 = (bf16[38,32,128]{2,1,0:T(8,128)(2,1)S(1)}, bf16[38,32,128]{2,1,0:T(8,128)(2,1)S(1)}, u32[]{:S(2)}, u32[]{:S(2)}) collective-permute-start(bf16[38,32,128]{2,1,0:T(8,128)(2,1)S(1)} %get-tuple-element.35), channel_id=1, source_target_pairs={{0,6},{2,4},{4,2},{6,0},{8,14},{10,12},{12,10},{14,8},{1,7},{3,5},... | collective-permute-start | bytes 933896 | tf_op jit(solution)/shard_map/ppermute | solution.py:371
  17.1 23.3 %collective-permute-start.7 = (bf16[38,32,128]{2,1,0:T(8,128)(2,1)S(1)}, bf16[38,32,128]{2,1,0:T(8,128)(2,1)S(1)}, u32[]{:S(2)}, u32[]{:S(2)}) collective-permute-start(bf16[38,32,128]{2,1,0:T(8,128)(2,1)S(1)} %get-tuple-element.36), channel_id=1, source_target_pairs={{0,4},{2,6},{4,0},{6,2},{8,12},{10,14},{12,8},{14,10},{1,5},{3,7},... | collective-permute-start | bytes 933896 | tf_op jit(solution)/shard_map/ppermute | solution.py:371
  17.6 22.9 %collective-permute-start.8 = (bf16[38,32,128]{2,1,0:T(8,128)(2,1)S(1)}, bf16[38,32,128]{2,1,0:T(8,128)(2,1)S(1)}, u32[]{:S(2)}, u32[]{:S(2)}) collective-permute-start(bf16[38,32,128]{2,1,0:T(8,128)(2,1)S(1)} %get-tuple-element.37), channel_id=1, source_target_pairs={{0,2},{2,0},{4,6},{6,4},{8,10},{10,8},{12,14},{14,12},{1,3},{3,1},... | collective-permute-start | bytes 933896 | tf_op jit(solution)/shard_map/ppermute | solution.py:371
  20.1 1.5 %collective-permute-start.4 = (bf16[13,64,128]{2,1,0:T(8,128)(2,1)S(1)}, bf16[13,64,128]{2,1,0:T(8,128)(2,1)S(1)}, u32[]{:S(2)}, u32[]{:S(2)}) collective-permute-start(bf16[13,64,128]{2,1,0:T(8,128)(2,1)S(1)} %pack_left.5), channel_id=1, source_target_pairs={{0,1},{1,0},{2,3},{3,2},{4,5},{5,4},{6,7},{7,6},{8,9},{9,8},{10,11... | collective-permute-start | bytes 638984 | tf_op jit(solution)/shard_map/ppermute | solution.py:21
  20.3 1.7 %collective-permute-start.1 = (bf16[13,64,128]{2,1,0:T(8,128)(2,1)S(1)}, bf16[13,64,128]{2,1,0:T(8,128)(2,1)S(1)}, u32[]{:S(2)}, u32[]{:S(2)}) collective-permute-start(bf16[13,64,128]{2,1,0:T(8,128)(2,1)S(1)} %pack_left.4), channel_id=1, source_target_pairs={{0,1},{1,0},{2,3},{3,2},{4,5},{5,4},{6,7},{7,6},{8,9},{9,8},{10,11... | collective-permute-start | bytes 638984 | tf_op jit(solution)/shard_map/ppermute | solution.py:21
  22.4 2.7 %copy-start.3 = (bf16[13,128,128]{2,1,0:T(8,128)(2,1)}, bf16[13,128,128]{2,1,0:T(8,128)(2,1)S(1)}, u32[]{:S(2)}) copy-start(bf16[13,128,128]{2,1,0:T(8,128)(2,1)S(1)} %get-tuple-element.34.after) | copy-start | bytes 1277956
  22.4 23.7 %collective-permute-start.14 = (bf16[13,128,128]{2,1,0:T(8,128)(2,1)S(1)}, bf16[13,128,128]{2,1,0:T(8,128)(2,1)S(1)}, u32[]{:S(2)}, u32[]{:S(2)}) collective-permute-start(bf16[13,128,128]{2,1,0:T(8,128)(2,1)S(1)} %get-tuple-element.34.after), channel_id=1, source_target_pairs={{0,8},{2,10},{4,12},{6,14},{8,0},{10,2},{12,4},{14,6},{1,9},{3,11}... | collective-permute-start | bytes 1277960 | tf_op jit(solution)/shard_map/ppermute | solution.py:371
  28.1 1.6 %copy-start = (f32[32,128,128]{2,1,0:T(8,128)S(1)}, f32[32,128,128]{2,1,0:T(8,128)}, u32[]{:S(2)}) copy-start(f32[32,128,128]{2,1,0:T(8,128)} %output_gate.1.after.refs_8_) | copy-start | bytes 6291460
  29.7 10.8 %copy-start.1 = (f32[32,128,128]{2,1,0:T(8,128)S(1)}, f32[32,128,128]{2,1,0:T(8,128)}, u32[]{:S(2)}) copy-start(f32[32,128,128]{2,1,0:T(8,128)} %output_gate.1.after.refs_8_) | copy-start | bytes 6291460
  29.7 10.9 %collective-permute-start.6 = (bf16[19,64,128]{2,1,0:T(8,128)(2,1)S(1)}, bf16[19,64,128]{2,1,0:T(8,128)(2,1)S(1)}, u32[]{:S(2)}, u32[]{:S(2)}) collective-permute-start(bf16[19,64,128]{2,1,0:T(8,128)(2,1)S(1)} %pack_left.6), channel_id=1, source_target_pairs={{0,1},{1,0},{2,3},{3,2},{4,5},{5,4},{6,7},{7,6},{8,9},{9,8},{10,11... | collective-permute-start | bytes 933896 | tf_op jit(solution)/shard_map/ppermute | solution.py:21
  40.5 31.0 %copy-start.6 = (bf16[128,128]{1,0:T(8,128)(2,1)S(1)}, bf16[128,128]{1,0:T(8,128)(2,1)}, u32[]{:S(2)}) copy-start(bf16[128,128]{1,0:T(8,128)(2,1)} %refs_11_.1) | copy-start | bytes 98308
  40.5 31.0 %copy-start.7 = (f32[128]{0:T(128)S(1)}, f32[128]{0:T(128)}, u32[]{:S(2)}) copy-start(f32[128]{0:T(128)} %param.17) | copy-start | bytes 1540
  40.5 31.0 %copy-start.8 = (f32[128]{0:T(128)S(1)}, f32[128]{0:T(128)}, u32[]{:S(2)}) copy-start(f32[128]{0:T(128)} %param.18) | copy-start | bytes 1540
  40.5 1.7 %collective-permute-start.9 = (bf16[19,64,128]{2,1,0:T(8,128)(2,1)S(1)}, bf16[19,64,128]{2,1,0:T(8,128)(2,1)S(1)}, u32[]{:S(2)}, u32[]{:S(2)}) collective-permute-start(bf16[19,64,128]{2,1,0:T(8,128)(2,1)S(1)} %pack_left.7), channel_id=1, source_target_pairs={{0,1},{1,0},{2,3},{3,2},{4,5},{5,4},{6,7},{7,6},{8,9},{9,8},{10,11... | collective-permute-start | bytes 933896 | tf_op jit(solution)/shard_map/ppermute | solution.py:21
  42.9 10.8 %collective-permute-start.10 = (bf16[19,32,128]{2,1,0:T(8,128)(2,1)S(1)}, bf16[19,32,128]{2,1,0:T(8,128)(2,1)S(1)}, u32[]{:S(2)}, u32[]{:S(2)}) collective-permute-start(bf16[19,32,128]{2,1,0:T(8,128)(2,1)S(1)} %get-tuple-element.38), channel_id=1, source_target_pairs={{0,14},{2,12},{4,10},{6,8},{8,6},{10,4},{12,2},{14,0},{1,15},{3,13... | collective-permute-start | bytes 466952 | tf_op jit(solution)/shard_map/ppermute | solution.py:371
  43.7 17.0 %collective-permute-start.11 = (bf16[19,32,128]{2,1,0:T(8,128)(2,1)S(1)}, bf16[19,32,128]{2,1,0:T(8,128)(2,1)S(1)}, u32[]{:S(2)}, u32[]{:S(2)}) collective-permute-start(bf16[19,32,128]{2,1,0:T(8,128)(2,1)S(1)} %get-tuple-element.39), channel_id=1, source_target_pairs={{0,12},{2,14},{4,8},{6,10},{8,4},{10,6},{12,0},{14,2},{1,13},{3,15... | collective-permute-start | bytes 466952 | tf_op jit(solution)/shard_map/ppermute | solution.py:371
  46.3 23.1 %collective-permute-start.15 = (bf16[32,32,128]{2,1,0:T(8,128)(2,1)S(1)}, bf16[32,32,128]{2,1,0:T(8,128)(2,1)S(1)}, u32[]{:S(2)}, u32[]{:S(2)}) collective-permute-start(bf16[32,32,128]{2,1,0:T(8,128)(2,1)S(1)} %get-tuple-element.48), channel_id=1, source_target_pairs={{0,6},{2,4},{4,2},{6,0},{8,14},{10,12},{12,10},{14,8},{1,7},{3,5},... | collective-permute-start | bytes 786440 | tf_op jit(solution)/shard_map/ppermute | solution.py:371
  46.9 24.6 %collective-permute-start.16 = (bf16[32,32,128]{2,1,0:T(8,128)(2,1)S(1)}, bf16[32,32,128]{2,1,0:T(8,128)(2,1)S(1)}, u32[]{:S(2)}, u32[]{:S(2)}) collective-permute-start(bf16[32,32,128]{2,1,0:T(8,128)(2,1)S(1)} %get-tuple-element.49), channel_id=1, source_target_pairs={{0,4},{2,6},{4,0},{6,2},{8,12},{10,14},{12,8},{14,10},{1,5},{3,7},... | collective-permute-start | bytes 786440 | tf_op jit(solution)/shard_map/ppermute | solution.py:371
  52.2 19.2 %collective-permute-start.17 = (bf16[32,32,128]{2,1,0:T(8,128)(2,1)S(1)}, bf16[32,32,128]{2,1,0:T(8,128)(2,1)S(1)}, u32[]{:S(2)}, u32[]{:S(2)}) collective-permute-start(bf16[32,32,128]{2,1,0:T(8,128)(2,1)S(1)} %get-tuple-element.50), channel_id=1, source_target_pairs={{0,2},{2,0},{4,6},{6,4},{8,10},{10,8},{12,14},{14,12},{1,3},{3,1},... | collective-permute-start | bytes 786440 | tf_op jit(solution)/shard_map/ppermute | solution.py:371
  53.6 13.2 %collective-permute-start.12 = (bf16[19,32,128]{2,1,0:T(8,128)(2,1)S(1)}, bf16[19,32,128]{2,1,0:T(8,128)(2,1)S(1)}, u32[]{:S(2)}, u32[]{:S(2)}) collective-permute-start(bf16[19,32,128]{2,1,0:T(8,128)(2,1)S(1)} %get-tuple-element.40), channel_id=1, source_target_pairs={{0,10},{2,8},{4,14},{6,12},{8,2},{10,0},{12,6},{14,4},{1,11},{3,9}... | collective-permute-start | bytes 466952 | tf_op jit(solution)/shard_map/ppermute | solution.py:371
  60.7 8.6 %collective-permute-start.13 = (bf16[19,32,128]{2,1,0:T(8,128)(2,1)S(1)}, bf16[19,32,128]{2,1,0:T(8,128)(2,1)S(1)}, u32[]{:S(2)}, u32[]{:S(2)}) collective-permute-start(bf16[19,32,128]{2,1,0:T(8,128)(2,1)S(1)} %get-tuple-element.41), channel_id=1, source_target_pairs={{0,8},{2,10},{4,12},{6,14},{8,0},{10,2},{12,4},{14,6},{1,9},{3,11}... | collective-permute-start | bytes 466952 | tf_op jit(solution)/shard_map/ppermute | solution.py:371

commit v8 on v7

--- a/solution.py
+++ b/solution.py
@@ -12,7 +12,7 @@
 away_masks = (3, 2, 1, 0)
 return_masks = (0, 3, 2, 1)
 vmem_all = 60 * 1024 * 1024
-vmem_part = 28 * 1024 * 1024
+vmem_part = 16 * 1024 * 1024
 
 
 def from_partner(value, axis, apart):

time: 74.4 us -> 74.4 us (level)
  no operation moved by 1% of the time
where the time goes in v8:
time: 74.4 us; the launch traced here: 74 us
  starting transfers between devices  30.8 us (41%)
  waiting for transfers between devices  25 us (34%)
  Pallas kernels  13 us (17%)
  local copies, waits for them, and re-layouts  4.52 us (6%)
  between operations  0.82 us (1%)
    ppermute x14, starting transfers between devices, exchanged(): lax.ppermute(value, 'row', [(source, source ^ mask) for source in range(r...  30 us
    ppermute x14, waiting for transfers between devices, exchanged(): lax.ppermute(value, 'row', [(source, source ^ mask) for source in range(r...  22.2 us
    unnamed x18, local copies, waits for them, and re-layouts  4.52 us
    pallas_call x1, Pallas kernels, shards_by_halves(): call(functools.partial(first_kernel, (0, early, block)), [array(pair.shap...  3.99 us
    pallas_call x1, Pallas kernels, shards_by_halves(): call(functools.partial(gate_kernel, block), [array(pair.shape, jnp.float3...  3 us
    ppermute x4, waiting for transfers between devices, from_partner(): return lax.ppermute(value, axis, pairs)  2.72 us
    pallas_call x1, Pallas kernels, shards_by_halves(): call(functools.partial(finish_kernel, 8, chunk_sizes), [array(pair.shape)...  2.54 us
    pallas_call x1, Pallas kernels, shards_by_halves(): call(functools.partial(later_kernel, (block, (0, early, (0, 1)), (4 * ear...  1.95 us
  transfers between devices with their start and end apart: 18, of which 8 were waited for; matrix products, arithmetic and copies ran while one was open for 0% of the time, Pallas kernels for 9%

profile of v8, /device:TPU:0, one launch (start us, length us, event | category | flops | bytes accessed | tf_op | source)
XLA Modules:
  0.0 74.0 jit_solution(12024582927753643442)
XLA Ops:
  0.7 4.0 %norm_and_first_edges.1 = (bf16[32,128,128]{2,1,0:T(8,128)(2,1)}, bf16[26,32,128]{2,1,0:T(8,128)(2,1)}, bf16[26,32,128]{2,1,0:T(8,128)(2,1)}, bf16[26,32,128]{2,1,0:T(8,128)(2,1)}) custom-call(s32[1]{0:T(128)S(6)} %copy.11.length, bf16[32,128,128]{2,1,0:T(8,128)(2,1)} %pair.1, f32[1,128]{1,0:T(1,128)} %bitcast.6, f32[1,128]{1,0:T(1,128)} %bitcast.7, ...), custom_call_target="tpu_custom_call" | custom-call | tf_op jit(solution)/shard_map/norm_and_first_edges/pallas_call | solution.py:390
  4.6 4.0 %collective-permute-start.2 = (bf16[26,32,128]{2,1,0:T(8,128)(2,1)}, bf16[26,32,128]{2,1,0:T(8,128)(2,1)S(1)}, u32[]{:S(2)}, u32[]{:S(2)}) collective-permute-start(bf16[26,32,128]{2,1,0:T(8,128)(2,1)} %get-tuple-element.32), channel_id=1, source_target_pairs={{0,6},{2,4},{4,2},{6,0},{8,14},{10,12},{12,10},{14,8},{1,7},{3,5},... | collective-permute-start | bytes 638984 | tf_op jit(solution)/shard_map/ppermute | solution.py:371
  8.7 0.4 collective-permute-start.3
  9.3 1.2 %copy-done.2 = bf16[32,128,128]{2,1,0:T(8,128)(2,1)S(1)} copy-done((bf16[32,128,128]{2,1,0:T(8,128)(2,1)S(1)}, bf16[32,128,128]{2,1,0:T(8,128)(2,1)}, u32[]{:S(2)}) %copy-start.2) | copy-done | bytes 1048600
  10.6 0.8 %copy-done.4 = bf16[128,256]{1,0:T(8,128)(2,1)S(1)} copy-done((bf16[128,256]{1,0:T(8,128)(2,1)S(1)}, bf16[128,256]{1,0:T(8,128)(2,1)}, u32[]{:S(2)}) %copy-start.4) | copy-done | bytes 65560
  11.4 0.8 %copy-done.5 = bf16[128,256]{1,0:T(8,128)(2,1)S(1)} copy-done((bf16[128,256]{1,0:T(8,128)(2,1)S(1)}, bf16[128,256]{1,0:T(8,128)(2,1)}, u32[]{:S(2)}) %copy-start.5) | copy-done | bytes 65560
  12.2 2.0 %later_edges.1 = (bf16[26,32,128]{2,1,0:T(8,128)(2,1)S(1)}, bf16[38,32,128]{2,1,0:T(8,128)(2,1)S(1)}, bf16[38,32,128]{2,1,0:T(8,128)(2,1)S(1)}, bf16[38,32,128]{2,1,0:T(8,128)(2,1)S(1)}, bf16[38,32,128]{2,1,0:T(8,128)(2,1)S(1)}) custom-call(s32[1]{0:T(128)S(6)} %copy.11.length, bf16[32,128,128]{2,1,0:T(8,128)(2,1)S(1)} %copy-done.2, ...), custom_call_target="tpu_custom_call" | custom-call | tf_op jit(solution)/shard_map/later_edges/pallas_call | solution.py:408
  14.2 2.9 %collective-permute-start.5 = (bf16[38,32,128]{2,1,0:T(8,128)(2,1)S(1)}, bf16[38,32,128]{2,1,0:T(8,128)(2,1)S(1)}, u32[]{:S(2)}, u32[]{:S(2)}) collective-permute-start(bf16[38,32,128]{2,1,0:T(8,128)(2,1)S(1)} %get-tuple-element.35), channel_id=1, source_target_pairs={{0,6},{2,4},{4,2},{6,0},{8,14},{10,12},{12,10},{14,8},{1,7},{3,5},... | collective-permute-start | bytes 933896 | tf_op jit(solution)/shard_map/ppermute | solution.py:371
  17.1 0.4 collective-permute-start.7
  17.8 2.3 %collective-permute-done.3.b.refs_5_ = bf16[26,32,128]{2,1,0:T(8,128)(2,1)S(1)} collective-permute-done((bf16[26,32,128]{2,1,0:T(8,128)(2,1)}, bf16[26,32,128]{2,1,0:T(8,128)(2,1)S(1)}, u32[]{:S(2)}, u32[]{:S(2)}) %collective-permute-start.3) | collective-permute-done | bytes 213024 | tf_op jit(solution)/shard_map/ppermute | solution.py:371
  20.3 0.6 collective-permute-start.1
  20.8 0.8 %collective-permute-done.4.refs_1_ = bf16[13,64,128]{2,1,0:T(8,128)(2,1)S(1)} collective-permute-done((bf16[13,64,128]{2,1,0:T(8,128)(2,1)S(1)}, bf16[13,64,128]{2,1,0:T(8,128)(2,1)S(1)}, u32[]{:S(2)}, u32[]{:S(2)}) %collective-permute-start.4) | collective-permute-done | bytes 213024 | tf_op jit(solution)/shard_map/ppermute | solution.py:21
  21.7 0.3 collective-permute-done.1.refs_0_
  22.0 0.4 contract.2
  22.4 2.6 %collective-permute-start.14 = (bf16[13,128,128]{2,1,0:T(8,128)(2,1)S(1)}, bf16[13,128,128]{2,1,0:T(8,128)(2,1)S(1)}, u32[]{:S(2)}, u32[]{:S(2)}) collective-permute-start(bf16[13,128,128]{2,1,0:T(8,128)(2,1)S(1)} %get-tuple-element.34.after), channel_id=1, source_target_pairs={{0,8},{2,10},{4,12},{6,14},{8,0},{10,2},{12,4},{14,6},{1,9},{3,11}... | collective-permute-start | bytes 1277960 | tf_op jit(solution)/shard_map/ppermute | solution.py:371
  25.1 3.0 %output_gate.1.after.refs_8_ = f32[32,128,128]{2,1,0:T(8,128)} custom-call(bf16[13,128,128]{2,1,0:T(8,128)(2,1)} %copy-done.3, bf16[32,128,128]{2,1,0:T(8,128)(2,1)} %get-tuple-element.28.normed, bf16[128,128]{1,0:T(8,128)(2,1)} %weights.1), custom_call_target="tpu_custom_call" | custom-call | tf_op jit(solution)/shard_map/output_gate/pallas_call | solution.py:430
  28.1 1.6 %copy-done = f32[32,128,128]{2,1,0:T(8,128)S(1)} copy-done((f32[32,128,128]{2,1,0:T(8,128)S(1)}, f32[32,128,128]{2,1,0:T(8,128)}, u32[]{:S(2)}) %copy-start) | copy-done | bytes 2097176
  29.8 10.6 %collective-permute-done.7.a.refs_4_ = bf16[38,32,128]{2,1,0:T(8,128)(2,1)S(1)} collective-permute-done((bf16[38,32,128]{2,1,0:T(8,128)(2,1)S(1)}, bf16[38,32,128]{2,1,0:T(8,128)(2,1)S(1)}, u32[]{:S(2)}, u32[]{:S(2)}) %collective-permute-start.7) | collective-permute-done | bytes 311328 | tf_op jit(solution)/shard_map/ppermute | solution.py:371
  40.6 1.6 %collective-permute-done.9.refs_1_ = bf16[19,64,128]{2,1,0:T(8,128)(2,1)S(1)} collective-permute-done((bf16[19,64,128]{2,1,0:T(8,128)(2,1)S(1)}, bf16[19,64,128]{2,1,0:T(8,128)(2,1)S(1)}, u32[]{:S(2)}, u32[]{:S(2)}) %collective-permute-start.9) | collective-permute-done | bytes 311328 | tf_op jit(solution)/shard_map/ppermute | solution.py:21
  42.2 0.6 contract.3
  42.9 0.9 %collective-permute-start.10 = (bf16[19,32,128]{2,1,0:T(8,128)(2,1)S(1)}, bf16[19,32,128]{2,1,0:T(8,128)(2,1)S(1)}, u32[]{:S(2)}, u32[]{:S(2)}) collective-permute-start(bf16[19,32,128]{2,1,0:T(8,128)(2,1)S(1)} %get-tuple-element.38), channel_id=1, source_target_pairs={{0,14},{2,12},{4,10},{6,8},{8,6},{10,4},{12,2},{14,0},{1,15},{3,13... | collective-permute-start | bytes 466952 | tf_op jit(solution)/shard_map/ppermute | solution.py:371
  43.7 2.3 %collective-permute-start.11 = (bf16[19,32,128]{2,1,0:T(8,128)(2,1)S(1)}, bf16[19,32,128]{2,1,0:T(8,128)(2,1)S(1)}, u32[]{:S(2)}, u32[]{:S(2)}) collective-permute-start(bf16[19,32,128]{2,1,0:T(8,128)(2,1)S(1)} %get-tuple-element.39), channel_id=1, source_target_pairs={{0,12},{2,14},{4,8},{6,10},{8,4},{10,6},{12,0},{14,2},{1,13},{3,15... | collective-permute-start | bytes 466952 | tf_op jit(solution)/shard_map/ppermute | solution.py:371
  46.1 0.2 add_halves.1
  46.3 0.6 collective-permute-start.15
  46.9 5.3 %collective-permute-start.16 = (bf16[32,32,128]{2,1,0:T(8,128)(2,1)S(1)}, bf16[32,32,128]{2,1,0:T(8,128)(2,1)S(1)}, u32[]{:S(2)}, u32[]{:S(2)}) collective-permute-start(bf16[32,32,128]{2,1,0:T(8,128)(2,1)S(1)} %get-tuple-element.49), channel_id=1, source_target_pairs={{0,4},{2,6},{4,0},{6,2},{8,12},{10,14},{12,8},{14,10},{1,5},{3,7},... | collective-permute-start | bytes 786440 | tf_op jit(solution)/shard_map/ppermute | solution.py:371
  52.2 1.4 %collective-permute-start.17 = (bf16[32,32,128]{2,1,0:T(8,128)(2,1)S(1)}, bf16[32,32,128]{2,1,0:T(8,128)(2,1)S(1)}, u32[]{:S(2)}, u32[]{:S(2)}) collective-permute-start(bf16[32,32,128]{2,1,0:T(8,128)(2,1)S(1)} %get-tuple-element.50), channel_id=1, source_target_pairs={{0,2},{2,0},{4,6},{6,4},{8,10},{10,8},{12,14},{14,12},{1,3},{3,1},... | collective-permute-start | bytes 786440 | tf_op jit(solution)/shard_map/ppermute | solution.py:371
  53.6 7.1 %collective-permute-start.12 = (bf16[19,32,128]{2,1,0:T(8,128)(2,1)S(1)}, bf16[19,32,128]{2,1,0:T(8,128)(2,1)S(1)}, u32[]{:S(2)}, u32[]{:S(2)}) collective-permute-start(bf16[19,32,128]{2,1,0:T(8,128)(2,1)S(1)} %get-tuple-element.40), channel_id=1, source_target_pairs={{0,10},{2,8},{4,14},{6,12},{8,2},{10,0},{12,6},{14,4},{1,11},{3,9}... | collective-permute-start | bytes 466952 | tf_op jit(solution)/shard_map/ppermute | solution.py:371
  60.7 1.4 %collective-permute-start.13 = (bf16[19,32,128]{2,1,0:T(8,128)(2,1)S(1)}, bf16[19,32,128]{2,1,0:T(8,128)(2,1)S(1)}, u32[]{:S(2)}, u32[]{:S(2)}) collective-permute-start(bf16[19,32,128]{2,1,0:T(8,128)(2,1)S(1)} %get-tuple-element.41), channel_id=1, source_target_pairs={{0,8},{2,10},{4,12},{6,14},{8,0},{10,2},{12,4},{14,6},{1,9},{3,11}... | collective-permute-start | bytes 466952 | tf_op jit(solution)/shard_map/ppermute | solution.py:371
  62.2 4.7 %collective-permute-done.12.refs_2_ = bf16[19,32,128]{2,1,0:T(8,128)(2,1)S(1)} collective-permute-done((bf16[19,32,128]{2,1,0:T(8,128)(2,1)S(1)}, bf16[19,32,128]{2,1,0:T(8,128)(2,1)S(1)}, u32[]{:S(2)}, u32[]{:S(2)}) %collective-permute-start.12) | collective-permute-done | bytes 155680 | tf_op jit(solution)/shard_map/ppermute | solution.py:371
  66.9 2.5 %collective-permute-done.13.refs_3_ = bf16[19,32,128]{2,1,0:T(8,128)(2,1)S(1)} collective-permute-done((bf16[19,32,128]{2,1,0:T(8,128)(2,1)S(1)}, bf16[19,32,128]{2,1,0:T(8,128)(2,1)S(1)}, u32[]{:S(2)}, u32[]{:S(2)}) %collective-permute-start.13) | collective-permute-done | bytes 155680 | tf_op jit(solution)/shard_map/ppermute | solution.py:371
  69.4 2.1 %collective-permute-done.16.refs_6_ = bf16[32,32,128]{2,1,0:T(8,128)(2,1)S(1)} collective-permute-done((bf16[32,32,128]{2,1,0:T(8,128)(2,1)S(1)}, bf16[32,32,128]{2,1,0:T(8,128)(2,1)S(1)}, u32[]{:S(2)}, u32[]{:S(2)}) %collective-permute-start.16) | collective-permute-done | bytes 262176 | tf_op jit(solution)/shard_map/ppermute | solution.py:371
  71.5 2.5 %norm_and_project_out.1 = bf16[32,128,128]{2,1,0:T(8,128)(2,1)} custom-call(bf16[19,32,128]{2,1,0:T(8,128)(2,1)S(1)} %collective-permute-done.10.refs_0_, bf16[19,32,128]{2,1,0:T(8,128)(2,1)S(1)} %collective-permute-done.11.refs_1_, bf16[19,32,128]{2,1,0:T(8,128)(2,1)S(1)} %collective-permute-done.12.refs_2_, ...), custom_call_target="tpu_custom_call" | custom-call | tf_op jit(solution)/shard_map/norm_and_project_out/pallas_call | solution.py:459
  (33 shorter events, 0.9 us)
Async XLA Ops:
  4.6 12.9 %collective-permute-start.2 = (bf16[26,32,128]{2,1,0:T(8,128)(2,1)}, bf16[26,32,128]{2,1,0:T(8,128)(2,1)S(1)}, u32[]{:S(2)}, u32[]{:S(2)}) collective-permute-start(bf16[26,32,128]{2,1,0:T(8,128)(2,1)} %get-tuple-element.32), channel_id=1, source_target_pairs={{0,6},{2,4},{4,2},{6,0},{8,14},{10,12},{12,10},{14,8},{1,7},{3,5},... | collective-permute-start | bytes 638984 | tf_op jit(solution)/shard_map/ppermute | solution.py:371
  8.7 11.4 %collective-permute-start.3 = (bf16[26,32,128]{2,1,0:T(8,128)(2,1)}, bf16[26,32,128]{2,1,0:T(8,128)(2,1)S(1)}, u32[]{:S(2)}, u32[]{:S(2)}) collective-permute-start(bf16[26,32,128]{2,1,0:T(8,128)(2,1)} %get-tuple-element.33), channel_id=1, source_target_pairs={{0,4},{2,6},{4,0},{6,2},{8,12},{10,14},{12,8},{14,10},{1,5},{3,7},... | collective-permute-start | bytes 638984 | tf_op jit(solution)/shard_map/ppermute | solution.py:371
  9.1 11.1 %collective-permute-start = (bf16[26,32,128]{2,1,0:T(8,128)(2,1)}, bf16[26,32,128]{2,1,0:T(8,128)(2,1)S(1)}, u32[]{:S(2)}, u32[]{:S(2)}) collective-permute-start(bf16[26,32,128]{2,1,0:T(8,128)(2,1)} %get-tuple-element.31), channel_id=1, source_target_pairs={{0,2},{2,0},{4,6},{6,4},{8,10},{10,8},{12,14},{14,12},{1,3},{3,1},... | collective-permute-start | bytes 638984 | tf_op jit(solution)/shard_map/ppermute | solution.py:371
  9.3 1.2 %copy-start.2 = (bf16[32,128,128]{2,1,0:T(8,128)(2,1)S(1)}, bf16[32,128,128]{2,1,0:T(8,128)(2,1)}, u32[]{:S(2)}) copy-start(bf16[32,128,128]{2,1,0:T(8,128)(2,1)} %get-tuple-element.28.normed) | copy-start | bytes 3145732
  10.6 0.8 %copy-start.4 = (bf16[128,256]{1,0:T(8,128)(2,1)S(1)}, bf16[128,256]{1,0:T(8,128)(2,1)}, u32[]{:S(2)}) copy-start(bf16[128,256]{1,0:T(8,128)(2,1)} %proj.3) | copy-start | bytes 196612
  11.4 0.8 %copy-start.5 = (bf16[128,256]{1,0:T(8,128)(2,1)S(1)}, bf16[128,256]{1,0:T(8,128)(2,1)}, u32[]{:S(2)}) copy-start(bf16[128,256]{1,0:T(8,128)(2,1)} %gate.3) | copy-start | bytes 196612
  14.2 13.9 %collective-permute-start.5 = (bf16[38,32,128]{2,1,0:T(8,128)(2,1)S(1)}, bf16[38,32,128]{2,1,0:T(8,128)(2,1)S(1)}, u32[]{:S(2)}, u32[]{:S(2)}) collective-permute-start(bf16[38,32,128]{2,1,0:T(8,128)(2,1)S(1)} %get-tuple-element.35), channel_id=1, source_target_pairs={{0,6},{2,4},{4,2},{6,0},{8,14},{10,12},{12,10},{14,8},{1,7},{3,5},... | collective-permute-start | bytes 933896 | tf_op jit(solution)/shard_map/ppermute | solution.py:371
  17.1 23.3 %collective-permute-start.7 = (bf16[38,32,128]{2,1,0:T(8,128)(2,1)S(1)}, bf16[38,32,128]{2,1,0:T(8,128)(2,1)S(1)}, u32[]{:S(2)}, u32[]{:S(2)}) collective-permute-start(bf16[38,32,128]{2,1,0:T(8,128)(2,1)S(1)} %get-tuple-element.36), channel_id=1, source_target_pairs={{0,4},{2,6},{4,0},{6,2},{8,12},{10,14},{12,8},{14,10},{1,5},{3,7},... | collective-permute-start | bytes 933896 | tf_op jit(solution)/shard_map/ppermute | solution.py:371
  17.6 22.9 %collective-permute-start.8 = (bf16[38,32,128]{2,1,0:T(8,128)(2,1)S(1)}, bf16[38,32,128]{2,1,0:T(8,128)(2,1)S(1)}, u32[]{:S(2)}, u32[]{:S(2)}) collective-permute-start(bf16[38,32,128]{2,1,0:T(8,128)(2,1)S(1)} %get-tuple-element.37), channel_id=1, source_target_pairs={{0,2},{2,0},{4,6},{6,4},{8,10},{10,8},{12,14},{14,12},{1,3},{3,1},... | collective-permute-start | bytes 933896 | tf_op jit(solution)/shard_map/ppermute | solution.py:371
  20.1 1.5 %collective-permute-start.4 = (bf16[13,64,128]{2,1,0:T(8,128)(2,1)S(1)}, bf16[13,64,128]{2,1,0:T(8,128)(2,1)S(1)}, u32[]{:S(2)}, u32[]{:S(2)}) collective-permute-start(bf16[13,64,128]{2,1,0:T(8,128)(2,1)S(1)} %pack_left.5), channel_id=1, source_target_pairs={{0,1},{1,0},{2,3},{3,2},{4,5},{5,4},{6,7},{7,6},{8,9},{9,8},{10,11... | collective-permute-start | bytes 638984 | tf_op jit(solution)/shard_map/ppermute | solution.py:21
  20.3 1.7 %collective-permute-start.1 = (bf16[13,64,128]{2,1,0:T(8,128)(2,1)S(1)}, bf16[13,64,128]{2,1,0:T(8,128)(2,1)S(1)}, u32[]{:S(2)}, u32[]{:S(2)}) collective-permute-start(bf16[13,64,128]{2,1,0:T(8,128)(2,1)S(1)} %pack_left.4), channel_id=1, source_target_pairs={{0,1},{1,0},{2,3},{3,2},{4,5},{5,4},{6,7},{7,6},{8,9},{9,8},{10,11... | collective-permute-start | bytes 638984 | tf_op jit(solution)/shard_map/ppermute | solution.py:21
  22.4 2.7 %copy-start.3 = (bf16[13,128,128]{2,1,0:T(8,128)(2,1)}, bf16[13,128,128]{2,1,0:T(8,128)(2,1)S(1)}, u32[]{:S(2)}) copy-start(bf16[13,128,128]{2,1,0:T(8,128)(2,1)S(1)} %get-tuple-element.34.after) | copy-start | bytes 1277956
  22.4 23.7 %collective-permute-start.14 = (bf16[13,128,128]{2,1,0:T(8,128)(2,1)S(1)}, bf16[13,128,128]{2,1,0:T(8,128)(2,1)S(1)}, u32[]{:S(2)}, u32[]{:S(2)}) collective-permute-start(bf16[13,128,128]{2,1,0:T(8,128)(2,1)S(1)} %get-tuple-element.34.after), channel_id=1, source_target_pairs={{0,8},{2,10},{4,12},{6,14},{8,0},{10,2},{12,4},{14,6},{1,9},{3,11}... | collective-permute-start | bytes 1277960 | tf_op jit(solution)/shard_map/ppermute | solution.py:371
  28.1 1.6 %copy-start = (f32[32,128,128]{2,1,0:T(8,128)S(1)}, f32[32,128,128]{2,1,0:T(8,128)}, u32[]{:S(2)}) copy-start(f32[32,128,128]{2,1,0:T(8,128)} %output_gate.1.after.refs_8_) | copy-start | bytes 6291460
  29.7 10.8 %copy-start.1 = (f32[32,128,128]{2,1,0:T(8,128)S(1)}, f32[32,128,128]{2,1,0:T(8,128)}, u32[]{:S(2)}) copy-start(f32[32,128,128]{2,1,0:T(8,128)} %output_gate.1.after.refs_8_) | copy-start | bytes 6291460
  29.7 10.9 %collective-permute-start.6 = (bf16[19,64,128]{2,1,0:T(8,128)(2,1)S(1)}, bf16[19,64,128]{2,1,0:T(8,128)(2,1)S(1)}, u32[]{:S(2)}, u32[]{:S(2)}) collective-permute-start(bf16[19,64,128]{2,1,0:T(8,128)(2,1)S(1)} %pack_left.6), channel_id=1, source_target_pairs={{0,1},{1,0},{2,3},{3,2},{4,5},{5,4},{6,7},{7,6},{8,9},{9,8},{10,11... | collective-permute-start | bytes 933896 | tf_op jit(solution)/shard_map/ppermute | solution.py:21
  40.5 31.0 %copy-start.6 = (bf16[128,128]{1,0:T(8,128)(2,1)S(1)}, bf16[128,128]{1,0:T(8,128)(2,1)}, u32[]{:S(2)}) copy-start(bf16[128,128]{1,0:T(8,128)(2,1)} %refs_11_.1) | copy-start | bytes 98308
  40.5 31.0 %copy-start.7 = (f32[128]{0:T(128)S(1)}, f32[128]{0:T(128)}, u32[]{:S(2)}) copy-start(f32[128]{0:T(128)} %param.17) | copy-start | bytes 1540
  40.5 31.0 %copy-start.8 = (f32[128]{0:T(128)S(1)}, f32[128]{0:T(128)}, u32[]{:S(2)}) copy-start(f32[128]{0:T(128)} %param.18) | copy-start | bytes 1540
  40.5 1.7 %collective-permute-start.9 = (bf16[19,64,128]{2,1,0:T(8,128)(2,1)S(1)}, bf16[19,64,128]{2,1,0:T(8,128)(2,1)S(1)}, u32[]{:S(2)}, u32[]{:S(2)}) collective-permute-start(bf16[19,64,128]{2,1,0:T(8,128)(2,1)S(1)} %pack_left.7), channel_id=1, source_target_pairs={{0,1},{1,0},{2,3},{3,2},{4,5},{5,4},{6,7},{7,6},{8,9},{9,8},{10,11... | collective-permute-start | bytes 933896 | tf_op jit(solution)/shard_map/ppermute | solution.py:21
  42.9 10.8 %collective-permute-start.10 = (bf16[19,32,128]{2,1,0:T(8,128)(2,1)S(1)}, bf16[19,32,128]{2,1,0:T(8,128)(2,1)S(1)}, u32[]{:S(2)}, u32[]{:S(2)}) collective-permute-start(bf16[19,32,128]{2,1,0:T(8,128)(2,1)S(1)} %get-tuple-element.38), channel_id=1, source_target_pairs={{0,14},{2,12},{4,10},{6,8},{8,6},{10,4},{12,2},{14,0},{1,15},{3,13... | collective-permute-start | bytes 466952 | tf_op jit(solution)/shard_map/ppermute | solution.py:371
  43.7 17.0 %collective-permute-start.11 = (bf16[19,32,128]{2,1,0:T(8,128)(2,1)S(1)}, bf16[19,32,128]{2,1,0:T(8,128)(2,1)S(1)}, u32[]{:S(2)}, u32[]{:S(2)}) collective-permute-start(bf16[19,32,128]{2,1,0:T(8,128)(2,1)S(1)} %get-tuple-element.39), channel_id=1, source_target_pairs={{0,12},{2,14},{4,8},{6,10},{8,4},{10,6},{12,0},{14,2},{1,13},{3,15... | collective-permute-start | bytes 466952 | tf_op jit(solution)/shard_map/ppermute | solution.py:371
  46.3 23.1 %collective-permute-start.15 = (bf16[32,32,128]{2,1,0:T(8,128)(2,1)S(1)}, bf16[32,32,128]{2,1,0:T(8,128)(2,1)S(1)}, u32[]{:S(2)}, u32[]{:S(2)}) collective-permute-start(bf16[32,32,128]{2,1,0:T(8,128)(2,1)S(1)} %get-tuple-element.48), channel_id=1, source_target_pairs={{0,6},{2,4},{4,2},{6,0},{8,14},{10,12},{12,10},{14,8},{1,7},{3,5},... | collective-permute-start | bytes 786440 | tf_op jit(solution)/shard_map/ppermute | solution.py:371
  46.9 24.6 %collective-permute-start.16 = (bf16[32,32,128]{2,1,0:T(8,128)(2,1)S(1)}, bf16[32,32,128]{2,1,0:T(8,128)(2,1)S(1)}, u32[]{:S(2)}, u32[]{:S(2)}) collective-permute-start(bf16[32,32,128]{2,1,0:T(8,128)(2,1)S(1)} %get-tuple-element.49), channel_id=1, source_target_pairs={{0,4},{2,6},{4,0},{6,2},{8,12},{10,14},{12,8},{14,10},{1,5},{3,7},... | collective-permute-start | bytes 786440 | tf_op jit(solution)/shard_map/ppermute | solution.py:371
  52.2 19.2 %collective-permute-start.17 = (bf16[32,32,128]{2,1,0:T(8,128)(2,1)S(1)}, bf16[32,32,128]{2,1,0:T(8,128)(2,1)S(1)}, u32[]{:S(2)}, u32[]{:S(2)}) collective-permute-start(bf16[32,32,128]{2,1,0:T(8,128)(2,1)S(1)} %get-tuple-element.50), channel_id=1, source_target_pairs={{0,2},{2,0},{4,6},{6,4},{8,10},{10,8},{12,14},{14,12},{1,3},{3,1},... | collective-permute-start | bytes 786440 | tf_op jit(solution)/shard_map/ppermute | solution.py:371
  53.6 13.2 %collective-permute-start.12 = (bf16[19,32,128]{2,1,0:T(8,128)(2,1)S(1)}, bf16[19,32,128]{2,1,0:T(8,128)(2,1)S(1)}, u32[]{:S(2)}, u32[]{:S(2)}) collective-permute-start(bf16[19,32,128]{2,1,0:T(8,128)(2,1)S(1)} %get-tuple-element.40), channel_id=1, source_target_pairs={{0,10},{2,8},{4,14},{6,12},{8,2},{10,0},{12,6},{14,4},{1,11},{3,9}... | collective-permute-start | bytes 466952 | tf_op jit(solution)/shard_map/ppermute | solution.py:371
  60.7 8.6 %collective-permute-start.13 = (bf16[19,32,128]{2,1,0:T(8,128)(2,1)S(1)}, bf16[19,32,128]{2,1,0:T(8,128)(2,1)S(1)}, u32[]{:S(2)}, u32[]{:S(2)}) collective-permute-start(bf16[19,32,128]{2,1,0:T(8,128)(2,1)S(1)} %get-tuple-element.41), channel_id=1, source_target_pairs={{0,8},{2,10},{4,12},{6,14},{8,0},{10,2},{12,4},{14,6},{1,9},{3,11}... | collective-permute-start | bytes 466952 | tf_op jit(solution)/shard_map/ppermute | solution.py:371
